TPU v7x, 32 devices: a whole 2x2x4 slice. The times are simulated.
32 devices in a mesh: band: 4 (over z), facet: 8 (over y, x, core).
Axes of the slice: x: 2, y: 2, z: 4, core: 2. Of those that a mesh axis runs over, the one named last changes fastest.
Arguments:
- facets: bfloat16 [4, 8, 2, 128, 4096], P('band', 'facet'), may hold values from -6 to 6
- col_window: float32 [4096], replicated, may hold values from 0.25 to 1
- slot_of_subgrid: int32 [12], replicated, may hold values from 0 to 15, as said below
- block_slot: int32 [4, 8, 4], P('band', 'facet'), may hold values from 0 to 1
- block_band: int32 [4, 8, 4], P('band', 'facet'), may hold values from 0 to 2
- block_offset: int32 [4, 8, 4], P('band', 'facet'), may hold values from 0 to 128
- block_weight: float32 [4, 8, 4], P('band', 'facet'), may hold values from 0 to 1
- vis_pos: float32 [4, 8, 4, 2, 2048], P('band', 'facet'), may hold values from 0 to 1
Outputs:
- subgrids: bfloat16 [4, 16, 2, 16, 256], P('band', 'facet')
- visibilities: float32 [4, 8, 4, 2, 2048], P('band', 'facet')
Inputs may be any that keep to these rules, and one draw needn't show every extreme that they name: `slot_of_subgrid`: values are distinct; at most 2 subgrids share an owner, and some owner holds 2.
All inputs are finite; a program needn't handle non-finite values.
Results may differ from a plain program's by a relative error of at most 0.009.
Values may be sent and summed in bfloat16 or wider, within the bound.
No kernel may reach another device: no remote copies, remote signals or barrier semaphores. Data moves between devices by JAX's collectives and lax.ppermute only.
A program may use at most 64 MiB of HBM per device.

v0:
```python
import math

import jax
import jax.numpy as jnp
from jax import lax
from jax.sharding import PartitionSpec as P

SG = 256
CR = 16
CAP = 2
PC = 128


kernel_sigma = 1.5
highest = lax.Precision.HIGHEST


def column_table(length, width):
    rows = jnp.arange(length, dtype=jnp.int32)[:, None]
    cols = jnp.arange(width, dtype=jnp.int32)[None, :]
    angle = 2.0 * math.pi / length * (rows * cols % length).astype(jnp.float32)
    return jnp.concatenate([jnp.cos(angle), -jnp.sin(angle)], axis=1).astype(jnp.bfloat16)


def combine(product, height, width):
    real_part = product[..., :height, :width] - product[..., height:, width:]
    imag_part = product[..., :height, width:] + product[..., height:, :width]
    return jnp.stack([real_part, imag_part], axis=-3)


def sky_phases(freqs, cells, total):
    angle = 2.0 * math.pi / total * (freqs[..., None] * cells % total).astype(jnp.float32)
    return jnp.concatenate([jnp.cos(angle), -jnp.sin(angle)], axis=-2).astype(jnp.bfloat16)


def inverse_columns(sigma):
    width = sigma.shape[-1]
    index = jnp.arange(width, dtype=jnp.int32)
    angle = 2.0 * math.pi / width * (index[:, None] * index[None, :] % width).astype(jnp.float32)
    cos_part = jnp.cos(angle) / math.sqrt(width)
    sin_part = jnp.sin(angle) / math.sqrt(width)
    real_in = sigma[..., 0, :, :]
    imag_in = sigma[..., 1, :, :]
    real_part = jnp.matmul(real_in, cos_part, precision=highest) - jnp.matmul(
        imag_in, sin_part, precision=highest
    )
    imag_part = jnp.matmul(real_in, sin_part, precision=highest) + jnp.matmul(
        imag_in, cos_part, precision=highest
    )
    return jnp.stack([real_part, imag_part], axis=-3).astype(jnp.bfloat16)


def degrid_block(patch, position):
    row_grid = jnp.arange(patch.shape[1], dtype=jnp.float32)[:, None]
    col_grid = jnp.arange(patch.shape[2], dtype=jnp.float32)[:, None]
    row_diff = row_grid - position[0][None, :] * (patch.shape[1] - 1)
    col_diff = col_grid - position[1][None, :] * (patch.shape[2] - 1)
    row_kernel = jnp.exp(-row_diff * row_diff / (2.0 * kernel_sigma * kernel_sigma))
    col_kernel = jnp.exp(-col_diff * col_diff / (2.0 * kernel_sigma * kernel_sigma))
    partial_sum = jnp.einsum("xrc,rv->xcv", patch, row_kernel, precision=highest)
    return jnp.sum(partial_sum * col_kernel[None], axis=1)


def local(
    facets, col_window, slot_of_subgrid, block_slot, block_band, block_offset, block_weight, vis_pos
):
    facet_count = lax.axis_size("facet")
    facet_index = lax.axis_index("facet")
    strip_rows = facets.shape[3]
    strip_length = facets.shape[4]
    subgrid_count = slot_of_subgrid.shape[0]
    sky_rows = facet_count * strip_rows
    windowed = (facets[0, 0].astype(jnp.float32) * col_window).astype(jnp.bfloat16)
    windowed = windowed.reshape(2 * strip_rows, strip_length)
    table = column_table(strip_length, SG)
    product = jnp.dot(windowed, table, preferred_element_type=jnp.float32)
    spectrum = (combine(product, strip_rows, SG) * (1.0 / math.sqrt(strip_length))).astype(
        jnp.bfloat16
    )
    spectrum_cat = jnp.concatenate([spectrum[0], spectrum[1]], axis=1)
    cells = facet_index * strip_rows + jnp.arange(strip_rows, dtype=jnp.int32)
    slots = jnp.arange(facet_count * CAP, dtype=jnp.int32)
    match = slot_of_subgrid[None, :] == slots[:, None]
    subgrid_id = jnp.sum(
        jnp.where(match, jnp.arange(subgrid_count, dtype=jnp.int32)[None, :], 0), axis=1
    )
    valid = jnp.any(match, axis=1)
    freqs = subgrid_id[:, None] * CR + jnp.arange(CR, dtype=jnp.int32)[None, :]
    phases = sky_phases(freqs, cells, sky_rows)
    summed = jnp.einsum("akj,jd->akd", phases, spectrum_cat, preferred_element_type=jnp.float32)
    scale = jnp.where(valid, 1.0 / math.sqrt(sky_rows), 0.0).astype(jnp.float32)
    every_slot = (combine(summed, CR, SG) * scale[:, None, None, None]).astype(jnp.bfloat16)
    received = lax.all_to_all(every_slot, "facet", split_axis=0, concat_axis=0, tiled=True)
    sigma = jnp.sum(received.astype(jnp.float32).reshape(facet_count, CAP, 2, CR, SG), axis=0)
    owned = inverse_columns(sigma)
    slot_list = block_slot[0, 0]
    band_list = block_band[0, 0]
    offset_list = block_offset[0, 0]
    zero = jnp.zeros((), jnp.int32)
    every_band = lax.all_gather(owned[None], "band", axis=0, tiled=True)

    def fetch(slot, lower_band, start):
        lower = lax.dynamic_slice(
            every_band, (lower_band, slot, zero, zero, start), (1, 1, 2, CR, PC)
        )[0, 0]
        upper = lax.dynamic_slice(
            every_band, (lower_band + 1, slot, zero, zero, start), (1, 1, 2, CR, PC)
        )[0, 0]
        return (lower.astype(jnp.float32), upper.astype(jnp.float32))

    lower_all, upper_all = jax.vmap(fetch)(slot_list, band_list, offset_list)
    weights = block_weight[0, 0][:, None, None, None]
    patches = (1.0 - weights) * lower_all + weights * upper_all
    visible = jax.vmap(degrid_block)(patches, vis_pos[0, 0])
    return (owned[None], visible[None, None])


def solution(mesh):
    in_specs = (
        P("band", "facet", None, None, None),
        P(),
        P(),
        P("band", "facet", None),
        P("band", "facet", None),
        P("band", "facet", None),
        P("band", "facet", None),
        P("band", "facet", None, None, None),
    )
    out_specs = (P("band", "facet", None, None, None), P("band", "facet", None, None, None))
    return jax.shard_map(local, mesh=mesh, in_specs=in_specs, out_specs=out_specs, check_vma=False)
```

profile of v0, /device:TPU:0, one launch (start us, length us, event | category | flops | bytes accessed | tf_op | source)
XLA Modules:
  0.0 65.6 jit_solution(1137736769884561213)
XLA Ops:
  0.6 0.0 copy-start.7
  0.7 17.1 %negate_convert_fusion = (bf16[4096,256]{1,0:T(8,128)(2,1)S(1)}, bf16[4096,256]{1,0:T(8,128)(2,1)S(1)}) fusion(), kind=kLoop, calls=%fused_computation.18 | loop fusion | flops 17825792 | bytes 4194304 | tf_op jit(solution)/shard_map/convert.9
  17.8 0.1 select_reduce_fusion
  17.9 0.1 fusion.66
  18.1 1.2 %fusion.5 = f32[256,512]{1,0:T(8,128)S(1)} fusion(bf16[4096,256]{1,0:T(8,128)(2,1)S(1)} %get-tuple-element.24, bf16[4096,256]{1,0:T(8,128)(2,1)S(1)} %get-tuple-element.25, bf16[256,4096]{1,0:T(8,128)(2,1)S(1)} %bitcast.98, f32[4096]{0:T(1024)S(1)} %copy-done.6), kind=kOutput, calls=%fused_computation.12 | convolution fusion | flops 1085276160 | bytes 6832128 | tf_op jit(solution)/shard_map/dot_general | solution.py:76
  19.3 0.0 copy-start.1
  19.4 0.1 iota_add_fusion
  19.5 0.6 cosine_convert_fusion.1
  20.1 0.3 fusion.48
  20.4 0.0 copy-start.8
  20.4 0.0 copy-start.2
  20.4 0.0 copy-start.3
  20.4 0.0 copy-start.4
  20.4 0.1 fusion.30
  20.5 0.1 fusion.23
  20.6 0.7 %copy.36 = bf16[16,2,16,256]{3,2,1,0:T(8,128)(2,1)} copy(bf16[16,2,16,256]{3,2,0,1:T(8,128)(2,1)S(1)} %fusion.23) | data formatting | bytes 524288 | tf_op jit(solution)/shard_map/convert_element_type | solution.py:92
  21.4 5.2 %all-to-all-start = ((bf16[16,2,16,256]{3,2,1,0:T(8,128)(2,1)}), bf16[16,2,16,256]{3,2,1,0:T(8,128)(2,1)S(1)}, u32[]{:S(2)}, u32[]{:S(2)}) async-start(bf16[16,2,16,256]{3,2,1,0:T(8,128)(2,1)} %copy.36), calls=%async_computation | async-start | bytes 524288 | tf_op jit(solution)/shard_map/all_to_all | solution.py:93
  26.5 0.1 slice_multiply_fusion.1
  26.6 2.8 %fusion.4 = f32[4,128,2048]{2,1,0:T(8,128)} fusion(f32[4,2048]{1,0:T(4,128)S(1)} %bitcast.95), kind=kLoop, calls=%fused_computation.11 | loop fusion | flops 4194304 | bytes 4227072 | tf_op jit(solution)/shard_map/vmap()/exp | solution.py:59
  29.5 4.0 %all-to-all-done = bf16[16,2,16,256]{3,2,1,0:T(8,128)(2,1)S(1)} async-done(((bf16[16,2,16,256]{3,2,1,0:T(8,128)(2,1)}), bf16[16,2,16,256]{3,2,1,0:T(8,128)(2,1)S(1)}, u32[]{:S(2)}, u32[]{:S(2)}) %all-to-all-start) | async-done | bytes 262176 | tf_op jit(solution)/shard_map/all_to_all | solution.py:93
  33.5 1.2 %fusion.36 = f32[2,16,256]{2,1,0:T(8,128)S(1)} fusion(f32[2,2,16,256]{3,2,1,0:T(8,128)S(1)} %convert_reduce_fusion), kind=kOutput, calls=%fused_computation.55 | convolution fusion | flops 26148864 | bytes 65536 | tf_op jit(solution)/shard_map/dot_general | solution.py:44
  34.8 1.2 %fusion.32 = f32[2,16,256]{2,1,0:T(8,128)S(1)} fusion(f32[2,2,16,256]{3,2,1,0:T(8,128)S(1)} %convert_reduce_fusion), kind=kOutput, calls=%fused_computation.51 | convolution fusion | flops 26148864 | bytes 65536 | tf_op jit(solution)/shard_map/dot_general | solution.py:47
  36.0 1.2 %fusion.18 = bf16[1,2,1,16,256]{4,3,1,2,0:T(8,128)(2,1)S(1)} fusion(f32[2,16,256]{2,1,0:T(8,128)S(1)} %fusion.36, f32[2,2,16,256]{3,2,1,0:T(8,128)S(1)} %convert_reduce_fusion), kind=kOutput, calls=%fused_computation.29 | convolution fusion | flops 26165248 | bytes 81920 | tf_op jit(solution)/shard_map/dot_general | solution.py:44
  37.2 1.2 %fusion.17 = bf16[1,2,1,16,256]{4,3,1,2,0:T(8,128)(2,1)S(1)} fusion(f32[2,16,256]{2,1,0:T(8,128)S(1)} %fusion.32, f32[2,2,16,256]{3,2,1,0:T(8,128)S(1)} %convert_reduce_fusion), kind=kOutput, calls=%fused_computation.28 | convolution fusion | flops 26165248 | bytes 81920 | tf_op jit(solution)/shard_map/dot_general | solution.py:47
  38.5 0.0 copy-start
  38.5 13.8 %all_gather.3 = bf16[4,2,2,16,256]{4,3,2,1,0:T(8,128)(2,1)S(1)} all-gather(bf16[1,2,2,16,256]{4,3,2,1,0:T(8,128)(2,1)S(1)} %copy.44), channel_id=1, replica_groups=mesh['band'=4,'facet'=8] {'band'}, dimensions={0}, use_global_device_ids=true | all-gather | bytes 163840 | tf_op jit(solution)/shard_map/all_gather | solution.py:100
  52.3 0.9 %copy.40 = bf16[4,2,2,16,256]{3,2,1,0,4:T(2,128)(2,1)S(1)} copy(bf16[4,2,2,16,256]{4,3,2,1,0:T(8,128)(2,1)S(1)} %all_gather.3) | data formatting | bytes 262144 | tf_op jit(solution)/shard_map/all_gather | solution.py:100
  53.2 1.2 %gather_fusion = bf16[4,2,16,128]{2,1,3,0:T(2,128)(2,1)S(1)} fusion(bf16[4,2,2,16,256]{3,2,1,0,4:T(2,128)(2,1)S(1)} %copy.40, s32[4]{0:T(128)S(1)} %get-tuple-element.22), kind=kCustom, calls=%fused_computation | custom fusion | bytes 65616 | tf_op jit(solution)/shard_map/vmap()/gather | solution.py:103
  54.5 0.1 copy.41
  54.6 1.3 %gather_fusion.1 = bf16[4,2,16,128]{2,1,3,0:T(2,128)(2,1)S(1)} fusion(bf16[4,2,2,16,256]{3,2,1,0,4:T(2,128)(2,1)S(1)} %copy.40, s32[4]{0:T(128)S(1)} %get-tuple-element.23), kind=kCustom, calls=%fused_computation.1 | custom fusion | bytes 65616 | tf_op jit(solution)/shard_map/vmap()/gather | solution.py:106
  55.9 0.1 copy.43
  56.0 9.6 %multiply_reduce_fusion = f32[4,2,2048]{2,1,0:T(2,128)} fusion(f32[4,128,2048]{2,1,0:T(8,128)} %fusion.4, f32[4,2048]{1,0:T(4,128)S(1)} %bitcast.97, bf16[4,2,16,128]{3,2,1,0:T(8,128)(2,1)S(1)} %copy.43, bf16[4,2,16,128]{3,2,1,0:T(8,128)(2,1)S(1)} %copy.41, f32[4]{0:T(128)S(1)} %bitcast.99, f32[4]{0:T(128)S(1)} %broadcast_subtract_fusion), kind=kOutput, calls=%fused_computation.2 | convolution fusion | flops 407437312 | bytes 4358176 | tf_op jit(solution)/shard_map/vmap(xrc,rv->xcv)/dot_general | solution.py:60
  (24 shorter events, 0.2 us)
Async XLA Ops:
  0.6 17.2 %copy-start.7 = (s32[12]{0:T(128)S(1)}, s32[12]{0:T(128)}, u32[]{:S(2)}) copy-start(s32[12]{0:T(128)} %param.10) | copy-start | bytes 148
  0.6 17.4 %copy-start.5 = (bf16[1,1,2,128,4096]{4,3,2,1,0:T(8,128)(2,1)S(1)}, bf16[1,1,2,128,4096]{4,3,2,1,0:T(8,128)(2,1)}, u32[]{:S(2)}) copy-start(bf16[1,1,2,128,4096]{4,3,2,1,0:T(8,128)(2,1)} %param.8) | copy-start | bytes 6291460
  0.6 17.4 %copy-start.6 = (f32[4096]{0:T(1024)S(1)}, f32[4096]{0:T(1024)}, u32[]{:S(2)}) copy-start(f32[4096]{0:T(1024)} %param.9) | copy-start | bytes 49156
  19.3 7.2 %copy-start.1 = (f32[1,1,4,2,2048]{4,3,2,1,0:T(2,128)S(1)}, f32[1,1,4,2,2048]{4,3,2,1,0:T(2,128)}, u32[]{:S(2)}) copy-start(f32[1,1,4,2,2048]{4,3,2,1,0:T(2,128)} %param.15) | copy-start | bytes 196612
  20.4 9.0 %copy-start.8 = (f32[1,1,4]{2,1,0:T(1,128)S(1)}, f32[1,1,4]{2,1,0:T(1,128)}, u32[]{:S(2)}) copy-start(f32[1,1,4]{2,1,0:T(1,128)} %param.14) | copy-start | bytes 52
  20.4 9.0 %copy-start.2 = (s32[1,1,4]{2,1,0:T(1,128)S(1)}, s32[1,1,4]{2,1,0:T(1,128)}, u32[]{:S(2)}) copy-start(s32[1,1,4]{2,1,0:T(1,128)} %param.12) | copy-start | bytes 52
  20.4 9.0 %copy-start.3 = (s32[1,1,4]{2,1,0:T(1,128)S(1)}, s32[1,1,4]{2,1,0:T(1,128)}, u32[]{:S(2)}) copy-start(s32[1,1,4]{2,1,0:T(1,128)} %param.13) | copy-start | bytes 52
  20.4 9.0 %copy-start.4 = (s32[1,1,4]{2,1,0:T(1,128)S(1)}, s32[1,1,4]{2,1,0:T(1,128)}, u32[]{:S(2)}) copy-start(s32[1,1,4]{2,1,0:T(1,128)} %param.11) | copy-start | bytes 52
  21.4 12.1 %all-to-all-start = ((bf16[16,2,16,256]{3,2,1,0:T(8,128)(2,1)}), bf16[16,2,16,256]{3,2,1,0:T(8,128)(2,1)S(1)}, u32[]{:S(2)}, u32[]{:S(2)}) async-start(bf16[16,2,16,256]{3,2,1,0:T(8,128)(2,1)} %copy.36), calls=%async_computation | async-start | bytes 524288 | tf_op jit(solution)/shard_map/all_to_all | solution.py:93
  38.5 27.1 %copy-start = (bf16[1,2,2,16,256]{4,3,2,1,0:T(8,128)(2,1)}, bf16[1,2,2,16,256]{4,3,2,1,0:T(8,128)(2,1)S(1)}, u32[]{:S(2)}) copy-start(bf16[1,2,2,16,256]{4,3,2,1,0:T(8,128)(2,1)S(1)} %copy.44) | copy-start | bytes 98308
where the time goes:
time: 65.8 us; the launch traced here: 65.6 us
  other arithmetic  21.2 us (32%)
  matrix products  16.1 us (24%)
  blocking collectives  13.8 us (21%)
  starting transfers between devices  5.17 us (8%)
  local copies, waits for them, and re-layouts  4.46 us (7%)
  waiting for transfers between devices  3.99 us (6%)
  between operations  0.94 us (1%)
    another operation x2, other arithmetic  17.7 us
    all_gather x1, blocking collectives, local(): every_band = lax.all_gather(owned[None], 'band', axis=0, tiled=True)  13.8 us
    dot_general x1, matrix products, degrid_block(): jnp.einsum('xrc,rv->xcv', patch, row_kernel, precision=highest)  9.65 us
    all_to_all x1, starting transfers between devices, local(): lax.all_to_all(every_slot, 'facet', split_axis=0, concat_axis=0, tiled=True)  5.17 us
    all_to_all x1, waiting for transfers between devices, local(): lax.all_to_all(every_slot, 'facet', split_axis=0, concat_axis=0, tiled=True)  3.99 us
    exp x1, other arithmetic, degrid_block(): jnp.exp(-col_diff * col_diff / (2.0 * kernel_sigma * kernel_sigma))  2.78 us
    gather x2, local copies, waits for them, and re-layouts, fetch(): lax.dynamic_slice(every_band, (lower_band + 1, slot, zero, zero, start),...  1.37 us
    gather x2, local copies, waits for them, and re-layouts, fetch(): lax.dynamic_slice(every_band, (lower_band, slot, zero, zero, start), (1,...  1.35 us
  transfers between devices with their start and end apart: 1, of which 1 were waited for; matrix products, arithmetic and copies ran while one was open for 4% of the time, Pallas kernels for 0%

commit v1 on v0

v1 whole, which is shorter than its diff:
```python
import functools
import math

import jax
import jax.numpy as jnp
import numpy as np
from jax import lax
from jax.experimental import pallas as pl
from jax.experimental.pallas import tpu as pltpu
from jax.sharding import PartitionSpec as P

SG = 256
CR = 16
CAP = 2
PC = 128
HALF = SG // 2

kernel_sigma = 1.5
VMEM = pl.BlockSpec(memory_space=pltpu.VMEM)
SMEM = pl.BlockSpec(memory_space=pltpu.SMEM)
ANY = pl.BlockSpec(memory_space=pl.ANY)


def send_to(k, i, n):
    return i ^ k if n & (n - 1) == 0 else (i + k) % n


def recv_from(k, i, n):
    return i ^ k if n & (n - 1) == 0 else (i - k + n) % n


def column_map(length, width):
    j = np.arange(length // 2)[:, None]
    out = []
    for parity in (0, 1):
        freq = np.arange(parity, width, 2)[None, :]
        forward = np.exp(-2j * np.pi / length * (j * freq % length)) / math.sqrt(length)
        k = np.arange(width // 2)[None, :]
        inverse = np.exp(2j * np.pi / width * (freq.T * k % width)) / math.sqrt(width)
        both = forward @ inverse
        out += [both.real, both.imag]
    return np.concatenate(out, axis=1).astype(jnp.bfloat16)


def front_kernel(
    total, chunks, slot_ref, facets_ref, window_ref, table_ref, spec_ref, phase_ref,
    strip, table, strip_sems, table_sems, subgrid_of
):
    rows, length = strip.shape
    half = length // 2
    width = half // chunks
    strip_rows = rows // 2
    copies = []
    for i in range(chunks):
        cols = pl.ds(i * width, width)
        upper = pl.ds(half + i * width, width)
        copies.append((
            pltpu.make_async_copy(facets_ref.at[:, cols], strip.at[:, cols], strip_sems.at[2 * i]),
            pltpu.make_async_copy(facets_ref.at[:, upper], strip.at[:, upper], strip_sems.at[2 * i + 1]),
            pltpu.make_async_copy(table_ref.at[cols], table.at[cols], table_sems.at[i]),
        ))
    for group in copies:
        for copy in group:
            copy.start()

    facet_count = lax.axis_size("facet")
    chips = facet_count // 2
    facet = lax.axis_index("facet")
    chip = facet // 2
    core = facet % 2
    slots = facet_count * CAP
    for s in range(slots):
        subgrid_of[s] = -1
    for s in range(slot_ref.shape[0]):
        subgrid_of[slot_ref[s]] = s
    step = 2.0 * math.pi / total
    lane = lax.broadcasted_iota(jnp.int32, (CR, strip_rows), 1)
    row = lax.broadcasted_iota(jnp.int32, (CR, strip_rows), 0)
    for side in range(2):
        side_facet = facet if side == 0 else facet ^ 1
        cell = side_facet * strip_rows + lane
        angle = step * lax.rem(row * cell, total).astype(jnp.float32)
        row_cos, row_sin = jnp.cos(angle), jnp.sin(angle)
        first = 2 * side * strip_rows
        left = pl.ds(first, strip_rows)
        right = pl.ds(first + strip_rows, strip_rows)
        for k in range(chips):
            owner = 2 * send_to(k, chip, chips) + core
            for c in range(CAP):
                sub = subgrid_of[owner * CAP + c]
                live = jnp.where(sub >= 0, 1.0, 0.0).astype(jnp.float32)
                base = jnp.maximum(sub, 0) * CR
                turn = step * lax.rem(base * cell[:8], total).astype(jnp.float32)
                base_cos = jnp.cos(turn) * live
                base_sin = jnp.sin(turn) * live
                base_cos = jnp.concatenate([base_cos, base_cos], axis=0)
                base_sin = jnp.concatenate([base_sin, base_sin], axis=0)
                cos = (base_cos * row_cos - base_sin * row_sin).astype(jnp.bfloat16)
                sin = (base_sin * row_cos + base_cos * row_sin).astype(jnp.bfloat16)
                at = (k * CAP + c) * 2 * CR
                phase_ref[pl.ds(at, CR), left] = cos
                phase_ref[pl.ds(at, CR), right] = sin
                phase_ref[pl.ds(at + CR, CR), left] = -sin
                phase_ref[pl.ds(at + CR, CR), right] = cos

    even = odd = None
    for i in range(chunks):
        for copy in copies[i]:
            copy.wait()
        cols = pl.ds(i * width, width)
        upper = pl.ds(half + i * width, width)
        near = strip[:, cols].astype(jnp.float32) * window_ref[:, cols]
        far = strip[:, upper].astype(jnp.float32) * window_ref[:, upper]
        even_part = jnp.dot(
            (near + far).astype(jnp.bfloat16), table[cols, :SG], preferred_element_type=jnp.float32
        )
        odd_part = jnp.dot(
            (near - far).astype(jnp.bfloat16), table[cols, SG:], preferred_element_type=jnp.float32
        )
        even = even_part if even is None else even + even_part
        odd = odd_part if odd is None else odd + odd_part
    n = strip_rows
    even_real = even[:n, :HALF] - even[n:, HALF:]
    even_imag = even[:n, HALF:] + even[n:, :HALF]
    odd_real = odd[:n, :HALF] - odd[n:, HALF:]
    odd_imag = odd[:n, HALF:] + odd[n:, :HALF]
    spec_ref[:n, :HALF] = (even_real + odd_real).astype(jnp.bfloat16)
    spec_ref[:n, HALF:] = (even_real - odd_real).astype(jnp.bfloat16)
    spec_ref[n:, :HALF] = (even_imag + odd_imag).astype(jnp.bfloat16)
    spec_ref[n:, HALF:] = (even_imag - odd_imag).astype(jnp.bfloat16)


def term_kernel(scale, phase_ref, own_ref, other_ref, *out_refs):
    depth = own_ref.shape[0]
    terms = jnp.dot(phase_ref[:, :depth], own_ref[...], preferred_element_type=jnp.float32)
    terms += jnp.dot(phase_ref[:, depth:], other_ref[...], preferred_element_type=jnp.float32)
    terms = (terms * scale).astype(jnp.bfloat16)
    height = CAP * 2 * CR
    for k, out_ref in enumerate(out_refs):
        out_ref[...] = terms[k * height : (k + 1) * height]


def weights_kernel(pos_ref, col_ref, row_ref):
    blocks, width, points = col_ref.shape
    factor = -1.0 / (2.0 * kernel_sigma * kernel_sigma)
    tile = 512
    for v in range(blocks):
        for t in range(0, points, tile):
            at = pl.ds(t, tile)
            diff = lax.broadcasted_iota(jnp.int32, (CR, tile), 0).astype(jnp.float32) - (
                pos_ref[v, 0:1, at] * (CR - 1.0)
            )
            row_ref[v, :, at] = jnp.exp(diff * diff * factor)
            diff = lax.broadcasted_iota(jnp.int32, (width, tile), 0).astype(jnp.float32) - (
                pos_ref[v, 1:2, at] * (width - 1.0)
            )
            col_ref[v, :, at] = jnp.exp(diff * diff * factor).astype(jnp.bfloat16)


def degrid_kernel(bands, slot_ref, band_ref, offset_ref, weight_ref, col_ref, row_ref, *refs):
    sub_refs, out_ref, every = refs[:bands], refs[bands], refs[bands + 1]
    me = lax.axis_index("band")
    for k in range(bands):
        every[recv_from(k, me, bands)] = sub_refs[k][...].astype(jnp.float32)
    blocks = col_ref.shape[0]
    for v in range(blocks):
        low = band_ref[v]
        at = pl.ds(pl.multiple_of(slot_ref[v] * 2 * CR, 2 * CR), 2 * CR)
        weight = weight_ref[v]
        patch = (1.0 - weight) * every[low, at, :] + weight * every[low + 1, at, :]
        patch = pltpu.roll(patch, lax.rem(SG - offset_ref[v], SG), 1)[:, :PC].astype(jnp.bfloat16)
        partial = jnp.dot(patch, col_ref[v], preferred_element_type=jnp.float32)
        out_ref[v, 0:1, :] = jnp.sum(partial[:CR] * row_ref[v], axis=0, keepdims=True)
        out_ref[v, 1:2, :] = jnp.sum(partial[CR:] * row_ref[v], axis=0, keepdims=True)


def local(
    facets, col_window, slot_of_subgrid, block_slot, block_band, block_offset, block_weight, vis_pos
):
    facet_count = lax.axis_size("facet")
    band_count = lax.axis_size("band")
    chips = facet_count // 2
    strip_rows = facets.shape[3]
    length = facets.shape[4]
    sky_rows = facet_count * strip_rows
    blocks, points = vis_pos.shape[2], vis_pos.shape[4]
    height = CAP * 2 * CR
    chunks = 4

    strip = facets.reshape(2 * strip_rows, length)
    table = jnp.asarray(column_map(length, SG))
    spectrum, phases = pl.pallas_call(
        functools.partial(front_kernel, sky_rows, chunks),
        out_shape=(
            jax.ShapeDtypeStruct((2 * strip_rows, SG), jnp.bfloat16),
            jax.ShapeDtypeStruct((chips * height, 4 * strip_rows), jnp.bfloat16),
        ),
        in_specs=[SMEM, ANY, VMEM, ANY],
        out_specs=(VMEM, VMEM),
        scratch_shapes=[
            pltpu.VMEM((2 * strip_rows, length), jnp.bfloat16),
            pltpu.VMEM((length // 2, 2 * SG), jnp.bfloat16),
            pltpu.SemaphoreType.DMA((2 * chunks,)),
            pltpu.SemaphoreType.DMA((chunks,)),
            pltpu.SMEM((facet_count * CAP,), jnp.int32),
        ],
        compiler_params=pltpu.CompilerParams(vmem_limit_bytes=32 * 2**20),
        name="front",
    )(slot_of_subgrid, strip, col_window.reshape(1, length), table)

    other = lax.ppermute(spectrum, "facet", [(i, i ^ 1) for i in range(facet_count)])
    term_shape = jax.ShapeDtypeStruct((height, SG), jnp.bfloat16)
    terms = pl.pallas_call(
        functools.partial(term_kernel, 1.0 / math.sqrt(sky_rows)),
        out_shape=(term_shape,) * chips,
        in_specs=[VMEM] * 3,
        out_specs=(VMEM,) * chips,
        compiler_params=pltpu.CompilerParams(vmem_limit_bytes=16 * 2**20),
        name="terms",
    )(phases, spectrum, other)
    arrived = [terms[0]] + [
        lax.ppermute(
            terms[k],
            "facet",
            [(i, 2 * send_to(k, i // 2, chips) + i % 2) for i in range(facet_count)],
        )
        for k in range(1, chips)
    ]
    total = arrived[0].astype(jnp.float32)
    for part in arrived[1:]:
        total = total + part.astype(jnp.float32)
    owned = total.astype(jnp.bfloat16)

    col_kernel, row_kernel = pl.pallas_call(
        weights_kernel,
        out_shape=(
            jax.ShapeDtypeStruct((blocks, PC, points), jnp.bfloat16),
            jax.ShapeDtypeStruct((blocks, CR, points), jnp.float32),
        ),
        in_specs=[VMEM],
        out_specs=(VMEM, VMEM),
        compiler_params=pltpu.CompilerParams(vmem_limit_bytes=16 * 2**20),
        cost_estimate=pl.CostEstimate(flops=8 * blocks * PC * points, bytes_accessed=0, transcendentals=blocks * PC * points),
        name="weights",
    )(vis_pos.reshape(blocks, 2, points))

    subs = [owned] + [
        lax.ppermute(owned, "band", [(i, send_to(k, i, band_count)) for i in range(band_count)])
        for k in range(1, band_count)
    ]
    visible = pl.pallas_call(
        functools.partial(degrid_kernel, band_count),
        out_shape=jax.ShapeDtypeStruct((blocks, 2, points), jnp.float32),
        in_specs=[SMEM] * 4 + [VMEM] * (2 + band_count),
        out_specs=VMEM,
        scratch_shapes=[pltpu.VMEM((band_count, height, SG), jnp.float32)],
        compiler_params=pltpu.CompilerParams(vmem_limit_bytes=24 * 2**20),
        name="degrid",
    )(
        block_slot.reshape(blocks), block_band.reshape(blocks), block_offset.reshape(blocks),
        block_weight.reshape(blocks), col_kernel, row_kernel, *subs
    )
    return (
        owned.reshape(1, CAP, 2, CR, SG),
        visible.reshape(1, 1, blocks, 2, points),
    )


def solution(mesh):
    in_specs = (
        P("band", "facet", None, None, None),
        P(),
        P(),
        P("band", "facet", None),
        P("band", "facet", None),
        P("band", "facet", None),
        P("band", "facet", None),
        P("band", "facet", None, None, None),
    )
    out_specs = (P("band", "facet", None, None, None), P("band", "facet", None, None, None))
    return jax.shard_map(local, mesh=mesh, in_specs=in_specs, out_specs=out_specs, check_vma=False)
```

time: 65.8 us -> 29.3 us (0.45)
  other arithmetic: 21.2 us -> 0.02 us
  matrix products: 16.1 us -> 0 us
  blocking collectives: 13.8 us -> 0 us
  Pallas kernels: 0 us -> 5.37 us
  waiting for transfers between devices: 3.99 us -> 8.95 us
  starting transfers between devices: 5.17 us -> 9.4 us
    another operation x5 -> x0, other arithmetic: 17.9 us -> none
    dot_general x7 -> x0, matrix products: 16.1 us -> none  [the longest x1 9.65 us: degrid_block(): jnp.einsum('xrc,rv->xcv', patch, row_kernel, precision=highest)]
    all_gather x1 -> x0, blocking collectives: 13.8 us -> none  [local(): every_band = lax.all_gather(owned[None], 'band', axis=0, tiled=True)]
    ppermute x0 -> x7, starting transfers between devices: none -> 9.4 us  [the longest x3 4.45 us: local(): lax.ppermute(terms[k], 'facet', [(i, 2 * send_to(k, i // 2, chips) + i %...]
    ppermute x0 -> x7, waiting for transfers between devices: none -> 8.95 us  [the longest x3 4.79 us: local(): lax.ppermute(terms[k], 'facet', [(i, 2 * send_to(k, i // 2, chips) + i %...]
    pallas_call x0 -> x4, Pallas kernels: none -> 5.37 us  [the longest x1 2.56 us: local(): pl.pallas_call(functools.partial(front_kernel, sky_rows, chunks), out_sha...]
    all_to_all x1 -> x0, starting transfers between devices: 5.17 us -> none  [local(): lax.all_to_all(every_slot, 'facet', split_axis=0, concat_axis=0, tiled=True)]
    unnamed x21 -> x20, local copies, waits for them, and re-layouts: 0.08 us -> 4.58 us
  transfers between devices with their start and end apart: 1 -> 7, of which waited for: 1 -> 6; matrix products, arithmetic and copies ran while one was open for 4% -> 0% of each run, Pallas kernels for 0% -> 3%
where the time goes in v1:
time: 29.3 us; the launch traced here: 29 us
  starting transfers between devices  9.4 us (32%)
  waiting for transfers between devices  8.95 us (31%)
  Pallas kernels  5.37 us (18%)
  local copies, waits for them, and re-layouts  4.58 us (16%)
  between operations  0.73 us (2%)
    ppermute x3, waiting for transfers between devices, local(): lax.ppermute(terms[k], 'facet', [(i, 2 * send_to(k, i // 2, chips) + i %...  4.79 us
    unnamed x20, local copies, waits for them, and re-layouts  4.58 us
    ppermute x3, starting transfers between devices, local(): lax.ppermute(terms[k], 'facet', [(i, 2 * send_to(k, i // 2, chips) + i %...  4.45 us
    ppermute x3, starting transfers between devices, local(): lax.ppermute(owned, 'band', [(i, send_to(k, i, band_count)) for i in rang...  4.45 us
    ppermute x3, waiting for transfers between devices, local(): lax.ppermute(owned, 'band', [(i, send_to(k, i, band_count)) for i in rang...  3.17 us
    pallas_call x1, Pallas kernels, local(): pl.pallas_call(functools.partial(front_kernel, sky_rows, chunks), out_sha...  2.56 us
    pallas_call x1, Pallas kernels, local(): pl.pallas_call(functools.partial(degrid_kernel, band_count), out_shape=ja...  1.72 us
    ppermute x1, waiting for transfers between devices, local(): lax.ppermute(spectrum, 'facet', [(i, i ^ 1) for i in range(facet_count)])  0.99 us
  transfers between devices with their start and end apart: 7, of which 6 were waited for; matrix products, arithmetic and copies ran while one was open for 0% of the time, Pallas kernels for 3%

profile of v1, /device:TPU:0, one launch (start us, length us, event | category | flops | bytes accessed | tf_op | source)
XLA Modules:
  0.0 29.0 jit_solution(14132315795163211856)
XLA Ops:
  0.6 0.0 copy-start
  0.6 1.6 %copy-done = bf16[1,1,2,128,4096]{4,3,2,1,0:T(8,128)(2,1)S(1)} copy-done((bf16[1,1,2,128,4096]{4,3,2,1,0:T(8,128)(2,1)S(1)}, bf16[1,1,2,128,4096]{4,3,2,1,0:T(8,128)(2,1)}, u32[]{:S(2)}) %copy-start) | copy-done | bytes 2097176
  2.2 1.6 %copy-done.1 = bf16[2048,512]{1,0:T(8,128)(2,1)S(1)} copy-done((bf16[2048,512]{1,0:T(8,128)(2,1)S(1)}, bf16[2048,512]{1,0:T(8,128)(2,1)}, u32[]{:S(2)}) %copy-start.1) | copy-done | bytes 2097176
  3.8 0.7 %copy-done.3 = f32[4096]{0:T(1024)S(1)} copy-done((f32[4096]{0:T(1024)S(1)}, f32[4096]{0:T(1024)}, u32[]{:S(2)}) %copy-start.3) | copy-done | bytes 16408
  4.5 0.7 %copy-done.4 = s32[12]{0:T(128)S(1)} copy-done((s32[12]{0:T(128)S(1)}, s32[12]{0:T(128)}, u32[]{:S(2)}) %copy-start.4) | copy-done | bytes 72
  5.2 2.6 %front.1 = (bf16[256,256]{1,0:T(8,128)(2,1)S(1)}, bf16[256,512]{1,0:T(8,128)(2,1)S(1)}) custom-call(s32[12]{0:T(128)S(1)} %copy-done.4, bf16[256,4096]{1,0:T(8,128)(2,1)S(1)} %bitcast.9, f32[1,4096]{1,0:T(1,128)S(1)} %bitcast.11, bf16[2048,512]{1,0:T(8,128)(2,1)S(1)} %copy-done.1), custom_call_target="tpu_custom_call" | custom-call | tf_op jit(solution)/shard_map/front/pallas_call | solution.py:192
  7.8 0.0 copy-start.5
  7.8 0.0 copy-start.6
  7.8 0.0 copy-start.7
  7.8 0.0 copy-start.8
  7.8 0.5 %collective-permute-start = (bf16[256,256]{1,0:T(8,128)(2,1)S(1)}, bf16[256,256]{1,0:T(8,128)(2,1)S(1)}, u32[]{:S(2)}, u32[]{:S(2)}) collective-permute-start(bf16[256,256]{1,0:T(8,128)(2,1)S(1)} %get-tuple-element.11.own_ref), channel_id=1, source_target_pairs={{0,1},{1,0},{2,3},{3,2},{4,5},{5,4},{6,7},{7,6},{8,9},{9,8},{10,11... | collective-permute-start | bytes 393224 | tf_op jit(solution)/shard_map/ppermute | solution.py:211
  8.3 1.0 %collective-permute-done.other_ref = bf16[256,256]{1,0:T(8,128)(2,1)S(1)} collective-permute-done((bf16[256,256]{1,0:T(8,128)(2,1)S(1)}, bf16[256,256]{1,0:T(8,128)(2,1)S(1)}, u32[]{:S(2)}, u32[]{:S(2)}) %collective-permute-start) | collective-permute-done | bytes 131104 | tf_op jit(solution)/shard_map/ppermute | solution.py:211
  9.3 0.2 terms.1
  9.5 2.9 %collective-permute-start.1 = (bf16[64,256]{1,0:T(8,128)(2,1)S(1)}, bf16[64,256]{1,0:T(8,128)(2,1)S(1)}, u32[]{:S(2)}, u32[]{:S(2)}) collective-permute-start(bf16[64,256]{1,0:T(8,128)(2,1)S(1)} %get-tuple-element.13), channel_id=1, source_target_pairs={{0,2},{1,3},{2,0},{3,1},{4,6},{5,7},{6,4},{7,5},{8,10},{9,11},{10,... | collective-permute-start | bytes 98312 | tf_op jit(solution)/shard_map/ppermute | solution.py:222
  12.4 1.5 %collective-permute-start.2 = (bf16[64,256]{1,0:T(8,128)(2,1)S(1)}, bf16[64,256]{1,0:T(8,128)(2,1)S(1)}, u32[]{:S(2)}, u32[]{:S(2)}) collective-permute-start(bf16[64,256]{1,0:T(8,128)(2,1)S(1)} %get-tuple-element.14), channel_id=1, source_target_pairs={{0,4},{1,5},{2,6},{3,7},{4,0},{5,1},{6,2},{7,3},{8,12},{9,13},{10,... | collective-permute-start | bytes 98312 | tf_op jit(solution)/shard_map/ppermute | solution.py:222
  13.9 0.0 collective-permute-start.3
  14.0 0.4 %collective-permute-done.1 = bf16[64,256]{1,0:T(8,128)(2,1)S(1)} collective-permute-done((bf16[64,256]{1,0:T(8,128)(2,1)S(1)}, bf16[64,256]{1,0:T(8,128)(2,1)S(1)}, u32[]{:S(2)}, u32[]{:S(2)}) %collective-permute-start.1) | collective-permute-done | bytes 32800 | tf_op jit(solution)/shard_map/ppermute | solution.py:222
  14.3 2.0 %collective-permute-done.2 = bf16[64,256]{1,0:T(8,128)(2,1)S(1)} collective-permute-done((bf16[64,256]{1,0:T(8,128)(2,1)S(1)}, bf16[64,256]{1,0:T(8,128)(2,1)S(1)}, u32[]{:S(2)}, u32[]{:S(2)}) %collective-permute-start.2) | collective-permute-done | bytes 32800 | tf_op jit(solution)/shard_map/ppermute | solution.py:222
  16.3 2.4 %collective-permute-done.3 = bf16[64,256]{1,0:T(8,128)(2,1)S(1)} collective-permute-done((bf16[64,256]{1,0:T(8,128)(2,1)S(1)}, bf16[64,256]{1,0:T(8,128)(2,1)S(1)}, u32[]{:S(2)}, u32[]{:S(2)}) %collective-permute-start.3) | collective-permute-done | bytes 32800 | tf_op jit(solution)/shard_map/ppermute | solution.py:222
  18.8 0.0 copy-start.2
  18.8 3.7 %collective-permute-start.6 = (bf16[64,256]{1,0:T(8,128)(2,1)S(1)}, bf16[64,256]{1,0:T(8,128)(2,1)S(1)}, u32[]{:S(2)}, u32[]{:S(2)}) collective-permute-start(bf16[64,256]{1,0:T(8,128)(2,1)S(1)} %add_convert_fusion.refs_0_), channel_id=1, source_target_pairs={{0,24},{8,16},{16,8},{24,0},{1,25},{9,17},{17,9},{25,1},{2,26},{10... | collective-permute-start | bytes 98312 | tf_op jit(solution)/shard_map/ppermute | solution.py:248
  22.5 0.0 collective-permute-start.5
  22.5 0.8 %collective-permute-start.4 = (bf16[64,256]{1,0:T(8,128)(2,1)S(1)}, bf16[64,256]{1,0:T(8,128)(2,1)S(1)}, u32[]{:S(2)}, u32[]{:S(2)}) collective-permute-start(bf16[64,256]{1,0:T(8,128)(2,1)S(1)} %add_convert_fusion.refs_0_), channel_id=1, source_target_pairs={{0,8},{8,0},{16,24},{24,16},{1,9},{9,1},{17,25},{25,17},{2,10},{10... | collective-permute-start | bytes 98312 | tf_op jit(solution)/shard_map/ppermute | solution.py:248
  23.3 0.0 copy-done.9
  23.3 0.9 %weights.1 = (bf16[4,128,2048]{2,1,0:T(8,128)(2,1)S(1)}, f32[4,16,2048]{2,1,0:T(8,128)S(1)}) custom-call(f32[4,2,2048]{2,1,0:T(2,128)S(1)} %bitcast.16), custom_call_target="tpu_custom_call" | custom-call | flops 8388608 | tf_op jit(solution)/shard_map/weights/pallas_call | solution.py:234
  24.1 0.6 %collective-permute-done.6.refs_3_ = bf16[64,256]{1,0:T(8,128)(2,1)S(1)} collective-permute-done((bf16[64,256]{1,0:T(8,128)(2,1)S(1)}, bf16[64,256]{1,0:T(8,128)(2,1)S(1)}, u32[]{:S(2)}, u32[]{:S(2)}) %collective-permute-start.6) | collective-permute-done | bytes 32800 | tf_op jit(solution)/shard_map/ppermute | solution.py:248
  24.7 2.6 %collective-permute-done.5.refs_2_ = bf16[64,256]{1,0:T(8,128)(2,1)S(1)} collective-permute-done((bf16[64,256]{1,0:T(8,128)(2,1)S(1)}, bf16[64,256]{1,0:T(8,128)(2,1)S(1)}, u32[]{:S(2)}, u32[]{:S(2)}) %collective-permute-start.5) | collective-permute-done | bytes 32800 | tf_op jit(solution)/shard_map/ppermute | solution.py:248
  27.3 0.0 collective-permute-done.4.refs_1_
  27.3 0.0 copy-done.6
  27.3 0.0 copy-done.7
  27.3 0.0 copy-done.8
  27.3 1.7 %degrid.1 = f32[4,2,2048]{2,1,0:T(2,128)} custom-call(s32[4]{0:T(128)S(1)} %bitcast.12, s32[4]{0:T(128)S(1)} %bitcast.13, s32[4]{0:T(128)S(1)} %bitcast.14, f32[4]{0:T(128)S(1)} %bitcast.15, bf16[4,128,2048]{2,1,0:T(8,128)(2,1)S(1)} %get-tuple-element.16.col_ref, f32[4,16,2048]{2,1,0:T(8,128)S(1)} %get-tuple-element.17.row_ref, ...), custom_call_target="tpu_custom_call" | custom-call | tf_op jit(solution)/shard_map/degrid/pallas_call | solution.py:251
  (7 shorter events, 0.0 us)
Async XLA Ops:
  0.6 1.6 %copy-start = (bf16[1,1,2,128,4096]{4,3,2,1,0:T(8,128)(2,1)S(1)}, bf16[1,1,2,128,4096]{4,3,2,1,0:T(8,128)(2,1)}, u32[]{:S(2)}) copy-start(bf16[1,1,2,128,4096]{4,3,2,1,0:T(8,128)(2,1)} %param.9) | copy-start | bytes 6291460
  2.2 1.6 %copy-start.1 = (bf16[2048,512]{1,0:T(8,128)(2,1)S(1)}, bf16[2048,512]{1,0:T(8,128)(2,1)}, u32[]{:S(2)}) copy-start(bf16[2048,512]{1,0:T(8,128)(2,1)} %constant.2.clone.table_ref) | copy-start | bytes 6291460
  3.8 0.7 %copy-start.3 = (f32[4096]{0:T(1024)S(1)}, f32[4096]{0:T(1024)}, u32[]{:S(2)}) copy-start(f32[4096]{0:T(1024)} %param.10) | copy-start | bytes 49156
  4.5 0.7 %copy-start.4 = (s32[12]{0:T(128)S(1)}, s32[12]{0:T(128)}, u32[]{:S(2)}) copy-start(s32[12]{0:T(128)} %slot_ref.1) | copy-start | bytes 148
  5.2 18.1 %copy-start.9 = (f32[1,1,4,2,2048]{4,3,2,1,0:T(2,128)S(1)}, f32[1,1,4,2,2048]{4,3,2,1,0:T(2,128)}, u32[]{:S(2)}) copy-start(f32[1,1,4,2,2048]{4,3,2,1,0:T(2,128)} %param.16) | copy-start | bytes 196612
  7.8 19.5 %copy-start.5 = (s32[1,1,4]{2,1,0:T(1,128)S(1)}, s32[1,1,4]{2,1,0:T(1,128)}, u32[]{:S(2)}) copy-start(s32[1,1,4]{2,1,0:T(1,128)} %param.12) | copy-start | bytes 52
  7.8 19.5 %copy-start.6 = (s32[1,1,4]{2,1,0:T(1,128)S(1)}, s32[1,1,4]{2,1,0:T(1,128)}, u32[]{:S(2)}) copy-start(s32[1,1,4]{2,1,0:T(1,128)} %param.13) | copy-start | bytes 52
  7.8 19.5 %copy-start.7 = (s32[1,1,4]{2,1,0:T(1,128)S(1)}, s32[1,1,4]{2,1,0:T(1,128)}, u32[]{:S(2)}) copy-start(s32[1,1,4]{2,1,0:T(1,128)} %param.14) | copy-start | bytes 52
  7.8 19.5 %copy-start.8 = (f32[1,1,4]{2,1,0:T(1,128)S(1)}, f32[1,1,4]{2,1,0:T(1,128)}, u32[]{:S(2)}) copy-start(f32[1,1,4]{2,1,0:T(1,128)} %param.15) | copy-start | bytes 52
  7.8 1.5 %collective-permute-start = (bf16[256,256]{1,0:T(8,128)(2,1)S(1)}, bf16[256,256]{1,0:T(8,128)(2,1)S(1)}, u32[]{:S(2)}, u32[]{:S(2)}) collective-permute-start(bf16[256,256]{1,0:T(8,128)(2,1)S(1)} %get-tuple-element.11.own_ref), channel_id=1, source_target_pairs={{0,1},{1,0},{2,3},{3,2},{4,5},{5,4},{6,7},{7,6},{8,9},{9,8},{10,11... | collective-permute-start | bytes 393224 | tf_op jit(solution)/shard_map/ppermute | solution.py:211
  9.5 4.8 %collective-permute-start.1 = (bf16[64,256]{1,0:T(8,128)(2,1)S(1)}, bf16[64,256]{1,0:T(8,128)(2,1)S(1)}, u32[]{:S(2)}, u32[]{:S(2)}) collective-permute-start(bf16[64,256]{1,0:T(8,128)(2,1)S(1)} %get-tuple-element.13), channel_id=1, source_target_pairs={{0,2},{1,3},{2,0},{3,1},{4,6},{5,7},{6,4},{7,5},{8,10},{9,11},{10,... | collective-permute-start | bytes 98312 | tf_op jit(solution)/shard_map/ppermute | solution.py:222
  12.4 3.9 %collective-permute-start.2 = (bf16[64,256]{1,0:T(8,128)(2,1)S(1)}, bf16[64,256]{1,0:T(8,128)(2,1)S(1)}, u32[]{:S(2)}, u32[]{:S(2)}) collective-permute-start(bf16[64,256]{1,0:T(8,128)(2,1)S(1)} %get-tuple-element.14), channel_id=1, source_target_pairs={{0,4},{1,5},{2,6},{3,7},{4,0},{5,1},{6,2},{7,3},{8,12},{9,13},{10,... | collective-permute-start | bytes 98312 | tf_op jit(solution)/shard_map/ppermute | solution.py:222
  13.9 4.8 %collective-permute-start.3 = (bf16[64,256]{1,0:T(8,128)(2,1)S(1)}, bf16[64,256]{1,0:T(8,128)(2,1)S(1)}, u32[]{:S(2)}, u32[]{:S(2)}) collective-permute-start(bf16[64,256]{1,0:T(8,128)(2,1)S(1)} %get-tuple-element.15), channel_id=1, source_target_pairs={{0,6},{1,7},{2,4},{3,5},{4,2},{5,3},{6,0},{7,1},{8,14},{9,15},{10,... | collective-permute-start | bytes 98312 | tf_op jit(solution)/shard_map/ppermute | solution.py:222
  18.8 10.3 %copy-start.2 = (bf16[64,256]{1,0:T(8,128)(2,1)}, bf16[64,256]{1,0:T(8,128)(2,1)S(1)}, u32[]{:S(2)}) copy-start(bf16[64,256]{1,0:T(8,128)(2,1)S(1)} %add_convert_fusion.refs_0_) | copy-start | bytes 98308
  18.8 5.9 %collective-permute-start.6 = (bf16[64,256]{1,0:T(8,128)(2,1)S(1)}, bf16[64,256]{1,0:T(8,128)(2,1)S(1)}, u32[]{:S(2)}, u32[]{:S(2)}) collective-permute-start(bf16[64,256]{1,0:T(8,128)(2,1)S(1)} %add_convert_fusion.refs_0_), channel_id=1, source_target_pairs={{0,24},{8,16},{16,8},{24,0},{1,25},{9,17},{17,9},{25,1},{2,26},{10... | collective-permute-start | bytes 98312 | tf_op jit(solution)/shard_map/ppermute | solution.py:248
  22.5 4.8 %collective-permute-start.5 = (bf16[64,256]{1,0:T(8,128)(2,1)S(1)}, bf16[64,256]{1,0:T(8,128)(2,1)S(1)}, u32[]{:S(2)}, u32[]{:S(2)}) collective-permute-start(bf16[64,256]{1,0:T(8,128)(2,1)S(1)} %add_convert_fusion.refs_0_), channel_id=1, source_target_pairs={{0,16},{8,24},{16,0},{24,8},{1,17},{9,25},{17,1},{25,9},{2,18},{10... | collective-permute-start | bytes 98312 | tf_op jit(solution)/shard_map/ppermute | solution.py:248
  22.5 4.8 %collective-permute-start.4 = (bf16[64,256]{1,0:T(8,128)(2,1)S(1)}, bf16[64,256]{1,0:T(8,128)(2,1)S(1)}, u32[]{:S(2)}, u32[]{:S(2)}) collective-permute-start(bf16[64,256]{1,0:T(8,128)(2,1)S(1)} %add_convert_fusion.refs_0_), channel_id=1, source_target_pairs={{0,8},{8,0},{16,24},{24,16},{1,9},{9,1},{17,25},{25,17},{2,10},{10... | collective-permute-start | bytes 98312 | tf_op jit(solution)/shard_map/ppermute | solution.py:248

commit v2 on v1

--- a/solution.py
+++ b/solution.py
@@ -18,7 +18,7 @@
 kernel_sigma = 1.5
 VMEM = pl.BlockSpec(memory_space=pltpu.VMEM)
 SMEM = pl.BlockSpec(memory_space=pltpu.SMEM)
-ANY = pl.BlockSpec(memory_space=pl.ANY)
+HBM = pl.BlockSpec(memory_space=pltpu.HBM)
 
 
 def send_to(k, i, n):
@@ -43,13 +43,17 @@
 
 
 def front_kernel(
-    total, chunks, slot_ref, facets_ref, window_ref, table_ref, spec_ref, phase_ref,
-    strip, table, strip_sems, table_sems, subgrid_of
+    total, chunks, slot_hbm, facets_ref, window_hbm, table_ref, spec_ref, phase_ref,
+    strip, table, window_ref, slot_ref, strip_sems, table_sems, small_sems, subgrid_of
 ):
     rows, length = strip.shape
     half = length // 2
     width = half // chunks
     strip_rows = rows // 2
+    slot_copy = pltpu.make_async_copy(slot_hbm, slot_ref, small_sems.at[0])
+    window_copy = pltpu.make_async_copy(window_hbm, window_ref, small_sems.at[1])
+    slot_copy.start()
+    window_copy.start()
     copies = []
     for i in range(chunks):
         cols = pl.ds(i * width, width)
@@ -71,6 +75,7 @@
     slots = facet_count * CAP
     for s in range(slots):
         subgrid_of[s] = -1
+    slot_copy.wait()
     for s in range(slot_ref.shape[0]):
         subgrid_of[slot_ref[s]] = s
     step = 2.0 * math.pi / total
@@ -103,6 +108,7 @@
                 phase_ref[pl.ds(at + CR, CR), left] = -sin
                 phase_ref[pl.ds(at + CR, CR), right] = cos
 
+    window_copy.wait()
     even = odd = None
     for i in range(chunks):
         for copy in copies[i]:
@@ -140,36 +146,57 @@
         out_ref[...] = terms[k * height : (k + 1) * height]
 
 
-def weights_kernel(pos_ref, col_ref, row_ref):
+def weights_kernel(
+    bands, slot_ref, band_ref, offset_ref, weight_ref, pos_ref, col_ref, row_ref, mix_ref, lane_ref
+):
     blocks, width, points = col_ref.shape
     factor = -1.0 / (2.0 * kernel_sigma * kernel_sigma)
     tile = 512
+    me = lax.axis_index("band")
+    column = lax.broadcasted_iota(jnp.int32, (width, tile), 0).astype(jnp.float32)
+    row = lax.broadcasted_iota(jnp.int32, (CR, tile), 0).astype(jnp.float32)
     for v in range(blocks):
+        low = band_ref[v]
+        slot = slot_ref[v]
+        weight = weight_ref[v]
+        for k in range(bands):
+            band = recv_from(k, me, bands)
+            share = jnp.where(band == low, 1.0 - weight, jnp.where(band == low + 1, weight, 0.0))
+            for c in range(CAP):
+                mix_ref[v, k * CAP + c] = jnp.full((8, 128), jnp.where(slot == c, share, 0.0), jnp.float32)
+        lane_ref[v] = offset_ref[v] + lax.broadcasted_iota(jnp.int32, (2 * CR, PC), 1)
         for t in range(0, points, tile):
             at = pl.ds(t, tile)
-            diff = lax.broadcasted_iota(jnp.int32, (CR, tile), 0).astype(jnp.float32) - (
-                pos_ref[v, 0:1, at] * (CR - 1.0)
-            )
+            diff = row - pos_ref[v, 0:1, at] * (CR - 1.0)
             row_ref[v, :, at] = jnp.exp(diff * diff * factor)
-            diff = lax.broadcasted_iota(jnp.int32, (width, tile), 0).astype(jnp.float32) - (
-                pos_ref[v, 1:2, at] * (width - 1.0)
-            )
+            diff = column - pos_ref[v, 1:2, at] * (PC - 1.0)
             col_ref[v, :, at] = jnp.exp(diff * diff * factor).astype(jnp.bfloat16)
 
 
-def degrid_kernel(bands, slot_ref, band_ref, offset_ref, weight_ref, col_ref, row_ref, *refs):
-    sub_refs, out_ref, every = refs[:bands], refs[bands], refs[bands + 1]
-    me = lax.axis_index("band")
-    for k in range(bands):
-        every[recv_from(k, me, bands)] = sub_refs[k][...].astype(jnp.float32)
-    blocks = col_ref.shape[0]
-    for v in range(blocks):
-        low = band_ref[v]
-        at = pl.ds(pl.multiple_of(slot_ref[v] * 2 * CR, 2 * CR), 2 * CR)
-        weight = weight_ref[v]
-        patch = (1.0 - weight) * every[low, at, :] + weight * every[low + 1, at, :]
-        patch = pltpu.roll(patch, lax.rem(SG - offset_ref[v], SG), 1)[:, :PC].astype(jnp.bfloat16)
-        partial = jnp.dot(patch, col_ref[v], preferred_element_type=jnp.float32)
+def degrid_kernel(bands, mix_ref, lane_ref, col_ref, row_ref, *refs):
+    sub_refs, out_ref = refs[:bands], refs[bands]
+    height = 2 * CR
+    held = [
+        sub_refs[k][c * height : (c + 1) * height, :].astype(jnp.float32)
+        for k in range(bands)
+        for c in range(CAP)
+    ]
+    for v in range(col_ref.shape[0]):
+        halves = []
+        for first in (0, HALF):
+            mixed = None
+            for i, sub in enumerate(held):
+                share = jnp.concatenate([mix_ref[v, i]] * (height // 8), axis=0)
+                part = sub[:, first : first + HALF] * share
+                mixed = part if mixed is None else mixed + part
+            halves.append(mixed)
+        lane = lane_ref[v]
+        within = lax.rem(lane, HALF)
+        near, far = (jnp.take_along_axis(half, within, axis=1, mode="promise_in_bounds") for half in halves)
+        patch = jnp.where(lane < HALF, near, far)
+        partial = jnp.dot(
+            patch.astype(jnp.bfloat16), col_ref[v], preferred_element_type=jnp.float32
+        )
         out_ref[v, 0:1, :] = jnp.sum(partial[:CR] * row_ref[v], axis=0, keepdims=True)
         out_ref[v, 1:2, :] = jnp.sum(partial[CR:] * row_ref[v], axis=0, keepdims=True)
 
@@ -195,18 +222,24 @@
             jax.ShapeDtypeStruct((2 * strip_rows, SG), jnp.bfloat16),
             jax.ShapeDtypeStruct((chips * height, 4 * strip_rows), jnp.bfloat16),
         ),
-        in_specs=[SMEM, ANY, VMEM, ANY],
+        in_specs=[HBM] * 4,
         out_specs=(VMEM, VMEM),
         scratch_shapes=[
             pltpu.VMEM((2 * strip_rows, length), jnp.bfloat16),
             pltpu.VMEM((length // 2, 2 * SG), jnp.bfloat16),
+            pltpu.VMEM((1, length), jnp.float32),
+            pltpu.SMEM(slot_of_subgrid.shape, jnp.int32),
             pltpu.SemaphoreType.DMA((2 * chunks,)),
             pltpu.SemaphoreType.DMA((chunks,)),
+            pltpu.SemaphoreType.DMA((2,)),
             pltpu.SMEM((facet_count * CAP,), jnp.int32),
         ],
         compiler_params=pltpu.CompilerParams(vmem_limit_bytes=32 * 2**20),
         name="front",
-    )(slot_of_subgrid, strip, col_window.reshape(1, length), table)
+    )(*(
+        pltpu.with_memory_space_constraint(x, pltpu.HBM)
+        for x in (slot_of_subgrid, strip, col_window.reshape(1, length), table)
+    ))
 
     other = lax.ppermute(spectrum, "facet", [(i, i ^ 1) for i in range(facet_count)])
     term_shape = jax.ShapeDtypeStruct((height, SG), jnp.bfloat16)
@@ -231,18 +264,25 @@
         total = total + part.astype(jnp.float32)
     owned = total.astype(jnp.bfloat16)
 
-    col_kernel, row_kernel = pl.pallas_call(
-        weights_kernel,
+    col_kernel, row_kernel, mix, lanes = pl.pallas_call(
+        functools.partial(weights_kernel, band_count),
         out_shape=(
             jax.ShapeDtypeStruct((blocks, PC, points), jnp.bfloat16),
             jax.ShapeDtypeStruct((blocks, CR, points), jnp.float32),
+            jax.ShapeDtypeStruct((blocks, band_count * CAP, 8, 128), jnp.float32),
+            jax.ShapeDtypeStruct((blocks, 2 * CR, PC), jnp.int32),
         ),
-        in_specs=[VMEM],
-        out_specs=(VMEM, VMEM),
+        in_specs=[SMEM] * 4 + [VMEM],
+        out_specs=(VMEM,) * 4,
         compiler_params=pltpu.CompilerParams(vmem_limit_bytes=16 * 2**20),
-        cost_estimate=pl.CostEstimate(flops=8 * blocks * PC * points, bytes_accessed=0, transcendentals=blocks * PC * points),
+        cost_estimate=pl.CostEstimate(
+            flops=8 * blocks * PC * points, bytes_accessed=0, transcendentals=blocks * PC * points
+        ),
         name="weights",
-    )(vis_pos.reshape(blocks, 2, points))
+    )(
+        block_slot.reshape(blocks), block_band.reshape(blocks), block_offset.reshape(blocks),
+        block_weight.reshape(blocks), vis_pos.reshape(blocks, 2, points),
+    )
 
     subs = [owned] + [
         lax.ppermute(owned, "band", [(i, send_to(k, i, band_count)) for i in range(band_count)])
@@ -251,15 +291,11 @@
     visible = pl.pallas_call(
         functools.partial(degrid_kernel, band_count),
         out_shape=jax.ShapeDtypeStruct((blocks, 2, points), jnp.float32),
-        in_specs=[SMEM] * 4 + [VMEM] * (2 + band_count),
+        in_specs=[VMEM] * (4 + band_count),
         out_specs=VMEM,
-        scratch_shapes=[pltpu.VMEM((band_count, height, SG), jnp.float32)],
         compiler_params=pltpu.CompilerParams(vmem_limit_bytes=24 * 2**20),
         name="degrid",
-    )(
-        block_slot.reshape(blocks), block_band.reshape(blocks), block_offset.reshape(blocks),
-        block_weight.reshape(blocks), col_kernel, row_kernel, *subs
-    )
+    )(mix, lanes, col_kernel, row_kernel, *subs)
     return (
         owned.reshape(1, CAP, 2, CR, SG),
         visible.reshape(1, 1, blocks, 2, points),

time: 29.3 us -> 24.5 us (0.84)
  local copies, waits for them, and re-layouts: 4.58 us -> 0.03 us
  waiting for transfers between devices: 8.95 us -> 8.34 us
  Pallas kernels: 5.37 us -> 5.83 us
    unnamed x20 -> x12, local copies, waits for them, and re-layouts: 4.58 us -> 0.03 us
    ppermute x3, waiting for transfers between devices: 3.17 us -> 2.56 us  [local(): lax.ppermute(owned, 'band', [(i, send_to(k, i, band_count)) for i in rang...]
    pallas_call x1, Pallas kernels: 1.72 us -> 1.14 us  [local(): pl.pallas_call(functools.partial(degrid_kernel, band_count), out_shape=ja...]
    pallas_call x1, Pallas kernels: 0.87 us -> 1.43 us  [local(): pl.pallas_call(functools.partial(weights_kernel, band_count), out_shape=(...]
    pallas_call x1, Pallas kernels: 2.56 us -> 3.04 us  [local(): pl.pallas_call(functools.partial(front_kernel, sky_rows, chunks), out_sha...]
  transfers between devices with their start and end apart: 7 -> 7, of which waited for: 6 -> 5; matrix products, arithmetic and copies ran while one was open for 0% -> 0% of each run, Pallas kernels for 3% -> 6%
where the time goes in v2:
time: 24.5 us; the launch traced here: 24.4 us
  starting transfers between devices  9.43 us (38%)
  waiting for transfers between devices  8.34 us (34%)
  Pallas kernels  5.83 us (24%)
  between operations  0.73 us (3%)
    ppermute x3, waiting for transfers between devices, local(): lax.ppermute(terms[k], 'facet', [(i, 2 * send_to(k, i // 2, chips) + i %...  4.79 us
    ppermute x3, starting transfers between devices, local(): lax.ppermute(terms[k], 'facet', [(i, 2 * send_to(k, i // 2, chips) + i %...  4.46 us
    ppermute x3, starting transfers between devices, local(): lax.ppermute(owned, 'band', [(i, send_to(k, i, band_count)) for i in rang...  4.45 us
    pallas_call x1, Pallas kernels, local(): pl.pallas_call(functools.partial(front_kernel, sky_rows, chunks), out_sha...  3.04 us
    ppermute x3, waiting for transfers between devices, local(): lax.ppermute(owned, 'band', [(i, send_to(k, i, band_count)) for i in rang...  2.56 us
    pallas_call x1, Pallas kernels, local(): pl.pallas_call(functools.partial(weights_kernel, band_count), out_shape=(...  1.43 us
    pallas_call x1, Pallas kernels, local(): pl.pallas_call(functools.partial(degrid_kernel, band_count), out_shape=ja...  1.14 us
    ppermute x1, waiting for transfers between devices, local(): lax.ppermute(spectrum, 'facet', [(i, i ^ 1) for i in range(facet_count)])  0.99 us
  transfers between devices with their start and end apart: 7, of which 5 were waited for; matrix products, arithmetic and copies ran while one was open for 0% of the time, Pallas kernels for 6%

profile of v2, /device:TPU:0, one launch (start us, length us, event | category | flops | bytes accessed | tf_op | source)
XLA Modules:
  0.0 24.4 jit_solution(12877984438196468908)
XLA Ops:
  0.6 0.0 copy-start.1
  0.6 0.0 copy-start.2
  0.7 0.0 copy-start.3
  0.7 0.0 copy-start.4
  0.7 0.0 copy-start.5
  0.7 3.0 %front.1 = (bf16[256,256]{1,0:T(8,128)(2,1)S(1)}, bf16[256,512]{1,0:T(8,128)(2,1)S(1)}) custom-call(s32[12]{0:T(128)} %slot_hbm.1, bf16[256,4096]{1,0:T(8,128)(2,1)} %bitcast.15, f32[1,4096]{1,0:T(1,128)} %bitcast.17, bf16[2048,512]{1,0:T(8,128)(2,1)} %constant.2.clone.table_ref), custom_call_target="tpu_custom_call" | custom-call | tf_op jit(solution)/shard_map/front/pallas_call | solution.py:219
  3.7 0.5 %collective-permute-start = (bf16[256,256]{1,0:T(8,128)(2,1)S(1)}, bf16[256,256]{1,0:T(8,128)(2,1)S(1)}, u32[]{:S(2)}, u32[]{:S(2)}) collective-permute-start(bf16[256,256]{1,0:T(8,128)(2,1)S(1)} %get-tuple-element.13.own_ref), channel_id=1, source_target_pairs={{0,1},{1,0},{2,3},{3,2},{4,5},{5,4},{6,7},{7,6},{8,9},{9,8},{10,11... | collective-permute-start | bytes 393224 | tf_op jit(solution)/shard_map/ppermute | solution.py:244
  4.2 1.0 %collective-permute-done.other_ref = bf16[256,256]{1,0:T(8,128)(2,1)S(1)} collective-permute-done((bf16[256,256]{1,0:T(8,128)(2,1)S(1)}, bf16[256,256]{1,0:T(8,128)(2,1)S(1)}, u32[]{:S(2)}, u32[]{:S(2)}) %collective-permute-start) | collective-permute-done | bytes 131104 | tf_op jit(solution)/shard_map/ppermute | solution.py:244
  5.2 0.2 terms.1
  5.5 2.9 %collective-permute-start.1 = (bf16[64,256]{1,0:T(8,128)(2,1)S(1)}, bf16[64,256]{1,0:T(8,128)(2,1)S(1)}, u32[]{:S(2)}, u32[]{:S(2)}) collective-permute-start(bf16[64,256]{1,0:T(8,128)(2,1)S(1)} %get-tuple-element.15), channel_id=1, source_target_pairs={{0,2},{1,3},{2,0},{3,1},{4,6},{5,7},{6,4},{7,5},{8,10},{9,11},{10,... | collective-permute-start | bytes 98312 | tf_op jit(solution)/shard_map/ppermute | solution.py:255
  8.4 1.5 %collective-permute-start.2 = (bf16[64,256]{1,0:T(8,128)(2,1)S(1)}, bf16[64,256]{1,0:T(8,128)(2,1)S(1)}, u32[]{:S(2)}, u32[]{:S(2)}) collective-permute-start(bf16[64,256]{1,0:T(8,128)(2,1)S(1)} %get-tuple-element.16), channel_id=1, source_target_pairs={{0,4},{1,5},{2,6},{3,7},{4,0},{5,1},{6,2},{7,3},{8,12},{9,13},{10,... | collective-permute-start | bytes 98312 | tf_op jit(solution)/shard_map/ppermute | solution.py:255
  9.9 0.0 collective-permute-start.3
  9.9 0.4 %collective-permute-done.1 = bf16[64,256]{1,0:T(8,128)(2,1)S(1)} collective-permute-done((bf16[64,256]{1,0:T(8,128)(2,1)S(1)}, bf16[64,256]{1,0:T(8,128)(2,1)S(1)}, u32[]{:S(2)}, u32[]{:S(2)}) %collective-permute-start.1) | collective-permute-done | bytes 32800 | tf_op jit(solution)/shard_map/ppermute | solution.py:255
  10.3 2.0 %collective-permute-done.2 = bf16[64,256]{1,0:T(8,128)(2,1)S(1)} collective-permute-done((bf16[64,256]{1,0:T(8,128)(2,1)S(1)}, bf16[64,256]{1,0:T(8,128)(2,1)S(1)}, u32[]{:S(2)}, u32[]{:S(2)}) %collective-permute-start.2) | collective-permute-done | bytes 32800 | tf_op jit(solution)/shard_map/ppermute | solution.py:255
  12.3 2.4 %collective-permute-done.3 = bf16[64,256]{1,0:T(8,128)(2,1)S(1)} collective-permute-done((bf16[64,256]{1,0:T(8,128)(2,1)S(1)}, bf16[64,256]{1,0:T(8,128)(2,1)S(1)}, u32[]{:S(2)}, u32[]{:S(2)}) %collective-permute-start.3) | collective-permute-done | bytes 32800 | tf_op jit(solution)/shard_map/ppermute | solution.py:255
  14.7 0.0 copy-start
  14.8 3.7 %collective-permute-start.6 = (bf16[64,256]{1,0:T(8,128)(2,1)S(1)}, bf16[64,256]{1,0:T(8,128)(2,1)S(1)}, u32[]{:S(2)}, u32[]{:S(2)}) collective-permute-start(bf16[64,256]{1,0:T(8,128)(2,1)S(1)} %add_convert_fusion.refs_0_), channel_id=1, source_target_pairs={{0,24},{8,16},{16,8},{24,0},{1,25},{9,17},{17,9},{25,1},{2,26},{10... | collective-permute-start | bytes 98312 | tf_op jit(solution)/shard_map/ppermute | solution.py:288
  18.4 0.0 collective-permute-start.5
  18.4 0.8 %collective-permute-start.4 = (bf16[64,256]{1,0:T(8,128)(2,1)S(1)}, bf16[64,256]{1,0:T(8,128)(2,1)S(1)}, u32[]{:S(2)}, u32[]{:S(2)}) collective-permute-start(bf16[64,256]{1,0:T(8,128)(2,1)S(1)} %add_convert_fusion.refs_0_), channel_id=1, source_target_pairs={{0,8},{8,0},{16,24},{24,16},{1,9},{9,1},{17,25},{25,17},{2,10},{10... | collective-permute-start | bytes 98312 | tf_op jit(solution)/shard_map/ppermute | solution.py:288
  19.2 0.0 copy-done.1
  19.2 0.0 copy-done.2
  19.2 0.0 copy-done.3
  19.2 0.0 copy-done.4
  19.2 0.0 copy-done.5
  19.2 1.4 %weights.1 = (bf16[4,128,2048]{2,1,0:T(8,128)(2,1)S(1)}, f32[4,16,2048]{2,1,0:T(8,128)S(1)}, f32[4,8,8,128]{3,2,1,0:T(8,128)S(1)}, s32[4,32,128]{2,1,0:T(8,128)S(1)}) custom-call(s32[4]{0:T(128)S(1)} %bitcast.11, s32[4]{0:T(128)S(1)} %bitcast.12, s32[4]{0:T(128)S(1)} %bitcast.13, f32[4]{0:T(128)S(1)} %bitcast.14, f32[4,2,2048]{2,1,0:T(2,128)S(1)} %bitcast.10), custom_call_target="tpu_custom_call" | custom-call | flops 8388608 | tf_op jit(solution)/shard_map/weights/pallas_call | solution.py:267
  20.7 0.0 collective-permute-done.6.refs_3_
  20.7 2.6 %collective-permute-done.5.refs_2_ = bf16[64,256]{1,0:T(8,128)(2,1)S(1)} collective-permute-done((bf16[64,256]{1,0:T(8,128)(2,1)S(1)}, bf16[64,256]{1,0:T(8,128)(2,1)S(1)}, u32[]{:S(2)}, u32[]{:S(2)}) %collective-permute-start.5) | collective-permute-done | bytes 32800 | tf_op jit(solution)/shard_map/ppermute | solution.py:288
  23.2 0.0 collective-permute-done.4.refs_1_
  23.2 1.1 %degrid.1 = f32[4,2,2048]{2,1,0:T(2,128)} custom-call(f32[4,8,8,128]{3,2,1,0:T(8,128)S(1)} %get-tuple-element.18.mix_ref, s32[4,32,128]{2,1,0:T(8,128)S(1)} %get-tuple-element.19.lane_ref, bf16[4,128,2048]{2,1,0:T(8,128)(2,1)S(1)} %get-tuple-element.20.col_ref, f32[4,16,2048]{2,1,0:T(8,128)S(1)} %get-tuple-element.21.row_ref, ...), custom_call_target="tpu_custom_call" | custom-call | tf_op jit(solution)/shard_map/degrid/pallas_call | solution.py:291
  24.4 0.0 copy-done
  (1 shorter events, 0.0 us)
Async XLA Ops:
  0.6 18.6 %copy-start.1 = (f32[1,1,4,2,2048]{4,3,2,1,0:T(2,128)S(1)}, f32[1,1,4,2,2048]{4,3,2,1,0:T(2,128)}, u32[]{:S(2)}) copy-start(f32[1,1,4,2,2048]{4,3,2,1,0:T(2,128)} %param.16) | copy-start | bytes 196612
  0.6 18.6 %copy-start.2 = (s32[1,1,4]{2,1,0:T(1,128)S(1)}, s32[1,1,4]{2,1,0:T(1,128)}, u32[]{:S(2)}) copy-start(s32[1,1,4]{2,1,0:T(1,128)} %param.12) | copy-start | bytes 52
  0.7 18.6 %copy-start.3 = (s32[1,1,4]{2,1,0:T(1,128)S(1)}, s32[1,1,4]{2,1,0:T(1,128)}, u32[]{:S(2)}) copy-start(s32[1,1,4]{2,1,0:T(1,128)} %param.13) | copy-start | bytes 52
  0.7 18.6 %copy-start.4 = (s32[1,1,4]{2,1,0:T(1,128)S(1)}, s32[1,1,4]{2,1,0:T(1,128)}, u32[]{:S(2)}) copy-start(s32[1,1,4]{2,1,0:T(1,128)} %param.14) | copy-start | bytes 52
  0.7 18.6 %copy-start.5 = (f32[1,1,4]{2,1,0:T(1,128)S(1)}, f32[1,1,4]{2,1,0:T(1,128)}, u32[]{:S(2)}) copy-start(f32[1,1,4]{2,1,0:T(1,128)} %param.15) | copy-start | bytes 52
  3.7 1.5 %collective-permute-start = (bf16[256,256]{1,0:T(8,128)(2,1)S(1)}, bf16[256,256]{1,0:T(8,128)(2,1)S(1)}, u32[]{:S(2)}, u32[]{:S(2)}) collective-permute-start(bf16[256,256]{1,0:T(8,128)(2,1)S(1)} %get-tuple-element.13.own_ref), channel_id=1, source_target_pairs={{0,1},{1,0},{2,3},{3,2},{4,5},{5,4},{6,7},{7,6},{8,9},{9,8},{10,11... | collective-permute-start | bytes 393224 | tf_op jit(solution)/shard_map/ppermute | solution.py:244
  5.5 4.8 %collective-permute-start.1 = (bf16[64,256]{1,0:T(8,128)(2,1)S(1)}, bf16[64,256]{1,0:T(8,128)(2,1)S(1)}, u32[]{:S(2)}, u32[]{:S(2)}) collective-permute-start(bf16[64,256]{1,0:T(8,128)(2,1)S(1)} %get-tuple-element.15), channel_id=1, source_target_pairs={{0,2},{1,3},{2,0},{3,1},{4,6},{5,7},{6,4},{7,5},{8,10},{9,11},{10,... | collective-permute-start | bytes 98312 | tf_op jit(solution)/shard_map/ppermute | solution.py:255
  8.4 3.9 %collective-permute-start.2 = (bf16[64,256]{1,0:T(8,128)(2,1)S(1)}, bf16[64,256]{1,0:T(8,128)(2,1)S(1)}, u32[]{:S(2)}, u32[]{:S(2)}) collective-permute-start(bf16[64,256]{1,0:T(8,128)(2,1)S(1)} %get-tuple-element.16), channel_id=1, source_target_pairs={{0,4},{1,5},{2,6},{3,7},{4,0},{5,1},{6,2},{7,3},{8,12},{9,13},{10,... | collective-permute-start | bytes 98312 | tf_op jit(solution)/shard_map/ppermute | solution.py:255
  9.9 4.8 %collective-permute-start.3 = (bf16[64,256]{1,0:T(8,128)(2,1)S(1)}, bf16[64,256]{1,0:T(8,128)(2,1)S(1)}, u32[]{:S(2)}, u32[]{:S(2)}) collective-permute-start(bf16[64,256]{1,0:T(8,128)(2,1)S(1)} %get-tuple-element.17), channel_id=1, source_target_pairs={{0,6},{1,7},{2,4},{3,5},{4,2},{5,3},{6,0},{7,1},{8,14},{9,15},{10,... | collective-permute-start | bytes 98312 | tf_op jit(solution)/shard_map/ppermute | solution.py:255
  14.7 9.6 %copy-start = (bf16[64,256]{1,0:T(8,128)(2,1)}, bf16[64,256]{1,0:T(8,128)(2,1)S(1)}, u32[]{:S(2)}) copy-start(bf16[64,256]{1,0:T(8,128)(2,1)S(1)} %add_convert_fusion.refs_0_) | copy-start | bytes 98308
  14.8 5.9 %collective-permute-start.6 = (bf16[64,256]{1,0:T(8,128)(2,1)S(1)}, bf16[64,256]{1,0:T(8,128)(2,1)S(1)}, u32[]{:S(2)}, u32[]{:S(2)}) collective-permute-start(bf16[64,256]{1,0:T(8,128)(2,1)S(1)} %add_convert_fusion.refs_0_), channel_id=1, source_target_pairs={{0,24},{8,16},{16,8},{24,0},{1,25},{9,17},{17,9},{25,1},{2,26},{10... | collective-permute-start | bytes 98312 | tf_op jit(solution)/shard_map/ppermute | solution.py:288
  18.4 4.8 %collective-permute-start.5 = (bf16[64,256]{1,0:T(8,128)(2,1)S(1)}, bf16[64,256]{1,0:T(8,128)(2,1)S(1)}, u32[]{:S(2)}, u32[]{:S(2)}) collective-permute-start(bf16[64,256]{1,0:T(8,128)(2,1)S(1)} %add_convert_fusion.refs_0_), channel_id=1, source_target_pairs={{0,16},{8,24},{16,0},{24,8},{1,17},{9,25},{17,1},{25,9},{2,18},{10... | collective-permute-start | bytes 98312 | tf_op jit(solution)/shard_map/ppermute | solution.py:288
  18.4 4.8 %collective-permute-start.4 = (bf16[64,256]{1,0:T(8,128)(2,1)S(1)}, bf16[64,256]{1,0:T(8,128)(2,1)S(1)}, u32[]{:S(2)}, u32[]{:S(2)}) collective-permute-start(bf16[64,256]{1,0:T(8,128)(2,1)S(1)} %add_convert_fusion.refs_0_), channel_id=1, source_target_pairs={{0,8},{8,0},{16,24},{24,16},{1,9},{9,1},{17,25},{25,17},{2,10},{10... | collective-permute-start | bytes 98312 | tf_op jit(solution)/shard_map/ppermute | solution.py:288

commit v3 on v2

--- a/solution.py
+++ b/solution.py
@@ -71,42 +71,54 @@
     chips = facet_count // 2
     facet = lax.axis_index("facet")
     chip = facet // 2
-    core = facet % 2
-    slots = facet_count * CAP
-    for s in range(slots):
+    for s in range(facet_count * CAP):
         subgrid_of[s] = -1
     slot_copy.wait()
     for s in range(slot_ref.shape[0]):
         subgrid_of[slot_ref[s]] = s
+
     step = 2.0 * math.pi / total
     lane = lax.broadcasted_iota(jnp.int32, (CR, strip_rows), 1)
     row = lax.broadcasted_iota(jnp.int32, (CR, strip_rows), 0)
+    cells, row_trig = [], []
     for side in range(2):
-        side_facet = facet if side == 0 else facet ^ 1
-        cell = side_facet * strip_rows + lane
+        cell = (facet if side == 0 else facet ^ 1) * strip_rows + lane
         angle = step * lax.rem(row * cell, total).astype(jnp.float32)
-        row_cos, row_sin = jnp.cos(angle), jnp.sin(angle)
-        first = 2 * side * strip_rows
-        left = pl.ds(first, strip_rows)
-        right = pl.ds(first + strip_rows, strip_rows)
-        for k in range(chips):
-            owner = 2 * send_to(k, chip, chips) + core
-            for c in range(CAP):
-                sub = subgrid_of[owner * CAP + c]
-                live = jnp.where(sub >= 0, 1.0, 0.0).astype(jnp.float32)
-                base = jnp.maximum(sub, 0) * CR
-                turn = step * lax.rem(base * cell[:8], total).astype(jnp.float32)
-                base_cos = jnp.cos(turn) * live
-                base_sin = jnp.sin(turn) * live
-                base_cos = jnp.concatenate([base_cos, base_cos], axis=0)
-                base_sin = jnp.concatenate([base_sin, base_sin], axis=0)
-                cos = (base_cos * row_cos - base_sin * row_sin).astype(jnp.bfloat16)
-                sin = (base_sin * row_cos + base_cos * row_sin).astype(jnp.bfloat16)
-                at = (k * CAP + c) * 2 * CR
-                phase_ref[pl.ds(at, CR), left] = cos
-                phase_ref[pl.ds(at, CR), right] = sin
-                phase_ref[pl.ds(at + CR, CR), left] = -sin
-                phase_ref[pl.ds(at + CR, CR), right] = cos
+        cells.append(cell)
+        row_trig.append((jnp.cos(angle), jnp.sin(angle)))
+
+    def write_phases(ref, first_row, owner_chip, side):
+        row_cos, row_sin = row_trig[side]
+        left = pl.ds(2 * side * strip_rows, strip_rows)
+        right = pl.ds((2 * side + 1) * strip_rows, strip_rows)
+        for c in range(2 * CAP):
+            sub = subgrid_of[owner_chip * 2 * CAP + c]
+            live = jnp.where(sub >= 0, 1.0, 0.0).astype(jnp.float32)
+            base = jnp.maximum(sub, 0) * CR
+            turn = step * lax.rem(base * cells[side][:8], total).astype(jnp.float32)
+            base_cos = jnp.cos(turn) * live
+            base_sin = jnp.sin(turn) * live
+            base_cos = jnp.concatenate([base_cos, base_cos], axis=0)
+            base_sin = jnp.concatenate([base_sin, base_sin], axis=0)
+            cos = (base_cos * row_cos - base_sin * row_sin).astype(jnp.bfloat16)
+            sin = (base_sin * row_cos + base_cos * row_sin).astype(jnp.bfloat16)
+            at = first_row + c * 2 * CR
+            ref[pl.ds(at, CR), left] = cos
+            ref[pl.ds(at, CR), right] = sin
+            ref[pl.ds(at + CR, CR), left] = -sin
+            ref[pl.ds(at + CR, CR), right] = cos
+
+    height = 2 * CAP * 2 * CR
+    @pl.when(facet % 2 == 0)
+    def _():
+        for side in range(2):
+            write_phases(phase_ref, 0, chip, side)
+
+    @pl.when(facet % 2 == 1)
+    def _():
+        for side in range(2):
+            for k in range(1, chips):
+                write_phases(phase_ref, (k - 1) * height, send_to(k, chip, chips), side)
 
     window_copy.wait()
     even = odd = None
@@ -138,21 +150,30 @@
 
 def term_kernel(scale, phase_ref, own_ref, other_ref, *out_refs):
     depth = own_ref.shape[0]
-    terms = jnp.dot(phase_ref[:, :depth], own_ref[...], preferred_element_type=jnp.float32)
-    terms += jnp.dot(phase_ref[:, depth:], other_ref[...], preferred_element_type=jnp.float32)
-    terms = (terms * scale).astype(jnp.bfloat16)
-    height = CAP * 2 * CR
-    for k, out_ref in enumerate(out_refs):
-        out_ref[...] = terms[k * height : (k + 1) * height]
+    height = out_refs[0].shape[0]
+
+    def write_terms(k):
+        at = pl.ds(k * height, height)
+        terms = jnp.dot(phase_ref[at, :depth], own_ref[...], preferred_element_type=jnp.float32)
+        terms += jnp.dot(phase_ref[at, depth:], other_ref[...], preferred_element_type=jnp.float32)
+        out_refs[k][...] = (terms * scale).astype(jnp.bfloat16)
+
+    write_terms(0)
+
+    @pl.when(lax.axis_index("facet") % 2 == 1)
+    def _():
+        for k in range(1, len(out_refs)):
+            write_terms(k)
 
 
 def weights_kernel(
-    bands, slot_ref, band_ref, offset_ref, weight_ref, pos_ref, col_ref, row_ref, mix_ref, lane_ref
+    bands, slot_ref, band_ref, offset_ref, weight_ref, pos_ref, after_ref, col_ref, row_ref, mix_ref, lane_ref, core_ref
 ):
     blocks, width, points = col_ref.shape
     factor = -1.0 / (2.0 * kernel_sigma * kernel_sigma)
     tile = 512
     me = lax.axis_index("band")
+    core_ref[...] = jnp.full(core_ref.shape, lax.axis_index("facet") % 2, jnp.int32)
     column = lax.broadcasted_iota(jnp.int32, (width, tile), 0).astype(jnp.float32)
     row = lax.broadcasted_iota(jnp.int32, (CR, tile), 0).astype(jnp.float32)
     for v in range(blocks):
@@ -173,13 +194,18 @@
             col_ref[v, :, at] = jnp.exp(diff * diff * factor).astype(jnp.bfloat16)
 
 
-def degrid_kernel(bands, mix_ref, lane_ref, col_ref, row_ref, *refs):
-    sub_refs, out_ref = refs[:bands], refs[bands]
+def degrid_kernel(bands, mix_ref, lane_ref, col_ref, row_ref, sub_ref, swap_ref, *refs):
+    band_refs, own_ref, out_ref = refs[: bands - 1], refs[bands - 1], refs[bands]
     height = 2 * CR
+    share_rows = CAP * height
+    core = lax.axis_index("facet") % 2
+    parts = [jnp.where(core == 0, sub_ref[:share_rows], swap_ref[:share_rows])]
+    own_ref[...] = parts[0]
+    for k in range(1, bands):
+        at = pl.ds((k - 1) * share_rows, share_rows)
+        parts.append(jnp.where(core == 0, swap_ref[at], band_refs[k - 1][share_rows:]))
     held = [
-        sub_refs[k][c * height : (c + 1) * height, :].astype(jnp.float32)
-        for k in range(bands)
-        for c in range(CAP)
+        part[c * height : (c + 1) * height].astype(jnp.float32) for part in parts for c in range(CAP)
     ]
     for v in range(col_ref.shape[0]):
         halves = []
@@ -211,19 +237,25 @@
     length = facets.shape[4]
     sky_rows = facet_count * strip_rows
     blocks, points = vis_pos.shape[2], vis_pos.shape[4]
-    height = CAP * 2 * CR
+    share_rows = CAP * 2 * CR
+    height = 2 * share_rows
     chunks = 4
+    core = lax.axis_index("facet") % 2
+
+    def swap(x):
+        return lax.ppermute(x, "facet", [(i, i ^ 1) for i in range(facet_count)])
 
     strip = facets.reshape(2 * strip_rows, length)
     table = jnp.asarray(column_map(length, SG))
+    term_shape = jax.ShapeDtypeStruct((height, SG), jnp.bfloat16)
     spectrum, phases = pl.pallas_call(
         functools.partial(front_kernel, sky_rows, chunks),
         out_shape=(
             jax.ShapeDtypeStruct((2 * strip_rows, SG), jnp.bfloat16),
-            jax.ShapeDtypeStruct((chips * height, 4 * strip_rows), jnp.bfloat16),
+            jax.ShapeDtypeStruct(((chips - 1) * height, 4 * strip_rows), jnp.bfloat16),
         ),
         in_specs=[HBM] * 4,
-        out_specs=(VMEM, VMEM),
+        out_specs=(VMEM,) * 2,
         scratch_shapes=[
             pltpu.VMEM((2 * strip_rows, length), jnp.bfloat16),
             pltpu.VMEM((length // 2, 2 * SG), jnp.bfloat16),
@@ -241,39 +273,42 @@
         for x in (slot_of_subgrid, strip, col_window.reshape(1, length), table)
     ))
 
-    other = lax.ppermute(spectrum, "facet", [(i, i ^ 1) for i in range(facet_count)])
-    term_shape = jax.ShapeDtypeStruct((height, SG), jnp.bfloat16)
+    other = swap(spectrum)
     terms = pl.pallas_call(
         functools.partial(term_kernel, 1.0 / math.sqrt(sky_rows)),
-        out_shape=(term_shape,) * chips,
+        out_shape=(term_shape,) * (chips - 1),
         in_specs=[VMEM] * 3,
-        out_specs=(VMEM,) * chips,
+        out_specs=(VMEM,) * (chips - 1),
         compiler_params=pltpu.CompilerParams(vmem_limit_bytes=16 * 2**20),
         name="terms",
     )(phases, spectrum, other)
-    arrived = [terms[0]] + [
+    arrived = [
         lax.ppermute(
-            terms[k],
+            terms[k - 1],
             "facet",
-            [(i, 2 * send_to(k, i // 2, chips) + i % 2) for i in range(facet_count)],
+            [
+                (i, 2 * send_to(k, i // 2, chips) if i % 2 else i + 1)
+                for i in range(facet_count)
+            ],
         )
         for k in range(1, chips)
     ]
-    total = arrived[0].astype(jnp.float32)
-    for part in arrived[1:]:
+    total = terms[0].astype(jnp.float32)
+    for part in arrived:
         total = total + part.astype(jnp.float32)
-    owned = total.astype(jnp.bfloat16)
-
-    col_kernel, row_kernel, mix, lanes = pl.pallas_call(
+    chip_subs = total.astype(jnp.bfloat16)
+
+    col_kernel, row_kernel, mix, lanes, core_map = pl.pallas_call(
         functools.partial(weights_kernel, band_count),
         out_shape=(
             jax.ShapeDtypeStruct((blocks, PC, points), jnp.bfloat16),
             jax.ShapeDtypeStruct((blocks, CR, points), jnp.float32),
             jax.ShapeDtypeStruct((blocks, band_count * CAP, 8, 128), jnp.float32),
             jax.ShapeDtypeStruct((blocks, 2 * CR, PC), jnp.int32),
+            jax.ShapeDtypeStruct((8, SG), jnp.int32),
         ),
-        in_specs=[SMEM] * 4 + [VMEM],
-        out_specs=(VMEM,) * 4,
+        in_specs=[SMEM] * 4 + [VMEM] * 2,
+        out_specs=(VMEM,) * 5,
         compiler_params=pltpu.CompilerParams(vmem_limit_bytes=16 * 2**20),
         cost_estimate=pl.CostEstimate(
             flops=8 * blocks * PC * points, bytes_accessed=0, transcendentals=blocks * PC * points
@@ -282,20 +317,39 @@
     )(
         block_slot.reshape(blocks), block_band.reshape(blocks), block_offset.reshape(blocks),
         block_weight.reshape(blocks), vis_pos.reshape(blocks, 2, points),
+        chip_subs,
     )
 
-    subs = [owned] + [
-        lax.ppermute(owned, "band", [(i, send_to(k, i, band_count)) for i in range(band_count)])
+    device = lambda band, facet: band * facet_count + facet
+    band_subs = [
+        lax.ppermute(
+            chip_subs,
+            ("band", "facet"),
+            [
+                (device(b, f), device(b, f - 1) if f % 2 else device(send_to(k, b, band_count), f + 1))
+                for b in range(band_count)
+                for f in range(facet_count)
+            ],
+        )
         for k in range(1, band_count)
     ]
-    visible = pl.pallas_call(
+    for_other = jnp.where(
+        core_map[:1] == 0,
+        jnp.concatenate([chip_subs[share_rows:]] * (band_count - 1)),
+        jnp.concatenate([part[:share_rows] for part in band_subs]),
+    )
+    from_other = swap(for_other)
+    owned, visible = pl.pallas_call(
         functools.partial(degrid_kernel, band_count),
-        out_shape=jax.ShapeDtypeStruct((blocks, 2, points), jnp.float32),
-        in_specs=[VMEM] * (4 + band_count),
-        out_specs=VMEM,
+        out_shape=(
+            jax.ShapeDtypeStruct((share_rows, SG), jnp.bfloat16),
+            jax.ShapeDtypeStruct((blocks, 2, points), jnp.float32),
+        ),
+        in_specs=[VMEM] * (5 + band_count),
+        out_specs=(VMEM,) * 2,
         compiler_params=pltpu.CompilerParams(vmem_limit_bytes=24 * 2**20),
         name="degrid",
-    )(mix, lanes, col_kernel, row_kernel, *subs)
+    )(mix, lanes, col_kernel, row_kernel, chip_subs, from_other, *band_subs)
     return (
         owned.reshape(1, CAP, 2, CR, SG),
         visible.reshape(1, 1, blocks, 2, points),

time: 24.5 us -> 21.9 us (0.89)
  waiting for transfers between devices: 8.34 us -> 6.05 us
  starting transfers between devices: 9.43 us -> 9 us
    ppermute x7 -> x8, waiting for transfers between devices: 8.34 us -> 6.05 us  [the longest x3 2.79 us: local(): lax.ppermute(terms[k - 1], 'facet', [(i, 2 * send_to(k, i // 2, chips) if...]
    ppermute x7 -> x8, starting transfers between devices: 9.43 us -> 9 us  [the longest x3 4.34 us: local(): lax.ppermute(terms[k - 1], 'facet', [(i, 2 * send_to(k, i // 2, chips) if...]
  transfers between devices with their start and end apart: 7 -> 8, of which waited for: 5 -> 8; matrix products, arithmetic and copies ran while one was open for 0% -> 0% of each run, Pallas kernels for 6% -> 7%
where the time goes in v3:
time: 21.9 us; the launch traced here: 21.7 us
  starting transfers between devices  9 us (41%)
  waiting for transfers between devices  6.05 us (28%)
  Pallas kernels  5.81 us (27%)
  between operations  0.75 us (3%)
    ppermute x3, starting transfers between devices, local(): lax.ppermute(terms[k - 1], 'facet', [(i, 2 * send_to(k, i // 2, chips) if...  4.34 us
    pallas_call x1, Pallas kernels, local(): pl.pallas_call(functools.partial(front_kernel, sky_rows, chunks), out_sha...  3.04 us
    ppermute x3, waiting for transfers between devices, local(): lax.ppermute(terms[k - 1], 'facet', [(i, 2 * send_to(k, i // 2, chips) if...  2.79 us
    ppermute x3, starting transfers between devices, local(): lax.ppermute(chip_subs, ('band', 'facet'), [(device(b, f), device(b, f -...  2.76 us
    ppermute x2, waiting for transfers between devices, swap(): return lax.ppermute(x, 'facet', [(i, i ^ 1) for i in range(facet_count)])  1.93 us
    ppermute x2, starting transfers between devices, swap(): return lax.ppermute(x, 'facet', [(i, i ^ 1) for i in range(facet_count)])  1.9 us
    pallas_call x1, Pallas kernels, local(): pl.pallas_call(functools.partial(weights_kernel, band_count), out_shape=(...  1.43 us
    ppermute x3, waiting for transfers between devices, local(): lax.ppermute(chip_subs, ('band', 'facet'), [(device(b, f), device(b, f -...  1.34 us
  transfers between devices with their start and end apart: 8, of which 8 were waited for; matrix products, arithmetic and copies ran while one was open for 0% of the time, Pallas kernels for 7%

profile of v3, /device:TPU:0, one launch (start us, length us, event | category | flops | bytes accessed | tf_op | source)
XLA Modules:
  0.0 21.7 jit_solution(10990089407338239521)
XLA Ops:
  0.6 0.0 copy-start
  0.6 0.0 copy-start.1
  0.7 0.0 copy-start.2
  0.7 0.0 copy-start.3
  0.7 0.0 copy-start.4
  0.7 3.0 %front.1 = (bf16[256,256]{1,0:T(8,128)(2,1)S(1)}, bf16[384,512]{1,0:T(8,128)(2,1)S(1)}) custom-call(s32[12]{0:T(128)} %slot_hbm.1, bf16[256,4096]{1,0:T(8,128)(2,1)} %bitcast.14, f32[1,4096]{1,0:T(1,128)} %bitcast.15, bf16[2048,512]{1,0:T(8,128)(2,1)} %constant.4.clone.table_ref), custom_call_target="tpu_custom_call" | custom-call | tf_op jit(solution)/shard_map/front/pallas_call | solution.py:251
  3.7 0.5 %collective-permute-start = (bf16[256,256]{1,0:T(8,128)(2,1)S(1)}, bf16[256,256]{1,0:T(8,128)(2,1)S(1)}, u32[]{:S(2)}, u32[]{:S(2)}) collective-permute-start(bf16[256,256]{1,0:T(8,128)(2,1)S(1)} %get-tuple-element.15.own_ref), channel_id=1, source_target_pairs={{0,1},{1,0},{2,3},{3,2},{4,5},{5,4},{6,7},{7,6},{8,9},{9,8},{10,11... | collective-permute-start | bytes 393224 | tf_op jit(solution)/shard_map/ppermute | solution.py:246
  4.2 1.0 %collective-permute-done.other_ref = bf16[256,256]{1,0:T(8,128)(2,1)S(1)} collective-permute-done((bf16[256,256]{1,0:T(8,128)(2,1)S(1)}, bf16[256,256]{1,0:T(8,128)(2,1)S(1)}, u32[]{:S(2)}, u32[]{:S(2)}) %collective-permute-start) | collective-permute-done | bytes 131104 | tf_op jit(solution)/shard_map/ppermute | solution.py:246
  5.2 0.2 terms.1
  5.4 0.6 %collective-permute-start.2 = (bf16[128,256]{1,0:T(8,128)(2,1)S(1)}, bf16[128,256]{1,0:T(8,128)(2,1)S(1)}, u32[]{:S(2)}, u32[]{:S(2)}) collective-permute-start(bf16[128,256]{1,0:T(8,128)(2,1)S(1)} %get-tuple-element.17), channel_id=1, source_target_pairs={{0,1},{1,4},{2,3},{3,6},{4,5},{5,0},{6,7},{7,2},{8,9},{9,12},{10,1... | collective-permute-start | bytes 196616 | tf_op jit(solution)/shard_map/ppermute | solution.py:286
  6.1 2.4 %collective-permute-start.3 = (bf16[128,256]{1,0:T(8,128)(2,1)S(1)}, bf16[128,256]{1,0:T(8,128)(2,1)S(1)}, u32[]{:S(2)}, u32[]{:S(2)}) collective-permute-start(bf16[128,256]{1,0:T(8,128)(2,1)S(1)} %get-tuple-element.18), channel_id=1, source_target_pairs={{0,1},{1,6},{2,3},{3,4},{4,5},{5,2},{6,7},{7,0},{8,9},{9,14},{10,1... | collective-permute-start | bytes 196616 | tf_op jit(solution)/shard_map/ppermute | solution.py:286
  8.5 1.3 %collective-permute-start.1 = (bf16[128,256]{1,0:T(8,128)(2,1)S(1)}, bf16[128,256]{1,0:T(8,128)(2,1)S(1)}, u32[]{:S(2)}, u32[]{:S(2)}) collective-permute-start(bf16[128,256]{1,0:T(8,128)(2,1)S(1)} %get-tuple-element.16), channel_id=1, source_target_pairs={{0,1},{1,2},{2,3},{3,0},{4,5},{5,6},{6,7},{7,4},{8,9},{9,10},{10,1... | collective-permute-start | bytes 196616 | tf_op jit(solution)/shard_map/ppermute | solution.py:286
  9.8 0.5 %collective-permute-done.2 = bf16[128,256]{1,0:T(8,128)(2,1)S(1)} collective-permute-done((bf16[128,256]{1,0:T(8,128)(2,1)S(1)}, bf16[128,256]{1,0:T(8,128)(2,1)S(1)}, u32[]{:S(2)}, u32[]{:S(2)}) %collective-permute-start.2) | collective-permute-done | bytes 65568 | tf_op jit(solution)/shard_map/ppermute | solution.py:286
  10.3 1.2 %collective-permute-done.3 = bf16[128,256]{1,0:T(8,128)(2,1)S(1)} collective-permute-done((bf16[128,256]{1,0:T(8,128)(2,1)S(1)}, bf16[128,256]{1,0:T(8,128)(2,1)S(1)}, u32[]{:S(2)}, u32[]{:S(2)}) %collective-permute-start.3) | collective-permute-done | bytes 65568 | tf_op jit(solution)/shard_map/ppermute | solution.py:286
  11.5 1.1 %collective-permute-done.1 = bf16[128,256]{1,0:T(8,128)(2,1)S(1)} collective-permute-done((bf16[128,256]{1,0:T(8,128)(2,1)S(1)}, bf16[128,256]{1,0:T(8,128)(2,1)S(1)}, u32[]{:S(2)}, u32[]{:S(2)}) %collective-permute-start.1) | collective-permute-done | bytes 65568 | tf_op jit(solution)/shard_map/ppermute | solution.py:286
  12.6 2.4 %collective-permute-start.6 = (bf16[128,256]{1,0:T(8,128)(2,1)S(1)}, bf16[128,256]{1,0:T(8,128)(2,1)S(1)}, u32[]{:S(2)}, u32[]{:S(2)}) collective-permute-start(bf16[128,256]{1,0:T(8,128)(2,1)S(1)} %add_convert_fusion.after_ref.sub_ref), channel_id=1, source_target_pairs={{0,25},{1,0},{2,27},{3,2},{4,29},{5,4},{6,31},{7,6},{8,17},{9,8},{... | collective-permute-start | bytes 196616 | tf_op jit(solution)/shard_map/ppermute | solution.py:325
  15.0 0.3 %collective-permute-start.5 = (bf16[128,256]{1,0:T(8,128)(2,1)S(1)}, bf16[128,256]{1,0:T(8,128)(2,1)S(1)}, u32[]{:S(2)}, u32[]{:S(2)}) collective-permute-start(bf16[128,256]{1,0:T(8,128)(2,1)S(1)} %add_convert_fusion.after_ref.sub_ref), channel_id=1, source_target_pairs={{0,17},{1,0},{2,19},{3,2},{4,21},{5,4},{6,23},{7,6},{8,25},{9,8},{... | collective-permute-start | bytes 196616 | tf_op jit(solution)/shard_map/ppermute | solution.py:325
  15.4 0.0 collective-permute-start.4
  15.4 0.0 copy-done
  15.4 0.0 copy-done.1
  15.4 0.0 copy-done.2
  15.4 0.0 copy-done.3
  15.4 0.0 copy-done.4
  15.4 1.4 %weights.1 = (bf16[4,128,2048]{2,1,0:T(8,128)(2,1)S(1)}, f32[4,16,2048]{2,1,0:T(8,128)S(1)}, f32[4,8,8,128]{3,2,1,0:T(8,128)S(1)}, s32[4,32,128]{2,1,0:T(8,128)S(1)}, s32[8,256]{1,0:T(8,128)S(1)}) custom-call(s32[4]{0:T(128)S(1)} %bitcast.10, s32[4]{0:T(128)S(1)} %bitcast.11, s32[4]{0:T(128)S(1)} %bitcast.12, f32[4]{0:T(128)S(1)} %bitcast.13, ...), custom_call_target="tpu_custom_call" | custom-call | flops 8388608 | tf_op jit(solution)/shard_map/weights/pallas_call | solution.py:301
  16.9 0.1 collective-permute-done.6.refs_2_
  16.9 0.6 %collective-permute-done.5.refs_1_ = bf16[128,256]{1,0:T(8,128)(2,1)S(1)} collective-permute-done((bf16[128,256]{1,0:T(8,128)(2,1)S(1)}, bf16[128,256]{1,0:T(8,128)(2,1)S(1)}, u32[]{:S(2)}, u32[]{:S(2)}) %collective-permute-start.5) | collective-permute-done | bytes 65568 | tf_op jit(solution)/shard_map/ppermute | solution.py:325
  17.6 0.7 %collective-permute-done.4.refs_0_ = bf16[128,256]{1,0:T(8,128)(2,1)S(1)} collective-permute-done((bf16[128,256]{1,0:T(8,128)(2,1)S(1)}, bf16[128,256]{1,0:T(8,128)(2,1)S(1)}, u32[]{:S(2)}, u32[]{:S(2)}) %collective-permute-start.4) | collective-permute-done | bytes 65568 | tf_op jit(solution)/shard_map/ppermute | solution.py:325
  18.2 1.4 %collective-permute-start.7 = (bf16[192,256]{1,0:T(8,128)(2,1)S(1)}, bf16[192,256]{1,0:T(8,128)(2,1)S(1)}, u32[]{:S(2)}, u32[]{:S(2)}) collective-permute-start(bf16[192,256]{1,0:T(8,128)(2,1)S(1)} %maximum_select_fusion), channel_id=1, source_target_pairs={{0,1},{1,0},{2,3},{3,2},{4,5},{5,4},{6,7},{7,6},{8,9},{9,8},{10,11... | collective-permute-start | bytes 294920 | tf_op jit(solution)/shard_map/ppermute | solution.py:246
  19.6 0.9 %collective-permute-done.7.swap_ref = bf16[192,256]{1,0:T(8,128)(2,1)S(1)} collective-permute-done((bf16[192,256]{1,0:T(8,128)(2,1)S(1)}, bf16[192,256]{1,0:T(8,128)(2,1)S(1)}, u32[]{:S(2)}, u32[]{:S(2)}) %collective-permute-start.7) | collective-permute-done | bytes 98336 | tf_op jit(solution)/shard_map/ppermute | solution.py:246
  20.6 1.2 %degrid.1 = (bf16[64,256]{1,0:T(8,128)(2,1)}, f32[4,2,2048]{2,1,0:T(2,128)}) custom-call(f32[4,8,8,128]{3,2,1,0:T(8,128)S(1)} %get-tuple-element.19.mix_ref, s32[4,32,128]{2,1,0:T(8,128)S(1)} %get-tuple-element.20.lane_ref, bf16[4,128,2048]{2,1,0:T(8,128)(2,1)S(1)} %get-tuple-element.21.col_ref, f32[4,16,2048]{2,1,0:T(8,128)S(1)} %get-tuple-element.22.row_ref, ...), custom_call_target="tpu_custom_call" | custom-call | tf_op jit(solution)/shard_map/degrid/pallas_call | solution.py:342
  (7 shorter events, 0.1 us)
Async XLA Ops:
  0.6 14.7 %copy-start = (f32[1,1,4,2,2048]{4,3,2,1,0:T(2,128)S(1)}, f32[1,1,4,2,2048]{4,3,2,1,0:T(2,128)}, u32[]{:S(2)}) copy-start(f32[1,1,4,2,2048]{4,3,2,1,0:T(2,128)} %param.16) | copy-start | bytes 196612
  0.6 14.7 %copy-start.1 = (s32[1,1,4]{2,1,0:T(1,128)S(1)}, s32[1,1,4]{2,1,0:T(1,128)}, u32[]{:S(2)}) copy-start(s32[1,1,4]{2,1,0:T(1,128)} %param.12) | copy-start | bytes 52
  0.7 14.7 %copy-start.2 = (s32[1,1,4]{2,1,0:T(1,128)S(1)}, s32[1,1,4]{2,1,0:T(1,128)}, u32[]{:S(2)}) copy-start(s32[1,1,4]{2,1,0:T(1,128)} %param.13) | copy-start | bytes 52
  0.7 14.7 %copy-start.3 = (s32[1,1,4]{2,1,0:T(1,128)S(1)}, s32[1,1,4]{2,1,0:T(1,128)}, u32[]{:S(2)}) copy-start(s32[1,1,4]{2,1,0:T(1,128)} %param.14) | copy-start | bytes 52
  0.7 14.7 %copy-start.4 = (f32[1,1,4]{2,1,0:T(1,128)S(1)}, f32[1,1,4]{2,1,0:T(1,128)}, u32[]{:S(2)}) copy-start(f32[1,1,4]{2,1,0:T(1,128)} %param.15) | copy-start | bytes 52
  3.7 1.5 %collective-permute-start = (bf16[256,256]{1,0:T(8,128)(2,1)S(1)}, bf16[256,256]{1,0:T(8,128)(2,1)S(1)}, u32[]{:S(2)}, u32[]{:S(2)}) collective-permute-start(bf16[256,256]{1,0:T(8,128)(2,1)S(1)} %get-tuple-element.15.own_ref), channel_id=1, source_target_pairs={{0,1},{1,0},{2,3},{3,2},{4,5},{5,4},{6,7},{7,6},{8,9},{9,8},{10,11... | collective-permute-start | bytes 393224 | tf_op jit(solution)/shard_map/ppermute | solution.py:246
  5.4 4.9 %collective-permute-start.2 = (bf16[128,256]{1,0:T(8,128)(2,1)S(1)}, bf16[128,256]{1,0:T(8,128)(2,1)S(1)}, u32[]{:S(2)}, u32[]{:S(2)}) collective-permute-start(bf16[128,256]{1,0:T(8,128)(2,1)S(1)} %get-tuple-element.17), channel_id=1, source_target_pairs={{0,1},{1,4},{2,3},{3,6},{4,5},{5,0},{6,7},{7,2},{8,9},{9,12},{10,1... | collective-permute-start | bytes 196616 | tf_op jit(solution)/shard_map/ppermute | solution.py:286
  6.1 5.4 %collective-permute-start.3 = (bf16[128,256]{1,0:T(8,128)(2,1)S(1)}, bf16[128,256]{1,0:T(8,128)(2,1)S(1)}, u32[]{:S(2)}, u32[]{:S(2)}) collective-permute-start(bf16[128,256]{1,0:T(8,128)(2,1)S(1)} %get-tuple-element.18), channel_id=1, source_target_pairs={{0,1},{1,6},{2,3},{3,4},{4,5},{5,2},{6,7},{7,0},{8,9},{9,14},{10,1... | collective-permute-start | bytes 196616 | tf_op jit(solution)/shard_map/ppermute | solution.py:286
  8.5 4.1 %collective-permute-start.1 = (bf16[128,256]{1,0:T(8,128)(2,1)S(1)}, bf16[128,256]{1,0:T(8,128)(2,1)S(1)}, u32[]{:S(2)}, u32[]{:S(2)}) collective-permute-start(bf16[128,256]{1,0:T(8,128)(2,1)S(1)} %get-tuple-element.16), channel_id=1, source_target_pairs={{0,1},{1,2},{2,3},{3,0},{4,5},{5,6},{6,7},{7,4},{8,9},{9,10},{10,1... | collective-permute-start | bytes 196616 | tf_op jit(solution)/shard_map/ppermute | solution.py:286
  12.6 4.3 %collective-permute-start.6 = (bf16[128,256]{1,0:T(8,128)(2,1)S(1)}, bf16[128,256]{1,0:T(8,128)(2,1)S(1)}, u32[]{:S(2)}, u32[]{:S(2)}) collective-permute-start(bf16[128,256]{1,0:T(8,128)(2,1)S(1)} %add_convert_fusion.after_ref.sub_ref), channel_id=1, source_target_pairs={{0,25},{1,0},{2,27},{3,2},{4,29},{5,4},{6,31},{7,6},{8,17},{9,8},{... | collective-permute-start | bytes 196616 | tf_op jit(solution)/shard_map/ppermute | solution.py:325
  15.0 2.5 %collective-permute-start.5 = (bf16[128,256]{1,0:T(8,128)(2,1)S(1)}, bf16[128,256]{1,0:T(8,128)(2,1)S(1)}, u32[]{:S(2)}, u32[]{:S(2)}) collective-permute-start(bf16[128,256]{1,0:T(8,128)(2,1)S(1)} %add_convert_fusion.after_ref.sub_ref), channel_id=1, source_target_pairs={{0,17},{1,0},{2,19},{3,2},{4,21},{5,4},{6,23},{7,6},{8,25},{9,8},{... | collective-permute-start | bytes 196616 | tf_op jit(solution)/shard_map/ppermute | solution.py:325
  15.4 2.9 %collective-permute-start.4 = (bf16[128,256]{1,0:T(8,128)(2,1)S(1)}, bf16[128,256]{1,0:T(8,128)(2,1)S(1)}, u32[]{:S(2)}, u32[]{:S(2)}) collective-permute-start(bf16[128,256]{1,0:T(8,128)(2,1)S(1)} %add_convert_fusion.after_ref.sub_ref), channel_id=1, source_target_pairs={{0,9},{1,0},{2,11},{3,2},{4,13},{5,4},{6,15},{7,6},{8,1},{9,8},{10... | collective-permute-start | bytes 196616 | tf_op jit(solution)/shard_map/ppermute | solution.py:325
  18.2 2.3 %collective-permute-start.7 = (bf16[192,256]{1,0:T(8,128)(2,1)S(1)}, bf16[192,256]{1,0:T(8,128)(2,1)S(1)}, u32[]{:S(2)}, u32[]{:S(2)}) collective-permute-start(bf16[192,256]{1,0:T(8,128)(2,1)S(1)} %maximum_select_fusion), channel_id=1, source_target_pairs={{0,1},{1,0},{2,3},{3,2},{4,5},{5,4},{6,7},{7,6},{8,9},{9,8},{10,11... | collective-permute-start | bytes 294920 | tf_op jit(solution)/shard_map/ppermute | solution.py:246

commit v4 on v3

--- a/solution.py
+++ b/solution.py
@@ -29,30 +29,29 @@
     return i ^ k if n & (n - 1) == 0 else (i - k + n) % n
 
 
-def column_map(length, width):
-    j = np.arange(length // 2)[:, None]
+def column_seed(length, width):
+    ratio = length // width
+    place = (ratio * np.arange(width // 2)[None, :] - np.arange(ratio)[:, None])[:, :, None]
     out = []
     for parity in (0, 1):
-        freq = np.arange(parity, width, 2)[None, :]
-        forward = np.exp(-2j * np.pi / length * (j * freq % length)) / math.sqrt(length)
-        k = np.arange(width // 2)[None, :]
-        inverse = np.exp(2j * np.pi / width * (freq.T * k % width)) / math.sqrt(width)
-        both = forward @ inverse
+        freq = np.arange(parity, width, 2)
+        both = np.exp(2j * np.pi / length * (place * freq % length)).sum(-1)
+        both = both / math.sqrt(length) / math.sqrt(width)
         out += [both.real, both.imag]
-    return np.concatenate(out, axis=1).astype(jnp.bfloat16)
+    return np.concatenate(out, axis=0).astype(jnp.bfloat16)
 
 
 def front_kernel(
-    total, chunks, slot_hbm, facets_ref, window_hbm, table_ref, spec_ref, phase_ref,
-    strip, table, window_ref, slot_ref, strip_sems, table_sems, small_sems, subgrid_of
+    chunks, facets_ref, window_hbm, seed_hbm, spec_ref,
+    strip, table, window_ref, seed_ref, strip_sems, small_sems
 ):
     rows, length = strip.shape
     half = length // 2
     width = half // chunks
     strip_rows = rows // 2
-    slot_copy = pltpu.make_async_copy(slot_hbm, slot_ref, small_sems.at[0])
+    seed_copy = pltpu.make_async_copy(seed_hbm, seed_ref, small_sems.at[0])
     window_copy = pltpu.make_async_copy(window_hbm, window_ref, small_sems.at[1])
-    slot_copy.start()
+    seed_copy.start()
     window_copy.start()
     copies = []
     for i in range(chunks):
@@ -61,64 +60,22 @@
         copies.append((
             pltpu.make_async_copy(facets_ref.at[:, cols], strip.at[:, cols], strip_sems.at[2 * i]),
             pltpu.make_async_copy(facets_ref.at[:, upper], strip.at[:, upper], strip_sems.at[2 * i + 1]),
-            pltpu.make_async_copy(table_ref.at[cols], table.at[cols], table_sems.at[i]),
         ))
     for group in copies:
         for copy in group:
             copy.start()
 
-    facet_count = lax.axis_size("facet")
-    chips = facet_count // 2
-    facet = lax.axis_index("facet")
-    chip = facet // 2
-    for s in range(facet_count * CAP):
-        subgrid_of[s] = -1
-    slot_copy.wait()
-    for s in range(slot_ref.shape[0]):
-        subgrid_of[slot_ref[s]] = s
-
-    step = 2.0 * math.pi / total
-    lane = lax.broadcasted_iota(jnp.int32, (CR, strip_rows), 1)
-    row = lax.broadcasted_iota(jnp.int32, (CR, strip_rows), 0)
-    cells, row_trig = [], []
-    for side in range(2):
-        cell = (facet if side == 0 else facet ^ 1) * strip_rows + lane
-        angle = step * lax.rem(row * cell, total).astype(jnp.float32)
-        cells.append(cell)
-        row_trig.append((jnp.cos(angle), jnp.sin(angle)))
-
-    def write_phases(ref, first_row, owner_chip, side):
-        row_cos, row_sin = row_trig[side]
-        left = pl.ds(2 * side * strip_rows, strip_rows)
-        right = pl.ds((2 * side + 1) * strip_rows, strip_rows)
-        for c in range(2 * CAP):
-            sub = subgrid_of[owner_chip * 2 * CAP + c]
-            live = jnp.where(sub >= 0, 1.0, 0.0).astype(jnp.float32)
-            base = jnp.maximum(sub, 0) * CR
-            turn = step * lax.rem(base * cells[side][:8], total).astype(jnp.float32)
-            base_cos = jnp.cos(turn) * live
-            base_sin = jnp.sin(turn) * live
-            base_cos = jnp.concatenate([base_cos, base_cos], axis=0)
-            base_sin = jnp.concatenate([base_sin, base_sin], axis=0)
-            cos = (base_cos * row_cos - base_sin * row_sin).astype(jnp.bfloat16)
-            sin = (base_sin * row_cos + base_cos * row_sin).astype(jnp.bfloat16)
-            at = first_row + c * 2 * CR
-            ref[pl.ds(at, CR), left] = cos
-            ref[pl.ds(at, CR), right] = sin
-            ref[pl.ds(at + CR, CR), left] = -sin
-            ref[pl.ds(at + CR, CR), right] = cos
-
-    height = 2 * CAP * 2 * CR
-    @pl.when(facet % 2 == 0)
-    def _():
-        for side in range(2):
-            write_phases(phase_ref, 0, chip, side)
-
-    @pl.when(facet % 2 == 1)
-    def _():
-        for side in range(2):
-            for k in range(1, chips):
-                write_phases(phase_ref, (k - 1) * height, send_to(k, chip, chips), side)
+    seed_copy.wait()
+    ratio = length // SG
+    lane = lax.broadcasted_iota(jnp.int32, (ratio, HALF), 1)
+    for a in range(HALF):
+        turned = pltpu.roll(seed_ref[...], a, 1) if a else seed_ref[...]
+        at = pl.ds(a * ratio, ratio)
+        for kind in range(4):
+            part = turned[kind * ratio : (kind + 1) * ratio]
+            if kind >= 2 and a:
+                part = jnp.where(lane < a, -part, part)
+            table[at, kind * HALF : (kind + 1) * HALF] = part.astype(jnp.bfloat16)
 
     window_copy.wait()
     even = odd = None
@@ -148,22 +105,83 @@
     spec_ref[n:, HALF:] = (even_imag - odd_imag).astype(jnp.bfloat16)
 
 
-def term_kernel(scale, phase_ref, own_ref, other_ref, *out_refs):
-    depth = own_ref.shape[0]
+def phase_kernel(total, slot_ref, spec_ref, phase_ref, partial_ref):
+    strip_rows = spec_ref.shape[0] // 2
+    slots = phase_ref.shape[0] // (2 * CR)
+    chip_slots = 2 * CAP
+    facet = lax.axis_index("facet")
+    chips = lax.axis_size("facet") // 2
+    chip = facet // 2
+    core = facet % 2
+
+    padded = -(-slots // 8) * 8
+    number = lax.broadcasted_iota(jnp.int32, (padded, strip_rows), 0)
+    message = number // chip_slots + 1
+    owner = jnp.where(core == 0, chip, send_to(message, chip, chips))
+    slot = owner * chip_slots + number % chip_slots
+    subgrids = slot_ref.shape[1]
+    match = slot[:, :subgrids] == slot_ref[...]
+    order = lax.broadcasted_iota(jnp.int32, match.shape, 1).astype(jnp.float32) + 1.0
+    found = jnp.sum(jnp.where(match, order, 0.0), axis=1, keepdims=True)
+    live = jnp.broadcast_to(jnp.where(found > 0.0, 1.0, 0.0), (padded, strip_rows))
+    first = jnp.broadcast_to(jnp.maximum(found - 1.0, 0.0).astype(jnp.int32) * CR, (padded, strip_rows))
+
+    step = 2.0 * math.pi / total
+
+    def turn(product):
+        if total & (total - 1) == 0:
+            product = product & (total - 1)
+        else:
+            product = lax.rem(product, total)
+        angle = step * product.astype(jnp.float32)
+        return jnp.cos(angle), jnp.sin(angle)
+
+    lane = lax.broadcasted_iota(jnp.int32, (padded, strip_rows), 1)
+    row = lax.broadcasted_iota(jnp.int32, (CR, strip_rows), 0)
+    for side in range(2):
+        cell = (facet if side == 0 else facet ^ 1) * strip_rows + lane
+        row_cos, row_sin = turn(row * cell[:1])
+        first_cos, first_sin = turn(first * cell)
+        first_cos, first_sin = first_cos * live, first_sin * live
+        left = pl.ds(2 * side * strip_rows, strip_rows)
+        right = pl.ds((2 * side + 1) * strip_rows, strip_rows)
+        for c in range(slots):
+            base_cos, base_sin = first_cos[c : c + 1], first_sin[c : c + 1]
+            cos = (base_cos * row_cos - base_sin * row_sin).astype(jnp.bfloat16)
+            sin = (base_sin * row_cos + base_cos * row_sin).astype(jnp.bfloat16)
+            at = c * 2 * CR
+            phase_ref[pl.ds(at, CR), left] = cos
+            phase_ref[pl.ds(at, CR), right] = sin
+            phase_ref[pl.ds(at + CR, CR), left] = -sin
+            phase_ref[pl.ds(at + CR, CR), right] = cos
+
+    partial_ref[...] = jnp.dot(
+        phase_ref[:, : 2 * strip_rows], spec_ref[...], preferred_element_type=jnp.float32
+    )
+
+
+def term_kernel(scale, phase_ref, partial_ref, other_ref, *out_refs):
+    depth = other_ref.shape[0]
     height = out_refs[0].shape[0]
 
-    def write_terms(k):
-        at = pl.ds(k * height, height)
-        terms = jnp.dot(phase_ref[at, :depth], own_ref[...], preferred_element_type=jnp.float32)
-        terms += jnp.dot(phase_ref[at, depth:], other_ref[...], preferred_element_type=jnp.float32)
-        out_refs[k][...] = (terms * scale).astype(jnp.bfloat16)
-
-    write_terms(0)
-
-    @pl.when(lax.axis_index("facet") % 2 == 1)
+    def write_terms(count):
+        rows = count * height
+        terms = partial_ref[:rows] + jnp.dot(
+            phase_ref[:rows, depth:], other_ref[...], preferred_element_type=jnp.float32
+        )
+        terms = (terms * scale).astype(jnp.bfloat16)
+        for k in range(count):
+            out_refs[k][...] = terms[k * height : (k + 1) * height]
+
+    core = lax.axis_index("facet") % 2
+
+    @pl.when(core == 0)
     def _():
-        for k in range(1, len(out_refs)):
-            write_terms(k)
+        write_terms(1)
+
+    @pl.when(core == 1)
+    def _():
+        write_terms(len(out_refs))
 
 
 def weights_kernel(
@@ -239,41 +257,48 @@
     blocks, points = vis_pos.shape[2], vis_pos.shape[4]
     share_rows = CAP * 2 * CR
     height = 2 * share_rows
-    chunks = 4
+    chunks = 1
     core = lax.axis_index("facet") % 2
 
     def swap(x):
         return lax.ppermute(x, "facet", [(i, i ^ 1) for i in range(facet_count)])
 
     strip = facets.reshape(2 * strip_rows, length)
-    table = jnp.asarray(column_map(length, SG))
+    seed = jnp.asarray(column_seed(length, SG))
     term_shape = jax.ShapeDtypeStruct((height, SG), jnp.bfloat16)
-    spectrum, phases = pl.pallas_call(
-        functools.partial(front_kernel, sky_rows, chunks),
-        out_shape=(
-            jax.ShapeDtypeStruct((2 * strip_rows, SG), jnp.bfloat16),
-            jax.ShapeDtypeStruct(((chips - 1) * height, 4 * strip_rows), jnp.bfloat16),
-        ),
-        in_specs=[HBM] * 4,
-        out_specs=(VMEM,) * 2,
+    spectrum = pl.pallas_call(
+        functools.partial(front_kernel, chunks),
+        out_shape=jax.ShapeDtypeStruct((2 * strip_rows, SG), jnp.bfloat16),
+        in_specs=[HBM] * 3,
+        out_specs=VMEM,
         scratch_shapes=[
             pltpu.VMEM((2 * strip_rows, length), jnp.bfloat16),
             pltpu.VMEM((length // 2, 2 * SG), jnp.bfloat16),
             pltpu.VMEM((1, length), jnp.float32),
-            pltpu.SMEM(slot_of_subgrid.shape, jnp.int32),
+            pltpu.VMEM(seed.shape, seed.dtype),
             pltpu.SemaphoreType.DMA((2 * chunks,)),
-            pltpu.SemaphoreType.DMA((chunks,)),
             pltpu.SemaphoreType.DMA((2,)),
-            pltpu.SMEM((facet_count * CAP,), jnp.int32),
         ],
         compiler_params=pltpu.CompilerParams(vmem_limit_bytes=32 * 2**20),
         name="front",
     )(*(
         pltpu.with_memory_space_constraint(x, pltpu.HBM)
-        for x in (slot_of_subgrid, strip, col_window.reshape(1, length), table)
+        for x in (strip, col_window.reshape(1, length), seed)
     ))
 
     other = swap(spectrum)
+    phase_rows = (chips - 1) * height
+    phases, partial = pl.pallas_call(
+        functools.partial(phase_kernel, sky_rows),
+        out_shape=(
+            jax.ShapeDtypeStruct((phase_rows, 4 * strip_rows), jnp.bfloat16),
+            jax.ShapeDtypeStruct((phase_rows, SG), jnp.float32),
+        ),
+        in_specs=[VMEM] * 2,
+        out_specs=(VMEM,) * 2,
+        compiler_params=pltpu.CompilerParams(vmem_limit_bytes=32 * 2**20),
+        name="phases",
+    )(slot_of_subgrid.reshape(1, -1), spectrum)
     terms = pl.pallas_call(
         functools.partial(term_kernel, 1.0 / math.sqrt(sky_rows)),
         out_shape=(term_shape,) * (chips - 1),
@@ -281,7 +306,7 @@
         out_specs=(VMEM,) * (chips - 1),
         compiler_params=pltpu.CompilerParams(vmem_limit_bytes=16 * 2**20),
         name="terms",
-    )(phases, spectrum, other)
+    )(phases, partial, other)
     arrived = [
         lax.ppermute(
             terms[k - 1],

time: 21.9 us -> 21 us (0.959)
  waiting for transfers between devices: 6.05 us -> 5.66 us
  Pallas kernels: 5.81 us -> 5.51 us
    ppermute x2, waiting for transfers between devices: 1.93 us -> 1.54 us  [swap(): return lax.ppermute(x, 'facet', [(i, i ^ 1) for i in range(facet_count)])]
    pallas_call x1 -> x2, Pallas kernels: 3.04 us -> 2.76 us  [the longest x1 2.38 us: local(): pl.pallas_call(functools.partial(front_kernel, chunks), out_shape=jax.Sha...]
  transfers between devices with their start and end apart: 8 -> 8, of which waited for: 8 -> 8; matrix products, arithmetic and copies ran while one was open for 0% -> 0% of each run, Pallas kernels for 7% -> 9%
where the time goes in v4:
time: 21 us; the launch traced here: 20.9 us
  starting transfers between devices  8.82 us (42%)
  waiting for transfers between devices  5.66 us (27%)
  Pallas kernels  5.51 us (26%)
  between operations  0.76 us (4%)
    ppermute x3, starting transfers between devices, local(): lax.ppermute(terms[k - 1], 'facet', [(i, 2 * send_to(k, i // 2, chips) if...  4.16 us
    ppermute x3, waiting for transfers between devices, local(): lax.ppermute(terms[k - 1], 'facet', [(i, 2 * send_to(k, i // 2, chips) if...  2.78 us
    ppermute x3, starting transfers between devices, local(): lax.ppermute(chip_subs, ('band', 'facet'), [(device(b, f), device(b, f -...  2.76 us
    pallas_call x1, Pallas kernels, local(): pl.pallas_call(functools.partial(front_kernel, chunks), out_shape=jax.Sha...  2.38 us
    ppermute x2, starting transfers between devices, swap(): return lax.ppermute(x, 'facet', [(i, i ^ 1) for i in range(facet_count)])  1.9 us
    ppermute x2, waiting for transfers between devices, swap(): return lax.ppermute(x, 'facet', [(i, i ^ 1) for i in range(facet_count)])  1.54 us
    pallas_call x1, Pallas kernels, local(): pl.pallas_call(functools.partial(weights_kernel, band_count), out_shape=(...  1.43 us
    ppermute x3, waiting for transfers between devices, local(): lax.ppermute(chip_subs, ('band', 'facet'), [(device(b, f), device(b, f -...  1.34 us
  transfers between devices with their start and end apart: 8, of which 8 were waited for; matrix products, arithmetic and copies ran while one was open for 0% of the time, Pallas kernels for 9%

profile of v4, /device:TPU:0, one launch (start us, length us, event | category | flops | bytes accessed | tf_op | source)
XLA Modules:
  0.0 20.9 jit_solution(6002840953898303640)
XLA Ops:
  0.6 0.0 copy-start
  0.6 0.0 copy-start.1
  0.7 0.0 copy-start.5
  0.7 0.0 copy-start.4
  0.7 0.0 copy-start.3
  0.7 0.0 copy-start.2
  0.7 2.4 %front.1.spec_ref = bf16[256,256]{1,0:T(8,128)(2,1)S(1)} custom-call(bf16[256,4096]{1,0:T(8,128)(2,1)} %bitcast.16, f32[1,4096]{1,0:T(1,128)} %bitcast.17, bf16[64,128]{1,0:T(8,128)(2,1)} %constant.4.clone.seed_hbm), custom_call_target="tpu_custom_call" | custom-call | tf_op jit(solution)/shard_map/front/pallas_call | solution.py:269
  3.1 0.5 %collective-permute-start = (bf16[256,256]{1,0:T(8,128)(2,1)S(1)}, bf16[256,256]{1,0:T(8,128)(2,1)S(1)}, u32[]{:S(2)}, u32[]{:S(2)}) collective-permute-start(bf16[256,256]{1,0:T(8,128)(2,1)S(1)} %front.1.spec_ref), channel_id=1, source_target_pairs={{0,1},{1,0},{2,3},{3,2},{4,5},{5,4},{6,7},{7,6},{8,9},{9,8},{10,11... | collective-permute-start | bytes 393224 | tf_op jit(solution)/shard_map/ppermute | solution.py:264
  3.6 0.0 copy-done
  3.6 0.4 %phases.1 = (bf16[384,512]{1,0:T(8,128)(2,1)S(1)}, f32[384,256]{1,0:T(8,128)S(1)}) custom-call(s32[1,12]{1,0:T(1,128)S(1)} %bitcast.10, bf16[256,256]{1,0:T(8,128)(2,1)S(1)} %front.1.spec_ref), custom_call_target="tpu_custom_call" | custom-call | tf_op jit(solution)/shard_map/phases/pallas_call | solution.py:291
  4.0 0.6 %collective-permute-done.other_ref = bf16[256,256]{1,0:T(8,128)(2,1)S(1)} collective-permute-done((bf16[256,256]{1,0:T(8,128)(2,1)S(1)}, bf16[256,256]{1,0:T(8,128)(2,1)S(1)}, u32[]{:S(2)}, u32[]{:S(2)}) %collective-permute-start) | collective-permute-done | bytes 131104 | tf_op jit(solution)/shard_map/ppermute | solution.py:264
  4.6 0.2 terms.1
  4.8 0.5 %collective-permute-start.2 = (bf16[128,256]{1,0:T(8,128)(2,1)S(1)}, bf16[128,256]{1,0:T(8,128)(2,1)S(1)}, u32[]{:S(2)}, u32[]{:S(2)}) collective-permute-start(bf16[128,256]{1,0:T(8,128)(2,1)S(1)} %get-tuple-element.17), channel_id=1, source_target_pairs={{0,1},{1,4},{2,3},{3,6},{4,5},{5,0},{6,7},{7,2},{8,9},{9,12},{10,1... | collective-permute-start | bytes 196616 | tf_op jit(solution)/shard_map/ppermute | solution.py:311
  5.2 2.6 %collective-permute-start.3 = (bf16[128,256]{1,0:T(8,128)(2,1)S(1)}, bf16[128,256]{1,0:T(8,128)(2,1)S(1)}, u32[]{:S(2)}, u32[]{:S(2)}) collective-permute-start(bf16[128,256]{1,0:T(8,128)(2,1)S(1)} %get-tuple-element.18), channel_id=1, source_target_pairs={{0,1},{1,6},{2,3},{3,4},{4,5},{5,2},{6,7},{7,0},{8,9},{9,14},{10,1... | collective-permute-start | bytes 196616 | tf_op jit(solution)/shard_map/ppermute | solution.py:311
  7.8 1.1 %collective-permute-start.1 = (bf16[128,256]{1,0:T(8,128)(2,1)S(1)}, bf16[128,256]{1,0:T(8,128)(2,1)S(1)}, u32[]{:S(2)}, u32[]{:S(2)}) collective-permute-start(bf16[128,256]{1,0:T(8,128)(2,1)S(1)} %get-tuple-element.16), channel_id=1, source_target_pairs={{0,1},{1,2},{2,3},{3,0},{4,5},{5,6},{6,7},{7,4},{8,9},{9,10},{10,1... | collective-permute-start | bytes 196616 | tf_op jit(solution)/shard_map/ppermute | solution.py:311
  8.9 0.5 %collective-permute-done.2 = bf16[128,256]{1,0:T(8,128)(2,1)S(1)} collective-permute-done((bf16[128,256]{1,0:T(8,128)(2,1)S(1)}, bf16[128,256]{1,0:T(8,128)(2,1)S(1)}, u32[]{:S(2)}, u32[]{:S(2)}) %collective-permute-start.2) | collective-permute-done | bytes 65568 | tf_op jit(solution)/shard_map/ppermute | solution.py:311
  9.4 1.4 %collective-permute-done.3 = bf16[128,256]{1,0:T(8,128)(2,1)S(1)} collective-permute-done((bf16[128,256]{1,0:T(8,128)(2,1)S(1)}, bf16[128,256]{1,0:T(8,128)(2,1)S(1)}, u32[]{:S(2)}, u32[]{:S(2)}) %collective-permute-start.3) | collective-permute-done | bytes 65568 | tf_op jit(solution)/shard_map/ppermute | solution.py:311
  10.8 0.9 %collective-permute-done.1 = bf16[128,256]{1,0:T(8,128)(2,1)S(1)} collective-permute-done((bf16[128,256]{1,0:T(8,128)(2,1)S(1)}, bf16[128,256]{1,0:T(8,128)(2,1)S(1)}, u32[]{:S(2)}, u32[]{:S(2)}) %collective-permute-start.1) | collective-permute-done | bytes 65568 | tf_op jit(solution)/shard_map/ppermute | solution.py:311
  11.8 2.4 %collective-permute-start.6 = (bf16[128,256]{1,0:T(8,128)(2,1)S(1)}, bf16[128,256]{1,0:T(8,128)(2,1)S(1)}, u32[]{:S(2)}, u32[]{:S(2)}) collective-permute-start(bf16[128,256]{1,0:T(8,128)(2,1)S(1)} %add_convert_fusion.after_ref.sub_ref), channel_id=1, source_target_pairs={{0,25},{1,0},{2,27},{3,2},{4,29},{5,4},{6,31},{7,6},{8,17},{9,8},{... | collective-permute-start | bytes 196616 | tf_op jit(solution)/shard_map/ppermute | solution.py:350
  14.2 0.3 %collective-permute-start.5 = (bf16[128,256]{1,0:T(8,128)(2,1)S(1)}, bf16[128,256]{1,0:T(8,128)(2,1)S(1)}, u32[]{:S(2)}, u32[]{:S(2)}) collective-permute-start(bf16[128,256]{1,0:T(8,128)(2,1)S(1)} %add_convert_fusion.after_ref.sub_ref), channel_id=1, source_target_pairs={{0,17},{1,0},{2,19},{3,2},{4,21},{5,4},{6,23},{7,6},{8,25},{9,8},{... | collective-permute-start | bytes 196616 | tf_op jit(solution)/shard_map/ppermute | solution.py:350
  14.5 0.0 collective-permute-start.4
  14.5 0.0 copy-done.1
  14.5 0.0 copy-done.5
  14.5 0.0 copy-done.4
  14.5 0.0 copy-done.3
  14.6 1.4 %weights.1 = (bf16[4,128,2048]{2,1,0:T(8,128)(2,1)S(1)}, f32[4,16,2048]{2,1,0:T(8,128)S(1)}, f32[4,8,8,128]{3,2,1,0:T(8,128)S(1)}, s32[4,32,128]{2,1,0:T(8,128)S(1)}, s32[8,256]{1,0:T(8,128)S(1)}) custom-call(s32[4]{0:T(128)S(1)} %bitcast.12, s32[4]{0:T(128)S(1)} %bitcast.13, s32[4]{0:T(128)S(1)} %bitcast.14, f32[4]{0:T(128)S(1)} %bitcast.15, ...), custom_call_target="tpu_custom_call" | custom-call | flops 8388608 | tf_op jit(solution)/shard_map/weights/pallas_call | solution.py:326
  16.0 0.1 collective-permute-done.6.refs_2_
  16.1 0.6 %collective-permute-done.5.refs_1_ = bf16[128,256]{1,0:T(8,128)(2,1)S(1)} collective-permute-done((bf16[128,256]{1,0:T(8,128)(2,1)S(1)}, bf16[128,256]{1,0:T(8,128)(2,1)S(1)}, u32[]{:S(2)}, u32[]{:S(2)}) %collective-permute-start.5) | collective-permute-done | bytes 65568 | tf_op jit(solution)/shard_map/ppermute | solution.py:350
  16.7 0.7 %collective-permute-done.4.refs_0_ = bf16[128,256]{1,0:T(8,128)(2,1)S(1)} collective-permute-done((bf16[128,256]{1,0:T(8,128)(2,1)S(1)}, bf16[128,256]{1,0:T(8,128)(2,1)S(1)}, u32[]{:S(2)}, u32[]{:S(2)}) %collective-permute-start.4) | collective-permute-done | bytes 65568 | tf_op jit(solution)/shard_map/ppermute | solution.py:350
  17.4 1.4 %collective-permute-start.7 = (bf16[192,256]{1,0:T(8,128)(2,1)S(1)}, bf16[192,256]{1,0:T(8,128)(2,1)S(1)}, u32[]{:S(2)}, u32[]{:S(2)}) collective-permute-start(bf16[192,256]{1,0:T(8,128)(2,1)S(1)} %maximum_select_fusion), channel_id=1, source_target_pairs={{0,1},{1,0},{2,3},{3,2},{4,5},{5,4},{6,7},{7,6},{8,9},{9,8},{10,11... | collective-permute-start | bytes 294920 | tf_op jit(solution)/shard_map/ppermute | solution.py:264
  18.8 0.9 %collective-permute-done.7.swap_ref = bf16[192,256]{1,0:T(8,128)(2,1)S(1)} collective-permute-done((bf16[192,256]{1,0:T(8,128)(2,1)S(1)}, bf16[192,256]{1,0:T(8,128)(2,1)S(1)}, u32[]{:S(2)}, u32[]{:S(2)}) %collective-permute-start.7) | collective-permute-done | bytes 98336 | tf_op jit(solution)/shard_map/ppermute | solution.py:264
  19.7 1.2 %degrid.1 = (bf16[64,256]{1,0:T(8,128)(2,1)}, f32[4,2,2048]{2,1,0:T(2,128)}) custom-call(f32[4,8,8,128]{3,2,1,0:T(8,128)S(1)} %get-tuple-element.19.mix_ref, s32[4,32,128]{2,1,0:T(8,128)S(1)} %get-tuple-element.20.lane_ref, bf16[4,128,2048]{2,1,0:T(8,128)(2,1)S(1)} %get-tuple-element.21.col_ref, f32[4,16,2048]{2,1,0:T(8,128)S(1)} %get-tuple-element.22.row_ref, ...), custom_call_target="tpu_custom_call" | custom-call | tf_op jit(solution)/shard_map/degrid/pallas_call | solution.py:367
  (8 shorter events, 0.1 us)
Async XLA Ops:
  0.6 3.0 %copy-start = (s32[12]{0:T(128)S(1)}, s32[12]{0:T(128)}, u32[]{:S(2)}) copy-start(s32[12]{0:T(128)} %param.11) | copy-start | bytes 148
  0.6 13.9 %copy-start.1 = (f32[1,1,4,2,2048]{4,3,2,1,0:T(2,128)S(1)}, f32[1,1,4,2,2048]{4,3,2,1,0:T(2,128)}, u32[]{:S(2)}) copy-start(f32[1,1,4,2,2048]{4,3,2,1,0:T(2,128)} %param.16) | copy-start | bytes 196612
  0.7 13.9 %copy-start.5 = (f32[1,1,4]{2,1,0:T(1,128)S(1)}, f32[1,1,4]{2,1,0:T(1,128)}, u32[]{:S(2)}) copy-start(f32[1,1,4]{2,1,0:T(1,128)} %param.15) | copy-start | bytes 52
  0.7 13.9 %copy-start.4 = (s32[1,1,4]{2,1,0:T(1,128)S(1)}, s32[1,1,4]{2,1,0:T(1,128)}, u32[]{:S(2)}) copy-start(s32[1,1,4]{2,1,0:T(1,128)} %param.14) | copy-start | bytes 52
  0.7 13.9 %copy-start.3 = (s32[1,1,4]{2,1,0:T(1,128)S(1)}, s32[1,1,4]{2,1,0:T(1,128)}, u32[]{:S(2)}) copy-start(s32[1,1,4]{2,1,0:T(1,128)} %param.13) | copy-start | bytes 52
  0.7 13.9 %copy-start.2 = (s32[1,1,4]{2,1,0:T(1,128)S(1)}, s32[1,1,4]{2,1,0:T(1,128)}, u32[]{:S(2)}) copy-start(s32[1,1,4]{2,1,0:T(1,128)} %param.12) | copy-start | bytes 52
  3.1 1.5 %collective-permute-start = (bf16[256,256]{1,0:T(8,128)(2,1)S(1)}, bf16[256,256]{1,0:T(8,128)(2,1)S(1)}, u32[]{:S(2)}, u32[]{:S(2)}) collective-permute-start(bf16[256,256]{1,0:T(8,128)(2,1)S(1)} %front.1.spec_ref), channel_id=1, source_target_pairs={{0,1},{1,0},{2,3},{3,2},{4,5},{5,4},{6,7},{7,6},{8,9},{9,8},{10,11... | collective-permute-start | bytes 393224 | tf_op jit(solution)/shard_map/ppermute | solution.py:264
  4.8 4.7 %collective-permute-start.2 = (bf16[128,256]{1,0:T(8,128)(2,1)S(1)}, bf16[128,256]{1,0:T(8,128)(2,1)S(1)}, u32[]{:S(2)}, u32[]{:S(2)}) collective-permute-start(bf16[128,256]{1,0:T(8,128)(2,1)S(1)} %get-tuple-element.17), channel_id=1, source_target_pairs={{0,1},{1,4},{2,3},{3,6},{4,5},{5,0},{6,7},{7,2},{8,9},{9,12},{10,1... | collective-permute-start | bytes 196616 | tf_op jit(solution)/shard_map/ppermute | solution.py:311
  5.2 5.6 %collective-permute-start.3 = (bf16[128,256]{1,0:T(8,128)(2,1)S(1)}, bf16[128,256]{1,0:T(8,128)(2,1)S(1)}, u32[]{:S(2)}, u32[]{:S(2)}) collective-permute-start(bf16[128,256]{1,0:T(8,128)(2,1)S(1)} %get-tuple-element.18), channel_id=1, source_target_pairs={{0,1},{1,6},{2,3},{3,4},{4,5},{5,2},{6,7},{7,0},{8,9},{9,14},{10,1... | collective-permute-start | bytes 196616 | tf_op jit(solution)/shard_map/ppermute | solution.py:311
  7.8 3.9 %collective-permute-start.1 = (bf16[128,256]{1,0:T(8,128)(2,1)S(1)}, bf16[128,256]{1,0:T(8,128)(2,1)S(1)}, u32[]{:S(2)}, u32[]{:S(2)}) collective-permute-start(bf16[128,256]{1,0:T(8,128)(2,1)S(1)} %get-tuple-element.16), channel_id=1, source_target_pairs={{0,1},{1,2},{2,3},{3,0},{4,5},{5,6},{6,7},{7,4},{8,9},{9,10},{10,1... | collective-permute-start | bytes 196616 | tf_op jit(solution)/shard_map/ppermute | solution.py:311
  11.8 4.3 %collective-permute-start.6 = (bf16[128,256]{1,0:T(8,128)(2,1)S(1)}, bf16[128,256]{1,0:T(8,128)(2,1)S(1)}, u32[]{:S(2)}, u32[]{:S(2)}) collective-permute-start(bf16[128,256]{1,0:T(8,128)(2,1)S(1)} %add_convert_fusion.after_ref.sub_ref), channel_id=1, source_target_pairs={{0,25},{1,0},{2,27},{3,2},{4,29},{5,4},{6,31},{7,6},{8,17},{9,8},{... | collective-permute-start | bytes 196616 | tf_op jit(solution)/shard_map/ppermute | solution.py:350
  14.2 2.5 %collective-permute-start.5 = (bf16[128,256]{1,0:T(8,128)(2,1)S(1)}, bf16[128,256]{1,0:T(8,128)(2,1)S(1)}, u32[]{:S(2)}, u32[]{:S(2)}) collective-permute-start(bf16[128,256]{1,0:T(8,128)(2,1)S(1)} %add_convert_fusion.after_ref.sub_ref), channel_id=1, source_target_pairs={{0,17},{1,0},{2,19},{3,2},{4,21},{5,4},{6,23},{7,6},{8,25},{9,8},{... | collective-permute-start | bytes 196616 | tf_op jit(solution)/shard_map/ppermute | solution.py:350
  14.5 2.9 %collective-permute-start.4 = (bf16[128,256]{1,0:T(8,128)(2,1)S(1)}, bf16[128,256]{1,0:T(8,128)(2,1)S(1)}, u32[]{:S(2)}, u32[]{:S(2)}) collective-permute-start(bf16[128,256]{1,0:T(8,128)(2,1)S(1)} %add_convert_fusion.after_ref.sub_ref), channel_id=1, source_target_pairs={{0,9},{1,0},{2,11},{3,2},{4,13},{5,4},{6,15},{7,6},{8,1},{9,8},{10... | collective-permute-start | bytes 196616 | tf_op jit(solution)/shard_map/ppermute | solution.py:350
  17.4 2.3 %collective-permute-start.7 = (bf16[192,256]{1,0:T(8,128)(2,1)S(1)}, bf16[192,256]{1,0:T(8,128)(2,1)S(1)}, u32[]{:S(2)}, u32[]{:S(2)}) collective-permute-start(bf16[192,256]{1,0:T(8,128)(2,1)S(1)} %maximum_select_fusion), channel_id=1, source_target_pairs={{0,1},{1,0},{2,3},{3,2},{4,5},{5,4},{6,7},{7,6},{8,9},{9,8},{10,11... | collective-permute-start | bytes 294920 | tf_op jit(solution)/shard_map/ppermute | solution.py:264

commit v5 on v4

--- a/solution.py
+++ b/solution.py
@@ -21,12 +21,16 @@
 HBM = pl.BlockSpec(memory_space=pltpu.HBM)
 
 
-def send_to(k, i, n):
+def chip_to(k, i, n):
     return i ^ k if n & (n - 1) == 0 else (i + k) % n
 
 
-def recv_from(k, i, n):
-    return i ^ k if n & (n - 1) == 0 else (i - k + n) % n
+def band_to(k, i, n):
+    return (i + k) % n
+
+
+def band_from(k, i, n):
+    return (i - k + n) % n
 
 
 def column_seed(length, width):
@@ -117,7 +121,7 @@
     padded = -(-slots // 8) * 8
     number = lax.broadcasted_iota(jnp.int32, (padded, strip_rows), 0)
     message = number // chip_slots + 1
-    owner = jnp.where(core == 0, chip, send_to(message, chip, chips))
+    owner = jnp.where(core == 0, chip, chip_to(message, chip, chips))
     slot = owner * chip_slots + number % chip_slots
     subgrids = slot_ref.shape[1]
     match = slot[:, :subgrids] == slot_ref[...]
@@ -199,7 +203,7 @@
         slot = slot_ref[v]
         weight = weight_ref[v]
         for k in range(bands):
-            band = recv_from(k, me, bands)
+            band = band_from(k, me, bands)
             share = jnp.where(band == low, 1.0 - weight, jnp.where(band == low + 1, weight, 0.0))
             for c in range(CAP):
                 mix_ref[v, k * CAP + c] = jnp.full((8, 128), jnp.where(slot == c, share, 0.0), jnp.float32)
@@ -220,8 +224,8 @@
     parts = [jnp.where(core == 0, sub_ref[:share_rows], swap_ref[:share_rows])]
     own_ref[...] = parts[0]
     for k in range(1, bands):
-        at = pl.ds((k - 1) * share_rows, share_rows)
-        parts.append(jnp.where(core == 0, swap_ref[at], band_refs[k - 1][share_rows:]))
+        at = pl.ds((bands - 1 - k) * share_rows, share_rows)
+        parts.append(jnp.where(core == 0, swap_ref[at], band_refs[bands - 1 - k][share_rows:]))
     held = [
         part[c * height : (c + 1) * height].astype(jnp.float32) for part in parts for c in range(CAP)
     ]
@@ -312,7 +316,7 @@
             terms[k - 1],
             "facet",
             [
-                (i, 2 * send_to(k, i // 2, chips) if i % 2 else i + 1)
+                (i, 2 * chip_to(k, i // 2, chips) if i % 2 else i + 1)
                 for i in range(facet_count)
             ],
         )
@@ -351,13 +355,13 @@
             chip_subs,
             ("band", "facet"),
             [
-                (device(b, f), device(b, f - 1) if f % 2 else device(send_to(k, b, band_count), f + 1))
+                (device(b, f), device(b, f - 1) if f % 2 else device(band_to(k, b, band_count), f + 1))
                 for b in range(band_count)
                 for f in range(facet_count)
             ],
         )
         for k in range(1, band_count)
-    ]
+    ][::-1]
     for_other = jnp.where(
         core_map[:1] == 0,
         jnp.concatenate([chip_subs[share_rows:]] * (band_count - 1)),

time: 21 us -> 20.7 us (0.986)
  waiting for transfers between devices: 5.66 us -> 4.7 us
  starting transfers between devices: 8.82 us -> 9.42 us
    ppermute x3, starting transfers between devices: 2.76 us -> 3.84 us  [local(): lax.ppermute(chip_subs, ('band', 'facet'), [(device(b, f), device(b, f -...]
    ppermute x3, waiting for transfers between devices: 1.34 us -> 0.38 us  [local(): lax.ppermute(chip_subs, ('band', 'facet'), [(device(b, f), device(b, f -...]
    ppermute x2, starting transfers between devices: 1.9 us -> 1.41 us  [swap(): return lax.ppermute(x, 'facet', [(i, i ^ 1) for i in range(facet_count)])]
  transfers between devices with their start and end apart: 8 -> 8, of which waited for: 8 -> 6; matrix products, arithmetic and copies ran while one was open for 0% -> 0% of each run, Pallas kernels for 9% -> 9%
where the time goes in v5:
time: 20.7 us; the launch traced here: 20.5 us
  starting transfers between devices  9.42 us (46%)
  Pallas kernels  5.51 us (27%)
  waiting for transfers between devices  4.7 us (23%)
  between operations  0.77 us (4%)
    ppermute x3, starting transfers between devices, local(): lax.ppermute(terms[k - 1], 'facet', [(i, 2 * chip_to(k, i // 2, chips) if...  4.16 us
    ppermute x3, starting transfers between devices, local(): lax.ppermute(chip_subs, ('band', 'facet'), [(device(b, f), device(b, f -...  3.84 us
    ppermute x3, waiting for transfers between devices, local(): lax.ppermute(terms[k - 1], 'facet', [(i, 2 * chip_to(k, i // 2, chips) if...  2.78 us
    pallas_call x1, Pallas kernels, local(): pl.pallas_call(functools.partial(front_kernel, chunks), out_shape=jax.Sha...  2.38 us
    ppermute x2, waiting for transfers between devices, swap(): return lax.ppermute(x, 'facet', [(i, i ^ 1) for i in range(facet_count)])  1.54 us
    pallas_call x1, Pallas kernels, local(): pl.pallas_call(functools.partial(weights_kernel, band_count), out_shape=(...  1.43 us
    ppermute x2, starting transfers between devices, swap(): return lax.ppermute(x, 'facet', [(i, i ^ 1) for i in range(facet_count)])  1.41 us
    pallas_call x1, Pallas kernels, local(): pl.pallas_call(functools.partial(degrid_kernel, band_count), out_shape=(j...  1.15 us
  transfers between devices with their start and end apart: 8, of which 6 were waited for; matrix products, arithmetic and copies ran while one was open for 0% of the time, Pallas kernels for 9%

profile of v5, /device:TPU:0, one launch (start us, length us, event | category | flops | bytes accessed | tf_op | source)
XLA Modules:
  0.0 20.5 jit_solution(7089072161481060887)
XLA Ops:
  0.6 0.0 copy-start
  0.6 0.0 copy-start.1
  0.7 0.0 copy-start.5
  0.7 0.0 copy-start.4
  0.7 0.0 copy-start.3
  0.7 0.0 copy-start.2
  0.7 2.4 %front.1.spec_ref = bf16[256,256]{1,0:T(8,128)(2,1)S(1)} custom-call(bf16[256,4096]{1,0:T(8,128)(2,1)} %bitcast.16, f32[1,4096]{1,0:T(1,128)} %bitcast.17, bf16[64,128]{1,0:T(8,128)(2,1)} %constant.4.clone.seed_hbm), custom_call_target="tpu_custom_call" | custom-call | tf_op jit(solution)/shard_map/front/pallas_call | solution.py:273
  3.1 0.5 %collective-permute-start = (bf16[256,256]{1,0:T(8,128)(2,1)S(1)}, bf16[256,256]{1,0:T(8,128)(2,1)S(1)}, u32[]{:S(2)}, u32[]{:S(2)}) collective-permute-start(bf16[256,256]{1,0:T(8,128)(2,1)S(1)} %front.1.spec_ref), channel_id=1, source_target_pairs={{0,1},{1,0},{2,3},{3,2},{4,5},{5,4},{6,7},{7,6},{8,9},{9,8},{10,11... | collective-permute-start | bytes 393224 | tf_op jit(solution)/shard_map/ppermute | solution.py:268
  3.6 0.0 copy-done
  3.6 0.4 %phases.1 = (bf16[384,512]{1,0:T(8,128)(2,1)S(1)}, f32[384,256]{1,0:T(8,128)S(1)}) custom-call(s32[1,12]{1,0:T(1,128)S(1)} %bitcast.10, bf16[256,256]{1,0:T(8,128)(2,1)S(1)} %front.1.spec_ref), custom_call_target="tpu_custom_call" | custom-call | tf_op jit(solution)/shard_map/phases/pallas_call | solution.py:295
  4.0 0.6 %collective-permute-done.other_ref = bf16[256,256]{1,0:T(8,128)(2,1)S(1)} collective-permute-done((bf16[256,256]{1,0:T(8,128)(2,1)S(1)}, bf16[256,256]{1,0:T(8,128)(2,1)S(1)}, u32[]{:S(2)}, u32[]{:S(2)}) %collective-permute-start) | collective-permute-done | bytes 131104 | tf_op jit(solution)/shard_map/ppermute | solution.py:268
  4.6 0.2 terms.1
  4.8 0.5 %collective-permute-start.2 = (bf16[128,256]{1,0:T(8,128)(2,1)S(1)}, bf16[128,256]{1,0:T(8,128)(2,1)S(1)}, u32[]{:S(2)}, u32[]{:S(2)}) collective-permute-start(bf16[128,256]{1,0:T(8,128)(2,1)S(1)} %get-tuple-element.17), channel_id=1, source_target_pairs={{0,1},{1,4},{2,3},{3,6},{4,5},{5,0},{6,7},{7,2},{8,9},{9,12},{10,1... | collective-permute-start | bytes 196616 | tf_op jit(solution)/shard_map/ppermute | solution.py:315
  5.2 2.6 %collective-permute-start.3 = (bf16[128,256]{1,0:T(8,128)(2,1)S(1)}, bf16[128,256]{1,0:T(8,128)(2,1)S(1)}, u32[]{:S(2)}, u32[]{:S(2)}) collective-permute-start(bf16[128,256]{1,0:T(8,128)(2,1)S(1)} %get-tuple-element.18), channel_id=1, source_target_pairs={{0,1},{1,6},{2,3},{3,4},{4,5},{5,2},{6,7},{7,0},{8,9},{9,14},{10,1... | collective-permute-start | bytes 196616 | tf_op jit(solution)/shard_map/ppermute | solution.py:315
  7.8 1.1 %collective-permute-start.1 = (bf16[128,256]{1,0:T(8,128)(2,1)S(1)}, bf16[128,256]{1,0:T(8,128)(2,1)S(1)}, u32[]{:S(2)}, u32[]{:S(2)}) collective-permute-start(bf16[128,256]{1,0:T(8,128)(2,1)S(1)} %get-tuple-element.16), channel_id=1, source_target_pairs={{0,1},{1,2},{2,3},{3,0},{4,5},{5,6},{6,7},{7,4},{8,9},{9,10},{10,1... | collective-permute-start | bytes 196616 | tf_op jit(solution)/shard_map/ppermute | solution.py:315
  8.9 0.5 %collective-permute-done.2 = bf16[128,256]{1,0:T(8,128)(2,1)S(1)} collective-permute-done((bf16[128,256]{1,0:T(8,128)(2,1)S(1)}, bf16[128,256]{1,0:T(8,128)(2,1)S(1)}, u32[]{:S(2)}, u32[]{:S(2)}) %collective-permute-start.2) | collective-permute-done | bytes 65568 | tf_op jit(solution)/shard_map/ppermute | solution.py:315
  9.4 1.4 %collective-permute-done.3 = bf16[128,256]{1,0:T(8,128)(2,1)S(1)} collective-permute-done((bf16[128,256]{1,0:T(8,128)(2,1)S(1)}, bf16[128,256]{1,0:T(8,128)(2,1)S(1)}, u32[]{:S(2)}, u32[]{:S(2)}) %collective-permute-start.3) | collective-permute-done | bytes 65568 | tf_op jit(solution)/shard_map/ppermute | solution.py:315
  10.8 0.9 %collective-permute-done.1 = bf16[128,256]{1,0:T(8,128)(2,1)S(1)} collective-permute-done((bf16[128,256]{1,0:T(8,128)(2,1)S(1)}, bf16[128,256]{1,0:T(8,128)(2,1)S(1)}, u32[]{:S(2)}, u32[]{:S(2)}) %collective-permute-start.1) | collective-permute-done | bytes 65568 | tf_op jit(solution)/shard_map/ppermute | solution.py:315
  11.8 0.4 %collective-permute-start.6 = (bf16[128,256]{1,0:T(8,128)(2,1)S(1)}, bf16[128,256]{1,0:T(8,128)(2,1)S(1)}, u32[]{:S(2)}, u32[]{:S(2)}) collective-permute-start(bf16[128,256]{1,0:T(8,128)(2,1)S(1)} %add_convert_fusion.after_ref.sub_ref), channel_id=1, source_target_pairs={{0,9},{1,0},{2,11},{3,2},{4,13},{5,4},{6,15},{7,6},{8,17},{9,8},{1... | collective-permute-start | bytes 196616 | tf_op jit(solution)/shard_map/ppermute | solution.py:354
  12.2 2.4 %collective-permute-start.5 = (bf16[128,256]{1,0:T(8,128)(2,1)S(1)}, bf16[128,256]{1,0:T(8,128)(2,1)S(1)}, u32[]{:S(2)}, u32[]{:S(2)}) collective-permute-start(bf16[128,256]{1,0:T(8,128)(2,1)S(1)} %add_convert_fusion.after_ref.sub_ref), channel_id=1, source_target_pairs={{0,17},{1,0},{2,19},{3,2},{4,21},{5,4},{6,23},{7,6},{8,25},{9,8},{... | collective-permute-start | bytes 196616 | tf_op jit(solution)/shard_map/ppermute | solution.py:354
  14.5 1.1 %collective-permute-start.4 = (bf16[128,256]{1,0:T(8,128)(2,1)S(1)}, bf16[128,256]{1,0:T(8,128)(2,1)S(1)}, u32[]{:S(2)}, u32[]{:S(2)}) collective-permute-start(bf16[128,256]{1,0:T(8,128)(2,1)S(1)} %add_convert_fusion.after_ref.sub_ref), channel_id=1, source_target_pairs={{0,25},{1,0},{2,27},{3,2},{4,29},{5,4},{6,31},{7,6},{8,1},{9,8},{1... | collective-permute-start | bytes 196616 | tf_op jit(solution)/shard_map/ppermute | solution.py:354
  15.6 0.0 copy-done.1
  15.6 0.0 copy-done.5
  15.6 0.0 copy-done.3
  15.6 0.0 copy-done.2
  15.6 1.4 %weights.1 = (bf16[4,128,2048]{2,1,0:T(8,128)(2,1)S(1)}, f32[4,16,2048]{2,1,0:T(8,128)S(1)}, f32[4,8,8,128]{3,2,1,0:T(8,128)S(1)}, s32[4,32,128]{2,1,0:T(8,128)S(1)}, s32[8,256]{1,0:T(8,128)S(1)}) custom-call(s32[4]{0:T(128)S(1)} %bitcast.12, s32[4]{0:T(128)S(1)} %bitcast.13, s32[4]{0:T(128)S(1)} %bitcast.14, f32[4]{0:T(128)S(1)} %bitcast.15, ...), custom_call_target="tpu_custom_call" | custom-call | flops 8388608 | tf_op jit(solution)/shard_map/weights/pallas_call | solution.py:330
  17.1 0.0 collective-permute-done.6.refs_2_
  17.1 0.0 collective-permute-done.5.refs_1_
  17.1 0.4 %collective-permute-done.4.refs_0_ = bf16[128,256]{1,0:T(8,128)(2,1)S(1)} collective-permute-done((bf16[128,256]{1,0:T(8,128)(2,1)S(1)}, bf16[128,256]{1,0:T(8,128)(2,1)S(1)}, u32[]{:S(2)}, u32[]{:S(2)}) %collective-permute-start.4) | collective-permute-done | bytes 65568 | tf_op jit(solution)/shard_map/ppermute | solution.py:354
  17.5 0.9 %collective-permute-start.7 = (bf16[192,256]{1,0:T(8,128)(2,1)S(1)}, bf16[192,256]{1,0:T(8,128)(2,1)S(1)}, u32[]{:S(2)}, u32[]{:S(2)}) collective-permute-start(bf16[192,256]{1,0:T(8,128)(2,1)S(1)} %maximum_select_fusion), channel_id=1, source_target_pairs={{0,1},{1,0},{2,3},{3,2},{4,5},{5,4},{6,7},{7,6},{8,9},{9,8},{10,11... | collective-permute-start | bytes 294920 | tf_op jit(solution)/shard_map/ppermute | solution.py:268
  18.4 0.9 %collective-permute-done.7.swap_ref = bf16[192,256]{1,0:T(8,128)(2,1)S(1)} collective-permute-done((bf16[192,256]{1,0:T(8,128)(2,1)S(1)}, bf16[192,256]{1,0:T(8,128)(2,1)S(1)}, u32[]{:S(2)}, u32[]{:S(2)}) %collective-permute-start.7) | collective-permute-done | bytes 98336 | tf_op jit(solution)/shard_map/ppermute | solution.py:268
  19.4 1.2 %degrid.1 = (bf16[64,256]{1,0:T(8,128)(2,1)}, f32[4,2,2048]{2,1,0:T(2,128)}) custom-call(f32[4,8,8,128]{3,2,1,0:T(8,128)S(1)} %get-tuple-element.19.mix_ref, s32[4,32,128]{2,1,0:T(8,128)S(1)} %get-tuple-element.20.lane_ref, bf16[4,128,2048]{2,1,0:T(8,128)(2,1)S(1)} %get-tuple-element.21.col_ref, f32[4,16,2048]{2,1,0:T(8,128)S(1)} %get-tuple-element.22.row_ref, ...), custom_call_target="tpu_custom_call" | custom-call | tf_op jit(solution)/shard_map/degrid/pallas_call | solution.py:371
  (8 shorter events, 0.1 us)
Async XLA Ops:
  0.6 3.0 %copy-start = (s32[12]{0:T(128)S(1)}, s32[12]{0:T(128)}, u32[]{:S(2)}) copy-start(s32[12]{0:T(128)} %param.11) | copy-start | bytes 148
  0.6 15.0 %copy-start.1 = (f32[1,1,4,2,2048]{4,3,2,1,0:T(2,128)S(1)}, f32[1,1,4,2,2048]{4,3,2,1,0:T(2,128)}, u32[]{:S(2)}) copy-start(f32[1,1,4,2,2048]{4,3,2,1,0:T(2,128)} %param.16) | copy-start | bytes 196612
  0.7 15.0 %copy-start.5 = (f32[1,1,4]{2,1,0:T(1,128)S(1)}, f32[1,1,4]{2,1,0:T(1,128)}, u32[]{:S(2)}) copy-start(f32[1,1,4]{2,1,0:T(1,128)} %param.15) | copy-start | bytes 52
  0.7 14.9 %copy-start.4 = (s32[1,1,4]{2,1,0:T(1,128)S(1)}, s32[1,1,4]{2,1,0:T(1,128)}, u32[]{:S(2)}) copy-start(s32[1,1,4]{2,1,0:T(1,128)} %param.14) | copy-start | bytes 52
  0.7 14.9 %copy-start.3 = (s32[1,1,4]{2,1,0:T(1,128)S(1)}, s32[1,1,4]{2,1,0:T(1,128)}, u32[]{:S(2)}) copy-start(s32[1,1,4]{2,1,0:T(1,128)} %param.13) | copy-start | bytes 52
  0.7 14.9 %copy-start.2 = (s32[1,1,4]{2,1,0:T(1,128)S(1)}, s32[1,1,4]{2,1,0:T(1,128)}, u32[]{:S(2)}) copy-start(s32[1,1,4]{2,1,0:T(1,128)} %param.12) | copy-start | bytes 52
  3.1 1.5 %collective-permute-start = (bf16[256,256]{1,0:T(8,128)(2,1)S(1)}, bf16[256,256]{1,0:T(8,128)(2,1)S(1)}, u32[]{:S(2)}, u32[]{:S(2)}) collective-permute-start(bf16[256,256]{1,0:T(8,128)(2,1)S(1)} %front.1.spec_ref), channel_id=1, source_target_pairs={{0,1},{1,0},{2,3},{3,2},{4,5},{5,4},{6,7},{7,6},{8,9},{9,8},{10,11... | collective-permute-start | bytes 393224 | tf_op jit(solution)/shard_map/ppermute | solution.py:268
  4.8 4.7 %collective-permute-start.2 = (bf16[128,256]{1,0:T(8,128)(2,1)S(1)}, bf16[128,256]{1,0:T(8,128)(2,1)S(1)}, u32[]{:S(2)}, u32[]{:S(2)}) collective-permute-start(bf16[128,256]{1,0:T(8,128)(2,1)S(1)} %get-tuple-element.17), channel_id=1, source_target_pairs={{0,1},{1,4},{2,3},{3,6},{4,5},{5,0},{6,7},{7,2},{8,9},{9,12},{10,1... | collective-permute-start | bytes 196616 | tf_op jit(solution)/shard_map/ppermute | solution.py:315
  5.2 5.6 %collective-permute-start.3 = (bf16[128,256]{1,0:T(8,128)(2,1)S(1)}, bf16[128,256]{1,0:T(8,128)(2,1)S(1)}, u32[]{:S(2)}, u32[]{:S(2)}) collective-permute-start(bf16[128,256]{1,0:T(8,128)(2,1)S(1)} %get-tuple-element.18), channel_id=1, source_target_pairs={{0,1},{1,6},{2,3},{3,4},{4,5},{5,2},{6,7},{7,0},{8,9},{9,14},{10,1... | collective-permute-start | bytes 196616 | tf_op jit(solution)/shard_map/ppermute | solution.py:315
  7.8 3.9 %collective-permute-start.1 = (bf16[128,256]{1,0:T(8,128)(2,1)S(1)}, bf16[128,256]{1,0:T(8,128)(2,1)S(1)}, u32[]{:S(2)}, u32[]{:S(2)}) collective-permute-start(bf16[128,256]{1,0:T(8,128)(2,1)S(1)} %get-tuple-element.16), channel_id=1, source_target_pairs={{0,1},{1,2},{2,3},{3,0},{4,5},{5,6},{6,7},{7,4},{8,9},{9,10},{10,1... | collective-permute-start | bytes 196616 | tf_op jit(solution)/shard_map/ppermute | solution.py:315
  11.8 5.3 %collective-permute-start.6 = (bf16[128,256]{1,0:T(8,128)(2,1)S(1)}, bf16[128,256]{1,0:T(8,128)(2,1)S(1)}, u32[]{:S(2)}, u32[]{:S(2)}) collective-permute-start(bf16[128,256]{1,0:T(8,128)(2,1)S(1)} %add_convert_fusion.after_ref.sub_ref), channel_id=1, source_target_pairs={{0,9},{1,0},{2,11},{3,2},{4,13},{5,4},{6,15},{7,6},{8,17},{9,8},{1... | collective-permute-start | bytes 196616 | tf_op jit(solution)/shard_map/ppermute | solution.py:354
  12.2 5.0 %collective-permute-start.5 = (bf16[128,256]{1,0:T(8,128)(2,1)S(1)}, bf16[128,256]{1,0:T(8,128)(2,1)S(1)}, u32[]{:S(2)}, u32[]{:S(2)}) collective-permute-start(bf16[128,256]{1,0:T(8,128)(2,1)S(1)} %add_convert_fusion.after_ref.sub_ref), channel_id=1, source_target_pairs={{0,17},{1,0},{2,19},{3,2},{4,21},{5,4},{6,23},{7,6},{8,25},{9,8},{... | collective-permute-start | bytes 196616 | tf_op jit(solution)/shard_map/ppermute | solution.py:354
  14.5 3.0 %collective-permute-start.4 = (bf16[128,256]{1,0:T(8,128)(2,1)S(1)}, bf16[128,256]{1,0:T(8,128)(2,1)S(1)}, u32[]{:S(2)}, u32[]{:S(2)}) collective-permute-start(bf16[128,256]{1,0:T(8,128)(2,1)S(1)} %add_convert_fusion.after_ref.sub_ref), channel_id=1, source_target_pairs={{0,25},{1,0},{2,27},{3,2},{4,29},{5,4},{6,31},{7,6},{8,1},{9,8},{1... | collective-permute-start | bytes 196616 | tf_op jit(solution)/shard_map/ppermute | solution.py:354
  17.5 1.8 %collective-permute-start.7 = (bf16[192,256]{1,0:T(8,128)(2,1)S(1)}, bf16[192,256]{1,0:T(8,128)(2,1)S(1)}, u32[]{:S(2)}, u32[]{:S(2)}) collective-permute-start(bf16[192,256]{1,0:T(8,128)(2,1)S(1)} %maximum_select_fusion), channel_id=1, source_target_pairs={{0,1},{1,0},{2,3},{3,2},{4,5},{5,4},{6,7},{7,6},{8,9},{9,8},{10,11... | collective-permute-start | bytes 294920 | tf_op jit(solution)/shard_map/ppermute | solution.py:268

commit v6 on v5

--- a/solution.py
+++ b/solution.py
@@ -164,33 +164,34 @@
     )
 
 
-def term_kernel(scale, phase_ref, partial_ref, other_ref, *out_refs):
+def term_kernel(core, first, scale, phase_ref, partial_ref, other_ref, *out_refs):
     depth = other_ref.shape[0]
     height = out_refs[0].shape[0]
-
-    def write_terms(count):
-        rows = count * height
-        terms = partial_ref[:rows] + jnp.dot(
-            phase_ref[:rows, depth:], other_ref[...], preferred_element_type=jnp.float32
+    rows = slice(first * height, (first + len(out_refs)) * height)
+
+    @pl.when(lax.axis_index("facet") % 2 == core)
+    def _():
+        terms = partial_ref[rows] + jnp.dot(
+            phase_ref[rows, depth:], other_ref[...], preferred_element_type=jnp.float32
         )
         terms = (terms * scale).astype(jnp.bfloat16)
-        for k in range(count):
-            out_refs[k][...] = terms[k * height : (k + 1) * height]
-
-    core = lax.axis_index("facet") % 2
-
-    @pl.when(core == 0)
-    def _():
-        write_terms(1)
-
-    @pl.when(core == 1)
-    def _():
-        write_terms(len(out_refs))
+        for k, out_ref in enumerate(out_refs):
+            out_ref[...] = terms[k * height : (k + 1) * height]
 
 
 def weights_kernel(
-    bands, slot_ref, band_ref, offset_ref, weight_ref, pos_ref, after_ref, col_ref, row_ref, mix_ref, lane_ref, core_ref
+    bands, slot_hbm, band_hbm, offset_hbm, weight_hbm, pos_hbm, after_ref, col_ref, row_ref, mix_ref,
+    lane_ref, core_ref, slot_ref, band_ref, offset_ref, weight_ref, pos_ref, sems
 ):
+    pairs = [
+        (slot_hbm, slot_ref), (band_hbm, band_ref), (offset_hbm, offset_ref),
+        (weight_hbm, weight_ref), (pos_hbm, pos_ref),
+    ]
+    copies = [pltpu.make_async_copy(a, b, sems.at[i]) for i, (a, b) in enumerate(pairs)]
+    for copy in copies:
+        copy.start()
+    for copy in copies:
+        copy.wait()
     blocks, width, points = col_ref.shape
     factor = -1.0 / (2.0 * kernel_sigma * kernel_sigma)
     tile = 512
@@ -303,14 +304,18 @@
         compiler_params=pltpu.CompilerParams(vmem_limit_bytes=32 * 2**20),
         name="phases",
     )(slot_of_subgrid.reshape(1, -1), spectrum)
-    terms = pl.pallas_call(
-        functools.partial(term_kernel, 1.0 / math.sqrt(sky_rows)),
-        out_shape=(term_shape,) * (chips - 1),
-        in_specs=[VMEM] * 3,
-        out_specs=(VMEM,) * (chips - 1),
-        compiler_params=pltpu.CompilerParams(vmem_limit_bytes=16 * 2**20),
-        name="terms",
-    )(phases, partial, other)
+    def make_terms(core, first, chip_count, name):
+        return pl.pallas_call(
+            functools.partial(term_kernel, core, first, 1.0 / math.sqrt(sky_rows)),
+            out_shape=(term_shape,) * chip_count,
+            in_specs=[VMEM] * 3,
+            out_specs=(VMEM,) * chip_count,
+            compiler_params=pltpu.CompilerParams(vmem_limit_bytes=16 * 2**20),
+            name=name,
+        )(phases, partial, other)
+
+    terms = [make_terms(1, k - 1, 1, "terms")[0] for k in range(1, chips)]
+    (own_terms,) = make_terms(0, 0, 1, "own_terms")
     arrived = [
         lax.ppermute(
             terms[k - 1],
@@ -322,8 +327,8 @@
         )
         for k in range(1, chips)
     ]
-    total = terms[0].astype(jnp.float32)
-    for part in arrived:
+    total = own_terms.astype(jnp.float32)
+    for part in [arrived[k - 1] for k in (2, 3, 1)]:
         total = total + part.astype(jnp.float32)
     chip_subs = total.astype(jnp.bfloat16)
 
@@ -336,16 +341,29 @@
             jax.ShapeDtypeStruct((blocks, 2 * CR, PC), jnp.int32),
             jax.ShapeDtypeStruct((8, SG), jnp.int32),
         ),
-        in_specs=[SMEM] * 4 + [VMEM] * 2,
+        in_specs=[HBM] * 5 + [VMEM],
         out_specs=(VMEM,) * 5,
+        scratch_shapes=[
+            pltpu.SMEM((blocks,), jnp.int32),
+            pltpu.SMEM((blocks,), jnp.int32),
+            pltpu.SMEM((blocks,), jnp.int32),
+            pltpu.SMEM((blocks,), jnp.float32),
+            pltpu.VMEM((blocks, 2, points), jnp.float32),
+            pltpu.SemaphoreType.DMA((5,)),
+        ],
         compiler_params=pltpu.CompilerParams(vmem_limit_bytes=16 * 2**20),
         cost_estimate=pl.CostEstimate(
             flops=8 * blocks * PC * points, bytes_accessed=0, transcendentals=blocks * PC * points
         ),
         name="weights",
     )(
-        block_slot.reshape(blocks), block_band.reshape(blocks), block_offset.reshape(blocks),
-        block_weight.reshape(blocks), vis_pos.reshape(blocks, 2, points),
+        *(
+            pltpu.with_memory_space_constraint(x, pltpu.HBM)
+            for x in (
+                block_slot.reshape(blocks), block_band.reshape(blocks), block_offset.reshape(blocks),
+                block_weight.reshape(blocks), vis_pos.reshape(blocks, 2, points),
+            )
+        ),
         chip_subs,
     )
 

time: 20.7 us -> 20.6 us (level)
  waiting for transfers between devices: 4.7 us -> 4.03 us
  starting transfers between devices: 9.42 us -> 9.75 us
  Pallas kernels: 5.51 us -> 5.78 us
    ppermute x3, waiting for transfers between devices: 2.78 us -> 2.4 us  [local(): lax.ppermute(terms[k - 1], 'facet', [(i, 2 * chip_to(k, i // 2, chips) if...]
    ppermute x3, starting transfers between devices: 4.16 us -> 4.51 us  [local(): lax.ppermute(terms[k - 1], 'facet', [(i, 2 * chip_to(k, i // 2, chips) if...]
    pallas_call x1, Pallas kernels: 1.43 us -> 1.75 us  [local(): pl.pallas_call(functools.partial(weights_kernel, band_count), out_shape=(...]
    ppermute x3, waiting for transfers between devices: 0.38 us -> 0.08 us  [local(): lax.ppermute(chip_subs, ('band', 'facet'), [(device(b, f), device(b, f -...]
  transfers between devices with their start and end apart: 8 -> 8, of which waited for: 6 -> 6; matrix products, arithmetic and copies ran while one was open for 0% -> 0% of each run, Pallas kernels for 9% -> 11%
where the time goes in v6:
time: 20.6 us; the launch traced here: 20.4 us
  starting transfers between devices  9.75 us (47%)
  Pallas kernels  5.78 us (28%)
  waiting for transfers between devices  4.03 us (20%)
  between operations  0.72 us (3%)
    ppermute x3, starting transfers between devices, local(): lax.ppermute(terms[k - 1], 'facet', [(i, 2 * chip_to(k, i // 2, chips) if...  4.51 us
    ppermute x3, starting transfers between devices, local(): lax.ppermute(chip_subs, ('band', 'facet'), [(device(b, f), device(b, f -...  3.84 us
    ppermute x3, waiting for transfers between devices, local(): lax.ppermute(terms[k - 1], 'facet', [(i, 2 * chip_to(k, i // 2, chips) if...  2.4 us
    pallas_call x1, Pallas kernels, local(): pl.pallas_call(functools.partial(front_kernel, chunks), out_shape=jax.Sha...  2.34 us
    pallas_call x1, Pallas kernels, local(): pl.pallas_call(functools.partial(weights_kernel, band_count), out_shape=(...  1.75 us
    ppermute x2, waiting for transfers between devices, swap(): return lax.ppermute(x, 'facet', [(i, i ^ 1) for i in range(facet_count)])  1.54 us
    ppermute x2, starting transfers between devices, swap(): return lax.ppermute(x, 'facet', [(i, i ^ 1) for i in range(facet_count)])  1.4 us
    pallas_call x1, Pallas kernels, local(): pl.pallas_call(functools.partial(degrid_kernel, band_count), out_shape=(j...  1.15 us
  transfers between devices with their start and end apart: 8, of which 6 were waited for; matrix products, arithmetic and copies ran while one was open for 0% of the time, Pallas kernels for 11%

profile of v6, /device:TPU:0, one launch (start us, length us, event | category | flops | bytes accessed | tf_op | source)
XLA Modules:
  0.0 20.4 jit_solution(12014355265875093133)
XLA Ops:
  0.6 0.0 copy-start
  0.6 2.3 %front.1.spec_ref = bf16[256,256]{1,0:T(8,128)(2,1)S(1)} custom-call(bf16[256,4096]{1,0:T(8,128)(2,1)} %bitcast.11, f32[1,4096]{1,0:T(1,128)} %bitcast.12, bf16[64,128]{1,0:T(8,128)(2,1)} %constant.4.clone.seed_hbm), custom_call_target="tpu_custom_call" | custom-call | tf_op jit(solution)/shard_map/front/pallas_call | solution.py:274
  3.0 0.5 %collective-permute-start = (bf16[256,256]{1,0:T(8,128)(2,1)S(1)}, bf16[256,256]{1,0:T(8,128)(2,1)S(1)}, u32[]{:S(2)}, u32[]{:S(2)}) collective-permute-start(bf16[256,256]{1,0:T(8,128)(2,1)S(1)} %front.1.spec_ref), channel_id=1, source_target_pairs={{0,1},{1,0},{2,3},{3,2},{4,5},{5,4},{6,7},{7,6},{8,9},{9,8},{10,11... | collective-permute-start | bytes 393224 | tf_op jit(solution)/shard_map/ppermute | solution.py:269
  3.5 0.0 copy-done
  3.5 0.4 %phases.1 = (bf16[384,512]{1,0:T(8,128)(2,1)S(1)}, f32[384,256]{1,0:T(8,128)S(1)}) custom-call(s32[1,12]{1,0:T(1,128)S(1)} %bitcast.10, bf16[256,256]{1,0:T(8,128)(2,1)S(1)} %front.1.spec_ref), custom_call_target="tpu_custom_call" | custom-call | tf_op jit(solution)/shard_map/phases/pallas_call | solution.py:296
  3.9 0.6 %collective-permute-done.other_ref = bf16[256,256]{1,0:T(8,128)(2,1)S(1)} collective-permute-done((bf16[256,256]{1,0:T(8,128)(2,1)S(1)}, bf16[256,256]{1,0:T(8,128)(2,1)S(1)}, u32[]{:S(2)}, u32[]{:S(2)}) %collective-permute-start) | collective-permute-done | bytes 131104 | tf_op jit(solution)/shard_map/ppermute | solution.py:269
  4.5 0.6 %collective-permute-start.1 = (bf16[128,256]{1,0:T(8,128)(2,1)S(1)}, bf16[128,256]{1,0:T(8,128)(2,1)S(1)}, u32[]{:S(2)}, u32[]{:S(2)}) collective-permute-start(bf16[128,256]{1,0:T(8,128)(2,1)S(1)} %terms.3), channel_id=1, source_target_pairs={{0,1},{1,4},{2,3},{3,6},{4,5},{5,0},{6,7},{7,2},{8,9},{9,12},{10,1... | collective-permute-start | bytes 196616 | tf_op jit(solution)/shard_map/ppermute | solution.py:320
  5.1 2.6 %collective-permute-start.2 = (bf16[128,256]{1,0:T(8,128)(2,1)S(1)}, bf16[128,256]{1,0:T(8,128)(2,1)S(1)}, u32[]{:S(2)}, u32[]{:S(2)}) collective-permute-start(bf16[128,256]{1,0:T(8,128)(2,1)S(1)} %terms.4), channel_id=1, source_target_pairs={{0,1},{1,6},{2,3},{3,4},{4,5},{5,2},{6,7},{7,0},{8,9},{9,14},{10,1... | collective-permute-start | bytes 196616 | tf_op jit(solution)/shard_map/ppermute | solution.py:320
  7.7 1.3 %collective-permute-start.3 = (bf16[128,256]{1,0:T(8,128)(2,1)S(1)}, bf16[128,256]{1,0:T(8,128)(2,1)S(1)}, u32[]{:S(2)}, u32[]{:S(2)}) collective-permute-start(bf16[128,256]{1,0:T(8,128)(2,1)S(1)} %terms.5), channel_id=1, source_target_pairs={{0,1},{1,2},{2,3},{3,0},{4,5},{5,6},{6,7},{7,4},{8,9},{9,10},{10,1... | collective-permute-start | bytes 196616 | tf_op jit(solution)/shard_map/ppermute | solution.py:320
  9.0 0.2 own_terms.1
  9.2 0.1 collective-permute-done.1
  9.3 1.4 %collective-permute-done.2 = bf16[128,256]{1,0:T(8,128)(2,1)S(1)} collective-permute-done((bf16[128,256]{1,0:T(8,128)(2,1)S(1)}, bf16[128,256]{1,0:T(8,128)(2,1)S(1)}, u32[]{:S(2)}, u32[]{:S(2)}) %collective-permute-start.2) | collective-permute-done | bytes 65568 | tf_op jit(solution)/shard_map/ppermute | solution.py:320
  10.7 0.9 %collective-permute-done.3 = bf16[128,256]{1,0:T(8,128)(2,1)S(1)} collective-permute-done((bf16[128,256]{1,0:T(8,128)(2,1)S(1)}, bf16[128,256]{1,0:T(8,128)(2,1)S(1)}, u32[]{:S(2)}, u32[]{:S(2)}) %collective-permute-start.3) | collective-permute-done | bytes 65568 | tf_op jit(solution)/shard_map/ppermute | solution.py:320
  11.6 0.4 %collective-permute-start.6 = (bf16[128,256]{1,0:T(8,128)(2,1)S(1)}, bf16[128,256]{1,0:T(8,128)(2,1)S(1)}, u32[]{:S(2)}, u32[]{:S(2)}) collective-permute-start(bf16[128,256]{1,0:T(8,128)(2,1)S(1)} %add_convert_fusion.after_ref.sub_ref), channel_id=1, source_target_pairs={{0,9},{1,0},{2,11},{3,2},{4,13},{5,4},{6,15},{7,6},{8,17},{9,8},{1... | collective-permute-start | bytes 196616 | tf_op jit(solution)/shard_map/ppermute | solution.py:372
  12.0 2.4 %collective-permute-start.5 = (bf16[128,256]{1,0:T(8,128)(2,1)S(1)}, bf16[128,256]{1,0:T(8,128)(2,1)S(1)}, u32[]{:S(2)}, u32[]{:S(2)}) collective-permute-start(bf16[128,256]{1,0:T(8,128)(2,1)S(1)} %add_convert_fusion.after_ref.sub_ref), channel_id=1, source_target_pairs={{0,17},{1,0},{2,19},{3,2},{4,21},{5,4},{6,23},{7,6},{8,25},{9,8},{... | collective-permute-start | bytes 196616 | tf_op jit(solution)/shard_map/ppermute | solution.py:372
  14.4 1.1 %collective-permute-start.4 = (bf16[128,256]{1,0:T(8,128)(2,1)S(1)}, bf16[128,256]{1,0:T(8,128)(2,1)S(1)}, u32[]{:S(2)}, u32[]{:S(2)}) collective-permute-start(bf16[128,256]{1,0:T(8,128)(2,1)S(1)} %add_convert_fusion.after_ref.sub_ref), channel_id=1, source_target_pairs={{0,25},{1,0},{2,27},{3,2},{4,29},{5,4},{6,31},{7,6},{8,1},{9,8},{1... | collective-permute-start | bytes 196616 | tf_op jit(solution)/shard_map/ppermute | solution.py:372
  15.5 1.8 %weights.1 = (bf16[4,128,2048]{2,1,0:T(8,128)(2,1)S(1)}, f32[4,16,2048]{2,1,0:T(8,128)S(1)}, f32[4,8,8,128]{3,2,1,0:T(8,128)S(1)}, s32[4,32,128]{2,1,0:T(8,128)S(1)}, s32[8,256]{1,0:T(8,128)S(1)}) custom-call(s32[4]{0:T(128)} %bitcast.16, s32[4]{0:T(128)} %bitcast.17, s32[4]{0:T(128)} %bitcast.18, f32[4]{0:T(128)} %bitcast.19, f32[4,2,2048]{2,1,0:T(2,128)} %bitcast.13, ...), custom_call_target="tpu_custom_call" | custom-call | flops 8388608 | tf_op jit(solution)/shard_map/weights/pallas_call | solution.py:335
  17.2 0.0 collective-permute-done.6.refs_2_
  17.3 0.0 collective-permute-done.5.refs_1_
  17.3 0.1 collective-permute-done.4.refs_0_
  17.4 0.9 %collective-permute-start.7 = (bf16[192,256]{1,0:T(8,128)(2,1)S(1)}, bf16[192,256]{1,0:T(8,128)(2,1)S(1)}, u32[]{:S(2)}, u32[]{:S(2)}) collective-permute-start(bf16[192,256]{1,0:T(8,128)(2,1)S(1)} %maximum_select_fusion), channel_id=1, source_target_pairs={{0,1},{1,0},{2,3},{3,2},{4,5},{5,4},{6,7},{7,6},{8,9},{9,8},{10,11... | collective-permute-start | bytes 294920 | tf_op jit(solution)/shard_map/ppermute | solution.py:269
  18.3 0.9 %collective-permute-done.7.swap_ref = bf16[192,256]{1,0:T(8,128)(2,1)S(1)} collective-permute-done((bf16[192,256]{1,0:T(8,128)(2,1)S(1)}, bf16[192,256]{1,0:T(8,128)(2,1)S(1)}, u32[]{:S(2)}, u32[]{:S(2)}) %collective-permute-start.7) | collective-permute-done | bytes 98336 | tf_op jit(solution)/shard_map/ppermute | solution.py:269
  19.2 1.2 %degrid.1 = (bf16[64,256]{1,0:T(8,128)(2,1)}, f32[4,2,2048]{2,1,0:T(2,128)}) custom-call(f32[4,8,8,128]{3,2,1,0:T(8,128)S(1)} %get-tuple-element.13.mix_ref, s32[4,32,128]{2,1,0:T(8,128)S(1)} %get-tuple-element.14.lane_ref, bf16[4,128,2048]{2,1,0:T(8,128)(2,1)S(1)} %get-tuple-element.15.col_ref, f32[4,16,2048]{2,1,0:T(8,128)S(1)} %get-tuple-element.16.row_ref, ...), custom_call_target="tpu_custom_call" | custom-call | tf_op jit(solution)/shard_map/degrid/pallas_call | solution.py:389
  (10 shorter events, 0.1 us)
Async XLA Ops:
  0.6 2.9 %copy-start = (s32[12]{0:T(128)S(1)}, s32[12]{0:T(128)}, u32[]{:S(2)}) copy-start(s32[12]{0:T(128)} %param.11) | copy-start | bytes 148
  3.0 1.5 %collective-permute-start = (bf16[256,256]{1,0:T(8,128)(2,1)S(1)}, bf16[256,256]{1,0:T(8,128)(2,1)S(1)}, u32[]{:S(2)}, u32[]{:S(2)}) collective-permute-start(bf16[256,256]{1,0:T(8,128)(2,1)S(1)} %front.1.spec_ref), channel_id=1, source_target_pairs={{0,1},{1,0},{2,3},{3,2},{4,5},{5,4},{6,7},{7,6},{8,9},{9,8},{10,11... | collective-permute-start | bytes 393224 | tf_op jit(solution)/shard_map/ppermute | solution.py:269
  4.5 4.8 %collective-permute-start.1 = (bf16[128,256]{1,0:T(8,128)(2,1)S(1)}, bf16[128,256]{1,0:T(8,128)(2,1)S(1)}, u32[]{:S(2)}, u32[]{:S(2)}) collective-permute-start(bf16[128,256]{1,0:T(8,128)(2,1)S(1)} %terms.3), channel_id=1, source_target_pairs={{0,1},{1,4},{2,3},{3,6},{4,5},{5,0},{6,7},{7,2},{8,9},{9,12},{10,1... | collective-permute-start | bytes 196616 | tf_op jit(solution)/shard_map/ppermute | solution.py:320
  5.1 5.6 %collective-permute-start.2 = (bf16[128,256]{1,0:T(8,128)(2,1)S(1)}, bf16[128,256]{1,0:T(8,128)(2,1)S(1)}, u32[]{:S(2)}, u32[]{:S(2)}) collective-permute-start(bf16[128,256]{1,0:T(8,128)(2,1)S(1)} %terms.4), channel_id=1, source_target_pairs={{0,1},{1,6},{2,3},{3,4},{4,5},{5,2},{6,7},{7,0},{8,9},{9,14},{10,1... | collective-permute-start | bytes 196616 | tf_op jit(solution)/shard_map/ppermute | solution.py:320
  7.7 3.9 %collective-permute-start.3 = (bf16[128,256]{1,0:T(8,128)(2,1)S(1)}, bf16[128,256]{1,0:T(8,128)(2,1)S(1)}, u32[]{:S(2)}, u32[]{:S(2)}) collective-permute-start(bf16[128,256]{1,0:T(8,128)(2,1)S(1)} %terms.5), channel_id=1, source_target_pairs={{0,1},{1,2},{2,3},{3,0},{4,5},{5,6},{6,7},{7,4},{8,9},{9,10},{10,1... | collective-permute-start | bytes 196616 | tf_op jit(solution)/shard_map/ppermute | solution.py:320
  11.6 5.6 %collective-permute-start.6 = (bf16[128,256]{1,0:T(8,128)(2,1)S(1)}, bf16[128,256]{1,0:T(8,128)(2,1)S(1)}, u32[]{:S(2)}, u32[]{:S(2)}) collective-permute-start(bf16[128,256]{1,0:T(8,128)(2,1)S(1)} %add_convert_fusion.after_ref.sub_ref), channel_id=1, source_target_pairs={{0,9},{1,0},{2,11},{3,2},{4,13},{5,4},{6,15},{7,6},{8,17},{9,8},{1... | collective-permute-start | bytes 196616 | tf_op jit(solution)/shard_map/ppermute | solution.py:372
  12.0 5.3 %collective-permute-start.5 = (bf16[128,256]{1,0:T(8,128)(2,1)S(1)}, bf16[128,256]{1,0:T(8,128)(2,1)S(1)}, u32[]{:S(2)}, u32[]{:S(2)}) collective-permute-start(bf16[128,256]{1,0:T(8,128)(2,1)S(1)} %add_convert_fusion.after_ref.sub_ref), channel_id=1, source_target_pairs={{0,17},{1,0},{2,19},{3,2},{4,21},{5,4},{6,23},{7,6},{8,25},{9,8},{... | collective-permute-start | bytes 196616 | tf_op jit(solution)/shard_map/ppermute | solution.py:372
  14.4 3.0 %collective-permute-start.4 = (bf16[128,256]{1,0:T(8,128)(2,1)S(1)}, bf16[128,256]{1,0:T(8,128)(2,1)S(1)}, u32[]{:S(2)}, u32[]{:S(2)}) collective-permute-start(bf16[128,256]{1,0:T(8,128)(2,1)S(1)} %add_convert_fusion.after_ref.sub_ref), channel_id=1, source_target_pairs={{0,25},{1,0},{2,27},{3,2},{4,29},{5,4},{6,31},{7,6},{8,1},{9,8},{1... | collective-permute-start | bytes 196616 | tf_op jit(solution)/shard_map/ppermute | solution.py:372
  17.4 1.8 %collective-permute-start.7 = (bf16[192,256]{1,0:T(8,128)(2,1)S(1)}, bf16[192,256]{1,0:T(8,128)(2,1)S(1)}, u32[]{:S(2)}, u32[]{:S(2)}) collective-permute-start(bf16[192,256]{1,0:T(8,128)(2,1)S(1)} %maximum_select_fusion), channel_id=1, source_target_pairs={{0,1},{1,0},{2,3},{3,2},{4,5},{5,4},{6,7},{7,6},{8,9},{9,8},{10,11... | collective-permute-start | bytes 294920 | tf_op jit(solution)/shard_map/ppermute | solution.py:269

commit v7 on v6

--- a/solution.py
+++ b/solution.py
@@ -328,7 +328,7 @@
         for k in range(1, chips)
     ]
     total = own_terms.astype(jnp.float32)
-    for part in [arrived[k - 1] for k in (2, 3, 1)]:
+    for part in arrived[1:] + arrived[:1]:
         total = total + part.astype(jnp.float32)
     chip_subs = total.astype(jnp.bfloat16)
 

time: 20.6 us -> 20.6 us (level)
  no operation moved by 1% of the time
where the time goes in v7:
time: 20.6 us; the launch traced here: 20.4 us
  starting transfers between devices  9.75 us (47%)
  Pallas kernels  5.78 us (28%)
  waiting for transfers between devices  4.03 us (20%)
  between operations  0.72 us (3%)
    ppermute x3, starting transfers between devices, local(): lax.ppermute(terms[k - 1], 'facet', [(i, 2 * chip_to(k, i // 2, chips) if...  4.51 us
    ppermute x3, starting transfers between devices, local(): lax.ppermute(chip_subs, ('band', 'facet'), [(device(b, f), device(b, f -...  3.84 us
    ppermute x3, waiting for transfers between devices, local(): lax.ppermute(terms[k - 1], 'facet', [(i, 2 * chip_to(k, i // 2, chips) if...  2.4 us
    pallas_call x1, Pallas kernels, local(): pl.pallas_call(functools.partial(front_kernel, chunks), out_shape=jax.Sha...  2.34 us
    pallas_call x1, Pallas kernels, local(): pl.pallas_call(functools.partial(weights_kernel, band_count), out_shape=(...  1.75 us
    ppermute x2, waiting for transfers between devices, swap(): return lax.ppermute(x, 'facet', [(i, i ^ 1) for i in range(facet_count)])  1.54 us
    ppermute x2, starting transfers between devices, swap(): return lax.ppermute(x, 'facet', [(i, i ^ 1) for i in range(facet_count)])  1.4 us
    pallas_call x1, Pallas kernels, local(): pl.pallas_call(functools.partial(degrid_kernel, band_count), out_shape=(j...  1.15 us
  transfers between devices with their start and end apart: 8, of which 6 were waited for; matrix products, arithmetic and copies ran while one was open for 0% of the time, Pallas kernels for 11%

profile of v7, /device:TPU:0, one launch (start us, length us, event | category | flops | bytes accessed | tf_op | source)
XLA Modules:
  0.0 20.4 jit_solution(12014355265875093133)
XLA Ops:
  0.6 0.0 copy-start
  0.6 2.3 %front.1.spec_ref = bf16[256,256]{1,0:T(8,128)(2,1)S(1)} custom-call(bf16[256,4096]{1,0:T(8,128)(2,1)} %bitcast.11, f32[1,4096]{1,0:T(1,128)} %bitcast.12, bf16[64,128]{1,0:T(8,128)(2,1)} %constant.4.clone.seed_hbm), custom_call_target="tpu_custom_call" | custom-call | tf_op jit(solution)/shard_map/front/pallas_call | solution.py:274
  3.0 0.5 %collective-permute-start = (bf16[256,256]{1,0:T(8,128)(2,1)S(1)}, bf16[256,256]{1,0:T(8,128)(2,1)S(1)}, u32[]{:S(2)}, u32[]{:S(2)}) collective-permute-start(bf16[256,256]{1,0:T(8,128)(2,1)S(1)} %front.1.spec_ref), channel_id=1, source_target_pairs={{0,1},{1,0},{2,3},{3,2},{4,5},{5,4},{6,7},{7,6},{8,9},{9,8},{10,11... | collective-permute-start | bytes 393224 | tf_op jit(solution)/shard_map/ppermute | solution.py:269
  3.5 0.0 copy-done
  3.5 0.4 %phases.1 = (bf16[384,512]{1,0:T(8,128)(2,1)S(1)}, f32[384,256]{1,0:T(8,128)S(1)}) custom-call(s32[1,12]{1,0:T(1,128)S(1)} %bitcast.10, bf16[256,256]{1,0:T(8,128)(2,1)S(1)} %front.1.spec_ref), custom_call_target="tpu_custom_call" | custom-call | tf_op jit(solution)/shard_map/phases/pallas_call | solution.py:296
  3.9 0.6 %collective-permute-done.other_ref = bf16[256,256]{1,0:T(8,128)(2,1)S(1)} collective-permute-done((bf16[256,256]{1,0:T(8,128)(2,1)S(1)}, bf16[256,256]{1,0:T(8,128)(2,1)S(1)}, u32[]{:S(2)}, u32[]{:S(2)}) %collective-permute-start) | collective-permute-done | bytes 131104 | tf_op jit(solution)/shard_map/ppermute | solution.py:269
  4.5 0.6 %collective-permute-start.1 = (bf16[128,256]{1,0:T(8,128)(2,1)S(1)}, bf16[128,256]{1,0:T(8,128)(2,1)S(1)}, u32[]{:S(2)}, u32[]{:S(2)}) collective-permute-start(bf16[128,256]{1,0:T(8,128)(2,1)S(1)} %terms.3), channel_id=1, source_target_pairs={{0,1},{1,4},{2,3},{3,6},{4,5},{5,0},{6,7},{7,2},{8,9},{9,12},{10,1... | collective-permute-start | bytes 196616 | tf_op jit(solution)/shard_map/ppermute | solution.py:320
  5.1 2.6 %collective-permute-start.2 = (bf16[128,256]{1,0:T(8,128)(2,1)S(1)}, bf16[128,256]{1,0:T(8,128)(2,1)S(1)}, u32[]{:S(2)}, u32[]{:S(2)}) collective-permute-start(bf16[128,256]{1,0:T(8,128)(2,1)S(1)} %terms.4), channel_id=1, source_target_pairs={{0,1},{1,6},{2,3},{3,4},{4,5},{5,2},{6,7},{7,0},{8,9},{9,14},{10,1... | collective-permute-start | bytes 196616 | tf_op jit(solution)/shard_map/ppermute | solution.py:320
  7.7 1.3 %collective-permute-start.3 = (bf16[128,256]{1,0:T(8,128)(2,1)S(1)}, bf16[128,256]{1,0:T(8,128)(2,1)S(1)}, u32[]{:S(2)}, u32[]{:S(2)}) collective-permute-start(bf16[128,256]{1,0:T(8,128)(2,1)S(1)} %terms.5), channel_id=1, source_target_pairs={{0,1},{1,2},{2,3},{3,0},{4,5},{5,6},{6,7},{7,4},{8,9},{9,10},{10,1... | collective-permute-start | bytes 196616 | tf_op jit(solution)/shard_map/ppermute | solution.py:320
  9.0 0.2 own_terms.1
  9.2 0.1 collective-permute-done.1
  9.3 1.4 %collective-permute-done.2 = bf16[128,256]{1,0:T(8,128)(2,1)S(1)} collective-permute-done((bf16[128,256]{1,0:T(8,128)(2,1)S(1)}, bf16[128,256]{1,0:T(8,128)(2,1)S(1)}, u32[]{:S(2)}, u32[]{:S(2)}) %collective-permute-start.2) | collective-permute-done | bytes 65568 | tf_op jit(solution)/shard_map/ppermute | solution.py:320
  10.7 0.9 %collective-permute-done.3 = bf16[128,256]{1,0:T(8,128)(2,1)S(1)} collective-permute-done((bf16[128,256]{1,0:T(8,128)(2,1)S(1)}, bf16[128,256]{1,0:T(8,128)(2,1)S(1)}, u32[]{:S(2)}, u32[]{:S(2)}) %collective-permute-start.3) | collective-permute-done | bytes 65568 | tf_op jit(solution)/shard_map/ppermute | solution.py:320
  11.6 0.4 %collective-permute-start.6 = (bf16[128,256]{1,0:T(8,128)(2,1)S(1)}, bf16[128,256]{1,0:T(8,128)(2,1)S(1)}, u32[]{:S(2)}, u32[]{:S(2)}) collective-permute-start(bf16[128,256]{1,0:T(8,128)(2,1)S(1)} %add_convert_fusion.after_ref.sub_ref), channel_id=1, source_target_pairs={{0,9},{1,0},{2,11},{3,2},{4,13},{5,4},{6,15},{7,6},{8,17},{9,8},{1... | collective-permute-start | bytes 196616 | tf_op jit(solution)/shard_map/ppermute | solution.py:372
  12.0 2.4 %collective-permute-start.5 = (bf16[128,256]{1,0:T(8,128)(2,1)S(1)}, bf16[128,256]{1,0:T(8,128)(2,1)S(1)}, u32[]{:S(2)}, u32[]{:S(2)}) collective-permute-start(bf16[128,256]{1,0:T(8,128)(2,1)S(1)} %add_convert_fusion.after_ref.sub_ref), channel_id=1, source_target_pairs={{0,17},{1,0},{2,19},{3,2},{4,21},{5,4},{6,23},{7,6},{8,25},{9,8},{... | collective-permute-start | bytes 196616 | tf_op jit(solution)/shard_map/ppermute | solution.py:372
  14.4 1.1 %collective-permute-start.4 = (bf16[128,256]{1,0:T(8,128)(2,1)S(1)}, bf16[128,256]{1,0:T(8,128)(2,1)S(1)}, u32[]{:S(2)}, u32[]{:S(2)}) collective-permute-start(bf16[128,256]{1,0:T(8,128)(2,1)S(1)} %add_convert_fusion.after_ref.sub_ref), channel_id=1, source_target_pairs={{0,25},{1,0},{2,27},{3,2},{4,29},{5,4},{6,31},{7,6},{8,1},{9,8},{1... | collective-permute-start | bytes 196616 | tf_op jit(solution)/shard_map/ppermute | solution.py:372
  15.5 1.8 %weights.1 = (bf16[4,128,2048]{2,1,0:T(8,128)(2,1)S(1)}, f32[4,16,2048]{2,1,0:T(8,128)S(1)}, f32[4,8,8,128]{3,2,1,0:T(8,128)S(1)}, s32[4,32,128]{2,1,0:T(8,128)S(1)}, s32[8,256]{1,0:T(8,128)S(1)}) custom-call(s32[4]{0:T(128)} %bitcast.16, s32[4]{0:T(128)} %bitcast.17, s32[4]{0:T(128)} %bitcast.18, f32[4]{0:T(128)} %bitcast.19, f32[4,2,2048]{2,1,0:T(2,128)} %bitcast.13, ...), custom_call_target="tpu_custom_call" | custom-call | flops 8388608 | tf_op jit(solution)/shard_map/weights/pallas_call | solution.py:335
  17.2 0.0 collective-permute-done.6.refs_2_
  17.3 0.0 collective-permute-done.5.refs_1_
  17.3 0.1 collective-permute-done.4.refs_0_
  17.4 0.9 %collective-permute-start.7 = (bf16[192,256]{1,0:T(8,128)(2,1)S(1)}, bf16[192,256]{1,0:T(8,128)(2,1)S(1)}, u32[]{:S(2)}, u32[]{:S(2)}) collective-permute-start(bf16[192,256]{1,0:T(8,128)(2,1)S(1)} %maximum_select_fusion), channel_id=1, source_target_pairs={{0,1},{1,0},{2,3},{3,2},{4,5},{5,4},{6,7},{7,6},{8,9},{9,8},{10,11... | collective-permute-start | bytes 294920 | tf_op jit(solution)/shard_map/ppermute | solution.py:269
  18.3 0.9 %collective-permute-done.7.swap_ref = bf16[192,256]{1,0:T(8,128)(2,1)S(1)} collective-permute-done((bf16[192,256]{1,0:T(8,128)(2,1)S(1)}, bf16[192,256]{1,0:T(8,128)(2,1)S(1)}, u32[]{:S(2)}, u32[]{:S(2)}) %collective-permute-start.7) | collective-permute-done | bytes 98336 | tf_op jit(solution)/shard_map/ppermute | solution.py:269
  19.2 1.2 %degrid.1 = (bf16[64,256]{1,0:T(8,128)(2,1)}, f32[4,2,2048]{2,1,0:T(2,128)}) custom-call(f32[4,8,8,128]{3,2,1,0:T(8,128)S(1)} %get-tuple-element.13.mix_ref, s32[4,32,128]{2,1,0:T(8,128)S(1)} %get-tuple-element.14.lane_ref, bf16[4,128,2048]{2,1,0:T(8,128)(2,1)S(1)} %get-tuple-element.15.col_ref, f32[4,16,2048]{2,1,0:T(8,128)S(1)} %get-tuple-element.16.row_ref, ...), custom_call_target="tpu_custom_call" | custom-call | tf_op jit(solution)/shard_map/degrid/pallas_call | solution.py:389
  (10 shorter events, 0.1 us)
Async XLA Ops:
  0.6 2.9 %copy-start = (s32[12]{0:T(128)S(1)}, s32[12]{0:T(128)}, u32[]{:S(2)}) copy-start(s32[12]{0:T(128)} %param.11) | copy-start | bytes 148
  3.0 1.5 %collective-permute-start = (bf16[256,256]{1,0:T(8,128)(2,1)S(1)}, bf16[256,256]{1,0:T(8,128)(2,1)S(1)}, u32[]{:S(2)}, u32[]{:S(2)}) collective-permute-start(bf16[256,256]{1,0:T(8,128)(2,1)S(1)} %front.1.spec_ref), channel_id=1, source_target_pairs={{0,1},{1,0},{2,3},{3,2},{4,5},{5,4},{6,7},{7,6},{8,9},{9,8},{10,11... | collective-permute-start | bytes 393224 | tf_op jit(solution)/shard_map/ppermute | solution.py:269
  4.5 4.8 %collective-permute-start.1 = (bf16[128,256]{1,0:T(8,128)(2,1)S(1)}, bf16[128,256]{1,0:T(8,128)(2,1)S(1)}, u32[]{:S(2)}, u32[]{:S(2)}) collective-permute-start(bf16[128,256]{1,0:T(8,128)(2,1)S(1)} %terms.3), channel_id=1, source_target_pairs={{0,1},{1,4},{2,3},{3,6},{4,5},{5,0},{6,7},{7,2},{8,9},{9,12},{10,1... | collective-permute-start | bytes 196616 | tf_op jit(solution)/shard_map/ppermute | solution.py:320
  5.1 5.6 %collective-permute-start.2 = (bf16[128,256]{1,0:T(8,128)(2,1)S(1)}, bf16[128,256]{1,0:T(8,128)(2,1)S(1)}, u32[]{:S(2)}, u32[]{:S(2)}) collective-permute-start(bf16[128,256]{1,0:T(8,128)(2,1)S(1)} %terms.4), channel_id=1, source_target_pairs={{0,1},{1,6},{2,3},{3,4},{4,5},{5,2},{6,7},{7,0},{8,9},{9,14},{10,1... | collective-permute-start | bytes 196616 | tf_op jit(solution)/shard_map/ppermute | solution.py:320
  7.7 3.9 %collective-permute-start.3 = (bf16[128,256]{1,0:T(8,128)(2,1)S(1)}, bf16[128,256]{1,0:T(8,128)(2,1)S(1)}, u32[]{:S(2)}, u32[]{:S(2)}) collective-permute-start(bf16[128,256]{1,0:T(8,128)(2,1)S(1)} %terms.5), channel_id=1, source_target_pairs={{0,1},{1,2},{2,3},{3,0},{4,5},{5,6},{6,7},{7,4},{8,9},{9,10},{10,1... | collective-permute-start | bytes 196616 | tf_op jit(solution)/shard_map/ppermute | solution.py:320
  11.6 5.6 %collective-permute-start.6 = (bf16[128,256]{1,0:T(8,128)(2,1)S(1)}, bf16[128,256]{1,0:T(8,128)(2,1)S(1)}, u32[]{:S(2)}, u32[]{:S(2)}) collective-permute-start(bf16[128,256]{1,0:T(8,128)(2,1)S(1)} %add_convert_fusion.after_ref.sub_ref), channel_id=1, source_target_pairs={{0,9},{1,0},{2,11},{3,2},{4,13},{5,4},{6,15},{7,6},{8,17},{9,8},{1... | collective-permute-start | bytes 196616 | tf_op jit(solution)/shard_map/ppermute | solution.py:372
  12.0 5.3 %collective-permute-start.5 = (bf16[128,256]{1,0:T(8,128)(2,1)S(1)}, bf16[128,256]{1,0:T(8,128)(2,1)S(1)}, u32[]{:S(2)}, u32[]{:S(2)}) collective-permute-start(bf16[128,256]{1,0:T(8,128)(2,1)S(1)} %add_convert_fusion.after_ref.sub_ref), channel_id=1, source_target_pairs={{0,17},{1,0},{2,19},{3,2},{4,21},{5,4},{6,23},{7,6},{8,25},{9,8},{... | collective-permute-start | bytes 196616 | tf_op jit(solution)/shard_map/ppermute | solution.py:372
  14.4 3.0 %collective-permute-start.4 = (bf16[128,256]{1,0:T(8,128)(2,1)S(1)}, bf16[128,256]{1,0:T(8,128)(2,1)S(1)}, u32[]{:S(2)}, u32[]{:S(2)}) collective-permute-start(bf16[128,256]{1,0:T(8,128)(2,1)S(1)} %add_convert_fusion.after_ref.sub_ref), channel_id=1, source_target_pairs={{0,25},{1,0},{2,27},{3,2},{4,29},{5,4},{6,31},{7,6},{8,1},{9,8},{1... | collective-permute-start | bytes 196616 | tf_op jit(solution)/shard_map/ppermute | solution.py:372
  17.4 1.8 %collective-permute-start.7 = (bf16[192,256]{1,0:T(8,128)(2,1)S(1)}, bf16[192,256]{1,0:T(8,128)(2,1)S(1)}, u32[]{:S(2)}, u32[]{:S(2)}) collective-permute-start(bf16[192,256]{1,0:T(8,128)(2,1)S(1)} %maximum_select_fusion), channel_id=1, source_target_pairs={{0,1},{1,0},{2,3},{3,2},{4,5},{5,4},{6,7},{7,6},{8,9},{9,8},{10,11... | collective-permute-start | bytes 294920 | tf_op jit(solution)/shard_map/ppermute | solution.py:269

commit v8 on v7

--- a/solution.py
+++ b/solution.py
@@ -31,6 +31,10 @@
 
 def band_from(k, i, n):
     return (i - k + n) % n
+
+
+def band_order(n):
+    return list(range(n - 1, 2, -1)) + [k for k in (1, 2) if k < n]
 
 
 def column_seed(length, width):
@@ -225,8 +229,9 @@
     parts = [jnp.where(core == 0, sub_ref[:share_rows], swap_ref[:share_rows])]
     own_ref[...] = parts[0]
     for k in range(1, bands):
-        at = pl.ds((bands - 1 - k) * share_rows, share_rows)
-        parts.append(jnp.where(core == 0, swap_ref[at], band_refs[bands - 1 - k][share_rows:]))
+        place = band_order(bands).index(k)
+        at = pl.ds(place * share_rows, share_rows)
+        parts.append(jnp.where(core == 0, swap_ref[at], band_refs[place][share_rows:]))
     held = [
         part[c * height : (c + 1) * height].astype(jnp.float32) for part in parts for c in range(CAP)
     ]
@@ -378,8 +383,8 @@
                 for f in range(facet_count)
             ],
         )
-        for k in range(1, band_count)
-    ][::-1]
+        for k in band_order(band_count)
+    ]
     for_other = jnp.where(
         core_map[:1] == 0,
         jnp.concatenate([chip_subs[share_rows:]] * (band_count - 1)),

time: 20.6 us -> 20.5 us (level)
  no operation moved by 1% of the time
where the time goes in v8:
time: 20.5 us; the launch traced here: 20.3 us
  starting transfers between devices  9.68 us (47%)
  Pallas kernels  5.78 us (28%)
  waiting for transfers between devices  4.03 us (20%)
  between operations  0.72 us (4%)
    ppermute x3, starting transfers between devices, local(): lax.ppermute(terms[k - 1], 'facet', [(i, 2 * chip_to(k, i // 2, chips) if...  4.51 us
    ppermute x3, starting transfers between devices, local(): lax.ppermute(chip_subs, ('band', 'facet'), [(device(b, f), device(b, f -...  3.84 us
    ppermute x3, waiting for transfers between devices, local(): lax.ppermute(terms[k - 1], 'facet', [(i, 2 * chip_to(k, i // 2, chips) if...  2.4 us
    pallas_call x1, Pallas kernels, local(): pl.pallas_call(functools.partial(front_kernel, chunks), out_shape=jax.Sha...  2.34 us
    pallas_call x1, Pallas kernels, local(): pl.pallas_call(functools.partial(weights_kernel, band_count), out_shape=(...  1.75 us
    ppermute x2, waiting for transfers between devices, swap(): return lax.ppermute(x, 'facet', [(i, i ^ 1) for i in range(facet_count)])  1.54 us
    ppermute x2, starting transfers between devices, swap(): return lax.ppermute(x, 'facet', [(i, i ^ 1) for i in range(facet_count)])  1.33 us
    pallas_call x1, Pallas kernels, local(): pl.pallas_call(functools.partial(degrid_kernel, band_count), out_shape=(j...  1.15 us
  transfers between devices with their start and end apart: 8, of which 6 were waited for; matrix products, arithmetic and copies ran while one was open for 0% of the time, Pallas kernels for 11%

profile of v8, /device:TPU:0, one launch (start us, length us, event | category | flops | bytes accessed | tf_op | source)
XLA Modules:
  0.0 20.3 jit_solution(17463288387902351680)
XLA Ops:
  0.6 0.0 copy-start
  0.6 2.3 %front.1.spec_ref = bf16[256,256]{1,0:T(8,128)(2,1)S(1)} custom-call(bf16[256,4096]{1,0:T(8,128)(2,1)} %bitcast.11, f32[1,4096]{1,0:T(1,128)} %bitcast.12, bf16[64,128]{1,0:T(8,128)(2,1)} %constant.4.clone.seed_hbm), custom_call_target="tpu_custom_call" | custom-call | tf_op jit(solution)/shard_map/front/pallas_call | solution.py:279
  3.0 0.5 %collective-permute-start = (bf16[256,256]{1,0:T(8,128)(2,1)S(1)}, bf16[256,256]{1,0:T(8,128)(2,1)S(1)}, u32[]{:S(2)}, u32[]{:S(2)}) collective-permute-start(bf16[256,256]{1,0:T(8,128)(2,1)S(1)} %front.1.spec_ref), channel_id=1, source_target_pairs={{0,1},{1,0},{2,3},{3,2},{4,5},{5,4},{6,7},{7,6},{8,9},{9,8},{10,11... | collective-permute-start | bytes 393224 | tf_op jit(solution)/shard_map/ppermute | solution.py:274
  3.5 0.0 copy-done
  3.5 0.4 %phases.1 = (bf16[384,512]{1,0:T(8,128)(2,1)S(1)}, f32[384,256]{1,0:T(8,128)S(1)}) custom-call(s32[1,12]{1,0:T(1,128)S(1)} %bitcast.10, bf16[256,256]{1,0:T(8,128)(2,1)S(1)} %front.1.spec_ref), custom_call_target="tpu_custom_call" | custom-call | tf_op jit(solution)/shard_map/phases/pallas_call | solution.py:301
  3.9 0.6 %collective-permute-done.other_ref = bf16[256,256]{1,0:T(8,128)(2,1)S(1)} collective-permute-done((bf16[256,256]{1,0:T(8,128)(2,1)S(1)}, bf16[256,256]{1,0:T(8,128)(2,1)S(1)}, u32[]{:S(2)}, u32[]{:S(2)}) %collective-permute-start) | collective-permute-done | bytes 131104 | tf_op jit(solution)/shard_map/ppermute | solution.py:274
  4.5 0.6 %collective-permute-start.1 = (bf16[128,256]{1,0:T(8,128)(2,1)S(1)}, bf16[128,256]{1,0:T(8,128)(2,1)S(1)}, u32[]{:S(2)}, u32[]{:S(2)}) collective-permute-start(bf16[128,256]{1,0:T(8,128)(2,1)S(1)} %terms.3), channel_id=1, source_target_pairs={{0,1},{1,4},{2,3},{3,6},{4,5},{5,0},{6,7},{7,2},{8,9},{9,12},{10,1... | collective-permute-start | bytes 196616 | tf_op jit(solution)/shard_map/ppermute | solution.py:325
  5.1 2.6 %collective-permute-start.2 = (bf16[128,256]{1,0:T(8,128)(2,1)S(1)}, bf16[128,256]{1,0:T(8,128)(2,1)S(1)}, u32[]{:S(2)}, u32[]{:S(2)}) collective-permute-start(bf16[128,256]{1,0:T(8,128)(2,1)S(1)} %terms.4), channel_id=1, source_target_pairs={{0,1},{1,6},{2,3},{3,4},{4,5},{5,2},{6,7},{7,0},{8,9},{9,14},{10,1... | collective-permute-start | bytes 196616 | tf_op jit(solution)/shard_map/ppermute | solution.py:325
  7.7 1.3 %collective-permute-start.3 = (bf16[128,256]{1,0:T(8,128)(2,1)S(1)}, bf16[128,256]{1,0:T(8,128)(2,1)S(1)}, u32[]{:S(2)}, u32[]{:S(2)}) collective-permute-start(bf16[128,256]{1,0:T(8,128)(2,1)S(1)} %terms.5), channel_id=1, source_target_pairs={{0,1},{1,2},{2,3},{3,0},{4,5},{5,6},{6,7},{7,4},{8,9},{9,10},{10,1... | collective-permute-start | bytes 196616 | tf_op jit(solution)/shard_map/ppermute | solution.py:325
  9.0 0.2 own_terms.1
  9.2 0.1 collective-permute-done.1
  9.3 1.4 %collective-permute-done.2 = bf16[128,256]{1,0:T(8,128)(2,1)S(1)} collective-permute-done((bf16[128,256]{1,0:T(8,128)(2,1)S(1)}, bf16[128,256]{1,0:T(8,128)(2,1)S(1)}, u32[]{:S(2)}, u32[]{:S(2)}) %collective-permute-start.2) | collective-permute-done | bytes 65568 | tf_op jit(solution)/shard_map/ppermute | solution.py:325
  10.7 0.9 %collective-permute-done.3 = bf16[128,256]{1,0:T(8,128)(2,1)S(1)} collective-permute-done((bf16[128,256]{1,0:T(8,128)(2,1)S(1)}, bf16[128,256]{1,0:T(8,128)(2,1)S(1)}, u32[]{:S(2)}, u32[]{:S(2)}) %collective-permute-start.3) | collective-permute-done | bytes 65568 | tf_op jit(solution)/shard_map/ppermute | solution.py:325
  11.6 1.4 %collective-permute-start.6 = (bf16[128,256]{1,0:T(8,128)(2,1)S(1)}, bf16[128,256]{1,0:T(8,128)(2,1)S(1)}, u32[]{:S(2)}, u32[]{:S(2)}) collective-permute-start(bf16[128,256]{1,0:T(8,128)(2,1)S(1)} %add_convert_fusion.after_ref.sub_ref), channel_id=1, source_target_pairs={{0,17},{1,0},{2,19},{3,2},{4,21},{5,4},{6,23},{7,6},{8,25},{9,8},{... | collective-permute-start | bytes 196616 | tf_op jit(solution)/shard_map/ppermute | solution.py:377
  13.0 0.3 %collective-permute-start.5 = (bf16[128,256]{1,0:T(8,128)(2,1)S(1)}, bf16[128,256]{1,0:T(8,128)(2,1)S(1)}, u32[]{:S(2)}, u32[]{:S(2)}) collective-permute-start(bf16[128,256]{1,0:T(8,128)(2,1)S(1)} %add_convert_fusion.after_ref.sub_ref), channel_id=1, source_target_pairs={{0,9},{1,0},{2,11},{3,2},{4,13},{5,4},{6,15},{7,6},{8,17},{9,8},{1... | collective-permute-start | bytes 196616 | tf_op jit(solution)/shard_map/ppermute | solution.py:377
  13.4 2.1 %collective-permute-start.4 = (bf16[128,256]{1,0:T(8,128)(2,1)S(1)}, bf16[128,256]{1,0:T(8,128)(2,1)S(1)}, u32[]{:S(2)}, u32[]{:S(2)}) collective-permute-start(bf16[128,256]{1,0:T(8,128)(2,1)S(1)} %add_convert_fusion.after_ref.sub_ref), channel_id=1, source_target_pairs={{0,25},{1,0},{2,27},{3,2},{4,29},{5,4},{6,31},{7,6},{8,1},{9,8},{1... | collective-permute-start | bytes 196616 | tf_op jit(solution)/shard_map/ppermute | solution.py:377
  15.5 1.8 %weights.1 = (bf16[4,128,2048]{2,1,0:T(8,128)(2,1)S(1)}, f32[4,16,2048]{2,1,0:T(8,128)S(1)}, f32[4,8,8,128]{3,2,1,0:T(8,128)S(1)}, s32[4,32,128]{2,1,0:T(8,128)S(1)}, s32[8,256]{1,0:T(8,128)S(1)}) custom-call(s32[4]{0:T(128)} %bitcast.16, s32[4]{0:T(128)} %bitcast.17, s32[4]{0:T(128)} %bitcast.18, f32[4]{0:T(128)} %bitcast.19, f32[4,2,2048]{2,1,0:T(2,128)} %bitcast.13, ...), custom_call_target="tpu_custom_call" | custom-call | flops 8388608 | tf_op jit(solution)/shard_map/weights/pallas_call | solution.py:340
  17.2 0.0 collective-permute-done.6.refs_2_
  17.3 0.0 collective-permute-done.5.refs_1_
  17.3 0.1 collective-permute-done.4.refs_0_
  17.4 0.8 %collective-permute-start.7 = (bf16[192,256]{1,0:T(8,128)(2,1)S(1)}, bf16[192,256]{1,0:T(8,128)(2,1)S(1)}, u32[]{:S(2)}, u32[]{:S(2)}) collective-permute-start(bf16[192,256]{1,0:T(8,128)(2,1)S(1)} %maximum_select_fusion), channel_id=1, source_target_pairs={{0,1},{1,0},{2,3},{3,2},{4,5},{5,4},{6,7},{7,6},{8,9},{9,8},{10,11... | collective-permute-start | bytes 294920 | tf_op jit(solution)/shard_map/ppermute | solution.py:274
  18.2 0.9 %collective-permute-done.7.swap_ref = bf16[192,256]{1,0:T(8,128)(2,1)S(1)} collective-permute-done((bf16[192,256]{1,0:T(8,128)(2,1)S(1)}, bf16[192,256]{1,0:T(8,128)(2,1)S(1)}, u32[]{:S(2)}, u32[]{:S(2)}) %collective-permute-start.7) | collective-permute-done | bytes 98336 | tf_op jit(solution)/shard_map/ppermute | solution.py:274
  19.2 1.2 %degrid.1 = (bf16[64,256]{1,0:T(8,128)(2,1)}, f32[4,2,2048]{2,1,0:T(2,128)}) custom-call(f32[4,8,8,128]{3,2,1,0:T(8,128)S(1)} %get-tuple-element.13.mix_ref, s32[4,32,128]{2,1,0:T(8,128)S(1)} %get-tuple-element.14.lane_ref, bf16[4,128,2048]{2,1,0:T(8,128)(2,1)S(1)} %get-tuple-element.15.col_ref, f32[4,16,2048]{2,1,0:T(8,128)S(1)} %get-tuple-element.16.row_ref, ...), custom_call_target="tpu_custom_call" | custom-call | tf_op jit(solution)/shard_map/degrid/pallas_call | solution.py:394
  (10 shorter events, 0.1 us)
Async XLA Ops:
  0.6 2.9 %copy-start = (s32[12]{0:T(128)S(1)}, s32[12]{0:T(128)}, u32[]{:S(2)}) copy-start(s32[12]{0:T(128)} %param.11) | copy-start | bytes 148
  3.0 1.5 %collective-permute-start = (bf16[256,256]{1,0:T(8,128)(2,1)S(1)}, bf16[256,256]{1,0:T(8,128)(2,1)S(1)}, u32[]{:S(2)}, u32[]{:S(2)}) collective-permute-start(bf16[256,256]{1,0:T(8,128)(2,1)S(1)} %front.1.spec_ref), channel_id=1, source_target_pairs={{0,1},{1,0},{2,3},{3,2},{4,5},{5,4},{6,7},{7,6},{8,9},{9,8},{10,11... | collective-permute-start | bytes 393224 | tf_op jit(solution)/shard_map/ppermute | solution.py:274
  4.5 4.8 %collective-permute-start.1 = (bf16[128,256]{1,0:T(8,128)(2,1)S(1)}, bf16[128,256]{1,0:T(8,128)(2,1)S(1)}, u32[]{:S(2)}, u32[]{:S(2)}) collective-permute-start(bf16[128,256]{1,0:T(8,128)(2,1)S(1)} %terms.3), channel_id=1, source_target_pairs={{0,1},{1,4},{2,3},{3,6},{4,5},{5,0},{6,7},{7,2},{8,9},{9,12},{10,1... | collective-permute-start | bytes 196616 | tf_op jit(solution)/shard_map/ppermute | solution.py:325
  5.1 5.6 %collective-permute-start.2 = (bf16[128,256]{1,0:T(8,128)(2,1)S(1)}, bf16[128,256]{1,0:T(8,128)(2,1)S(1)}, u32[]{:S(2)}, u32[]{:S(2)}) collective-permute-start(bf16[128,256]{1,0:T(8,128)(2,1)S(1)} %terms.4), channel_id=1, source_target_pairs={{0,1},{1,6},{2,3},{3,4},{4,5},{5,2},{6,7},{7,0},{8,9},{9,14},{10,1... | collective-permute-start | bytes 196616 | tf_op jit(solution)/shard_map/ppermute | solution.py:325
  7.7 3.9 %collective-permute-start.3 = (bf16[128,256]{1,0:T(8,128)(2,1)S(1)}, bf16[128,256]{1,0:T(8,128)(2,1)S(1)}, u32[]{:S(2)}, u32[]{:S(2)}) collective-permute-start(bf16[128,256]{1,0:T(8,128)(2,1)S(1)} %terms.5), channel_id=1, source_target_pairs={{0,1},{1,2},{2,3},{3,0},{4,5},{5,6},{6,7},{7,4},{8,9},{9,10},{10,1... | collective-permute-start | bytes 196616 | tf_op jit(solution)/shard_map/ppermute | solution.py:325
  11.6 5.6 %collective-permute-start.6 = (bf16[128,256]{1,0:T(8,128)(2,1)S(1)}, bf16[128,256]{1,0:T(8,128)(2,1)S(1)}, u32[]{:S(2)}, u32[]{:S(2)}) collective-permute-start(bf16[128,256]{1,0:T(8,128)(2,1)S(1)} %add_convert_fusion.after_ref.sub_ref), channel_id=1, source_target_pairs={{0,17},{1,0},{2,19},{3,2},{4,21},{5,4},{6,23},{7,6},{8,25},{9,8},{... | collective-permute-start | bytes 196616 | tf_op jit(solution)/shard_map/ppermute | solution.py:377
  13.0 4.2 %collective-permute-start.5 = (bf16[128,256]{1,0:T(8,128)(2,1)S(1)}, bf16[128,256]{1,0:T(8,128)(2,1)S(1)}, u32[]{:S(2)}, u32[]{:S(2)}) collective-permute-start(bf16[128,256]{1,0:T(8,128)(2,1)S(1)} %add_convert_fusion.after_ref.sub_ref), channel_id=1, source_target_pairs={{0,9},{1,0},{2,11},{3,2},{4,13},{5,4},{6,15},{7,6},{8,17},{9,8},{1... | collective-permute-start | bytes 196616 | tf_op jit(solution)/shard_map/ppermute | solution.py:377
  13.4 4.0 %collective-permute-start.4 = (bf16[128,256]{1,0:T(8,128)(2,1)S(1)}, bf16[128,256]{1,0:T(8,128)(2,1)S(1)}, u32[]{:S(2)}, u32[]{:S(2)}) collective-permute-start(bf16[128,256]{1,0:T(8,128)(2,1)S(1)} %add_convert_fusion.after_ref.sub_ref), channel_id=1, source_target_pairs={{0,25},{1,0},{2,27},{3,2},{4,29},{5,4},{6,31},{7,6},{8,1},{9,8},{1... | collective-permute-start | bytes 196616 | tf_op jit(solution)/shard_map/ppermute | solution.py:377
  17.4 1.8 %collective-permute-start.7 = (bf16[192,256]{1,0:T(8,128)(2,1)S(1)}, bf16[192,256]{1,0:T(8,128)(2,1)S(1)}, u32[]{:S(2)}, u32[]{:S(2)}) collective-permute-start(bf16[192,256]{1,0:T(8,128)(2,1)S(1)} %maximum_select_fusion), channel_id=1, source_target_pairs={{0,1},{1,0},{2,3},{3,2},{4,5},{5,4},{6,7},{7,6},{8,9},{9,8},{10,11... | collective-permute-start | bytes 294920 | tf_op jit(solution)/shard_map/ppermute | solution.py:274

commit v9 on v7

--- a/solution.py
+++ b/solution.py
@@ -56,7 +56,6 @@
     seed_copy = pltpu.make_async_copy(seed_hbm, seed_ref, small_sems.at[0])
     window_copy = pltpu.make_async_copy(window_hbm, window_ref, small_sems.at[1])
     seed_copy.start()
-    window_copy.start()
     copies = []
     for i in range(chunks):
         cols = pl.ds(i * width, width)
@@ -68,6 +67,7 @@
     for group in copies:
         for copy in group:
             copy.start()
+    window_copy.start()
 
     seed_copy.wait()
     ratio = length // SG

time: 20.6 us -> 20.6 us (level)
  no operation moved by 1% of the time
where the time goes in v9:
time: 20.6 us; the launch traced here: 20.4 us
  starting transfers between devices  9.75 us (47%)
  Pallas kernels  5.77 us (28%)
  waiting for transfers between devices  4.03 us (20%)
  between operations  0.71 us (3%)
    ppermute x3, starting transfers between devices, local(): lax.ppermute(terms[k - 1], 'facet', [(i, 2 * chip_to(k, i // 2, chips) if...  4.5 us
    ppermute x3, starting transfers between devices, local(): lax.ppermute(chip_subs, ('band', 'facet'), [(device(b, f), device(b, f -...  3.84 us
    ppermute x3, waiting for transfers between devices, local(): lax.ppermute(terms[k - 1], 'facet', [(i, 2 * chip_to(k, i // 2, chips) if...  2.4 us
    pallas_call x1, Pallas kernels, local(): pl.pallas_call(functools.partial(front_kernel, chunks), out_shape=jax.Sha...  2.32 us
    pallas_call x1, Pallas kernels, local(): pl.pallas_call(functools.partial(weights_kernel, band_count), out_shape=(...  1.75 us
    ppermute x2, waiting for transfers between devices, swap(): return lax.ppermute(x, 'facet', [(i, i ^ 1) for i in range(facet_count)])  1.54 us
    ppermute x2, starting transfers between devices, swap(): return lax.ppermute(x, 'facet', [(i, i ^ 1) for i in range(facet_count)])  1.41 us
    pallas_call x1, Pallas kernels, local(): pl.pallas_call(functools.partial(degrid_kernel, band_count), out_shape=(j...  1.15 us
  transfers between devices with their start and end apart: 8, of which 6 were waited for; matrix products, arithmetic and copies ran while one was open for 0% of the time, Pallas kernels for 11%

profile of v9, /device:TPU:0, one launch (start us, length us, event | category | flops | bytes accessed | tf_op | source)
XLA Modules:
  0.0 20.4 jit_solution(13694332437736041666)
XLA Ops:
  0.6 0.0 copy-start
  0.6 2.3 %front.1.spec_ref = bf16[256,256]{1,0:T(8,128)(2,1)S(1)} custom-call(bf16[256,4096]{1,0:T(8,128)(2,1)} %bitcast.11, f32[1,4096]{1,0:T(1,128)} %bitcast.12, bf16[64,128]{1,0:T(8,128)(2,1)} %constant.4.clone.seed_hbm), custom_call_target="tpu_custom_call" | custom-call | tf_op jit(solution)/shard_map/front/pallas_call | solution.py:274
  3.0 0.5 %collective-permute-start = (bf16[256,256]{1,0:T(8,128)(2,1)S(1)}, bf16[256,256]{1,0:T(8,128)(2,1)S(1)}, u32[]{:S(2)}, u32[]{:S(2)}) collective-permute-start(bf16[256,256]{1,0:T(8,128)(2,1)S(1)} %front.1.spec_ref), channel_id=1, source_target_pairs={{0,1},{1,0},{2,3},{3,2},{4,5},{5,4},{6,7},{7,6},{8,9},{9,8},{10,11... | collective-permute-start | bytes 393224 | tf_op jit(solution)/shard_map/ppermute | solution.py:269
  3.5 0.0 copy-done
  3.5 0.4 %phases.1 = (bf16[384,512]{1,0:T(8,128)(2,1)S(1)}, f32[384,256]{1,0:T(8,128)S(1)}) custom-call(s32[1,12]{1,0:T(1,128)S(1)} %bitcast.10, bf16[256,256]{1,0:T(8,128)(2,1)S(1)} %front.1.spec_ref), custom_call_target="tpu_custom_call" | custom-call | tf_op jit(solution)/shard_map/phases/pallas_call | solution.py:296
  3.9 0.6 %collective-permute-done.other_ref = bf16[256,256]{1,0:T(8,128)(2,1)S(1)} collective-permute-done((bf16[256,256]{1,0:T(8,128)(2,1)S(1)}, bf16[256,256]{1,0:T(8,128)(2,1)S(1)}, u32[]{:S(2)}, u32[]{:S(2)}) %collective-permute-start) | collective-permute-done | bytes 131104 | tf_op jit(solution)/shard_map/ppermute | solution.py:269
  4.5 0.6 %collective-permute-start.1 = (bf16[128,256]{1,0:T(8,128)(2,1)S(1)}, bf16[128,256]{1,0:T(8,128)(2,1)S(1)}, u32[]{:S(2)}, u32[]{:S(2)}) collective-permute-start(bf16[128,256]{1,0:T(8,128)(2,1)S(1)} %terms.3), channel_id=1, source_target_pairs={{0,1},{1,4},{2,3},{3,6},{4,5},{5,0},{6,7},{7,2},{8,9},{9,12},{10,1... | collective-permute-start | bytes 196616 | tf_op jit(solution)/shard_map/ppermute | solution.py:320
  5.1 2.6 %collective-permute-start.2 = (bf16[128,256]{1,0:T(8,128)(2,1)S(1)}, bf16[128,256]{1,0:T(8,128)(2,1)S(1)}, u32[]{:S(2)}, u32[]{:S(2)}) collective-permute-start(bf16[128,256]{1,0:T(8,128)(2,1)S(1)} %terms.4), channel_id=1, source_target_pairs={{0,1},{1,6},{2,3},{3,4},{4,5},{5,2},{6,7},{7,0},{8,9},{9,14},{10,1... | collective-permute-start | bytes 196616 | tf_op jit(solution)/shard_map/ppermute | solution.py:320
  7.7 1.3 %collective-permute-start.3 = (bf16[128,256]{1,0:T(8,128)(2,1)S(1)}, bf16[128,256]{1,0:T(8,128)(2,1)S(1)}, u32[]{:S(2)}, u32[]{:S(2)}) collective-permute-start(bf16[128,256]{1,0:T(8,128)(2,1)S(1)} %terms.5), channel_id=1, source_target_pairs={{0,1},{1,2},{2,3},{3,0},{4,5},{5,6},{6,7},{7,4},{8,9},{9,10},{10,1... | collective-permute-start | bytes 196616 | tf_op jit(solution)/shard_map/ppermute | solution.py:320
  9.0 0.2 own_terms.1
  9.2 0.1 collective-permute-done.1
  9.3 1.4 %collective-permute-done.2 = bf16[128,256]{1,0:T(8,128)(2,1)S(1)} collective-permute-done((bf16[128,256]{1,0:T(8,128)(2,1)S(1)}, bf16[128,256]{1,0:T(8,128)(2,1)S(1)}, u32[]{:S(2)}, u32[]{:S(2)}) %collective-permute-start.2) | collective-permute-done | bytes 65568 | tf_op jit(solution)/shard_map/ppermute | solution.py:320
  10.7 0.9 %collective-permute-done.3 = bf16[128,256]{1,0:T(8,128)(2,1)S(1)} collective-permute-done((bf16[128,256]{1,0:T(8,128)(2,1)S(1)}, bf16[128,256]{1,0:T(8,128)(2,1)S(1)}, u32[]{:S(2)}, u32[]{:S(2)}) %collective-permute-start.3) | collective-permute-done | bytes 65568 | tf_op jit(solution)/shard_map/ppermute | solution.py:320
  11.6 0.4 %collective-permute-start.6 = (bf16[128,256]{1,0:T(8,128)(2,1)S(1)}, bf16[128,256]{1,0:T(8,128)(2,1)S(1)}, u32[]{:S(2)}, u32[]{:S(2)}) collective-permute-start(bf16[128,256]{1,0:T(8,128)(2,1)S(1)} %add_convert_fusion.after_ref.sub_ref), channel_id=1, source_target_pairs={{0,9},{1,0},{2,11},{3,2},{4,13},{5,4},{6,15},{7,6},{8,17},{9,8},{1... | collective-permute-start | bytes 196616 | tf_op jit(solution)/shard_map/ppermute | solution.py:372
  12.0 2.4 %collective-permute-start.5 = (bf16[128,256]{1,0:T(8,128)(2,1)S(1)}, bf16[128,256]{1,0:T(8,128)(2,1)S(1)}, u32[]{:S(2)}, u32[]{:S(2)}) collective-permute-start(bf16[128,256]{1,0:T(8,128)(2,1)S(1)} %add_convert_fusion.after_ref.sub_ref), channel_id=1, source_target_pairs={{0,17},{1,0},{2,19},{3,2},{4,21},{5,4},{6,23},{7,6},{8,25},{9,8},{... | collective-permute-start | bytes 196616 | tf_op jit(solution)/shard_map/ppermute | solution.py:372
  14.4 1.1 %collective-permute-start.4 = (bf16[128,256]{1,0:T(8,128)(2,1)S(1)}, bf16[128,256]{1,0:T(8,128)(2,1)S(1)}, u32[]{:S(2)}, u32[]{:S(2)}) collective-permute-start(bf16[128,256]{1,0:T(8,128)(2,1)S(1)} %add_convert_fusion.after_ref.sub_ref), channel_id=1, source_target_pairs={{0,25},{1,0},{2,27},{3,2},{4,29},{5,4},{6,31},{7,6},{8,1},{9,8},{1... | collective-permute-start | bytes 196616 | tf_op jit(solution)/shard_map/ppermute | solution.py:372
  15.4 1.8 %weights.1 = (bf16[4,128,2048]{2,1,0:T(8,128)(2,1)S(1)}, f32[4,16,2048]{2,1,0:T(8,128)S(1)}, f32[4,8,8,128]{3,2,1,0:T(8,128)S(1)}, s32[4,32,128]{2,1,0:T(8,128)S(1)}, s32[8,256]{1,0:T(8,128)S(1)}) custom-call(s32[4]{0:T(128)} %bitcast.16, s32[4]{0:T(128)} %bitcast.17, s32[4]{0:T(128)} %bitcast.18, f32[4]{0:T(128)} %bitcast.19, f32[4,2,2048]{2,1,0:T(2,128)} %bitcast.13, ...), custom_call_target="tpu_custom_call" | custom-call | flops 8388608 | tf_op jit(solution)/shard_map/weights/pallas_call | solution.py:335
  17.2 0.0 collective-permute-done.6.refs_2_
  17.2 0.0 collective-permute-done.5.refs_1_
  17.3 0.1 collective-permute-done.4.refs_0_
  17.4 0.9 %collective-permute-start.7 = (bf16[192,256]{1,0:T(8,128)(2,1)S(1)}, bf16[192,256]{1,0:T(8,128)(2,1)S(1)}, u32[]{:S(2)}, u32[]{:S(2)}) collective-permute-start(bf16[192,256]{1,0:T(8,128)(2,1)S(1)} %maximum_select_fusion), channel_id=1, source_target_pairs={{0,1},{1,0},{2,3},{3,2},{4,5},{5,4},{6,7},{7,6},{8,9},{9,8},{10,11... | collective-permute-start | bytes 294920 | tf_op jit(solution)/shard_map/ppermute | solution.py:269
  18.3 0.9 %collective-permute-done.7.swap_ref = bf16[192,256]{1,0:T(8,128)(2,1)S(1)} collective-permute-done((bf16[192,256]{1,0:T(8,128)(2,1)S(1)}, bf16[192,256]{1,0:T(8,128)(2,1)S(1)}, u32[]{:S(2)}, u32[]{:S(2)}) %collective-permute-start.7) | collective-permute-done | bytes 98336 | tf_op jit(solution)/shard_map/ppermute | solution.py:269
  19.2 1.2 %degrid.1 = (bf16[64,256]{1,0:T(8,128)(2,1)}, f32[4,2,2048]{2,1,0:T(2,128)}) custom-call(f32[4,8,8,128]{3,2,1,0:T(8,128)S(1)} %get-tuple-element.13.mix_ref, s32[4,32,128]{2,1,0:T(8,128)S(1)} %get-tuple-element.14.lane_ref, bf16[4,128,2048]{2,1,0:T(8,128)(2,1)S(1)} %get-tuple-element.15.col_ref, f32[4,16,2048]{2,1,0:T(8,128)S(1)} %get-tuple-element.16.row_ref, ...), custom_call_target="tpu_custom_call" | custom-call | tf_op jit(solution)/shard_map/degrid/pallas_call | solution.py:389
  (10 shorter events, 0.1 us)
Async XLA Ops:
  0.6 2.9 %copy-start = (s32[12]{0:T(128)S(1)}, s32[12]{0:T(128)}, u32[]{:S(2)}) copy-start(s32[12]{0:T(128)} %param.11) | copy-start | bytes 148
  3.0 1.5 %collective-permute-start = (bf16[256,256]{1,0:T(8,128)(2,1)S(1)}, bf16[256,256]{1,0:T(8,128)(2,1)S(1)}, u32[]{:S(2)}, u32[]{:S(2)}) collective-permute-start(bf16[256,256]{1,0:T(8,128)(2,1)S(1)} %front.1.spec_ref), channel_id=1, source_target_pairs={{0,1},{1,0},{2,3},{3,2},{4,5},{5,4},{6,7},{7,6},{8,9},{9,8},{10,11... | collective-permute-start | bytes 393224 | tf_op jit(solution)/shard_map/ppermute | solution.py:269
  4.5 4.8 %collective-permute-start.1 = (bf16[128,256]{1,0:T(8,128)(2,1)S(1)}, bf16[128,256]{1,0:T(8,128)(2,1)S(1)}, u32[]{:S(2)}, u32[]{:S(2)}) collective-permute-start(bf16[128,256]{1,0:T(8,128)(2,1)S(1)} %terms.3), channel_id=1, source_target_pairs={{0,1},{1,4},{2,3},{3,6},{4,5},{5,0},{6,7},{7,2},{8,9},{9,12},{10,1... | collective-permute-start | bytes 196616 | tf_op jit(solution)/shard_map/ppermute | solution.py:320
  5.1 5.6 %collective-permute-start.2 = (bf16[128,256]{1,0:T(8,128)(2,1)S(1)}, bf16[128,256]{1,0:T(8,128)(2,1)S(1)}, u32[]{:S(2)}, u32[]{:S(2)}) collective-permute-start(bf16[128,256]{1,0:T(8,128)(2,1)S(1)} %terms.4), channel_id=1, source_target_pairs={{0,1},{1,6},{2,3},{3,4},{4,5},{5,2},{6,7},{7,0},{8,9},{9,14},{10,1... | collective-permute-start | bytes 196616 | tf_op jit(solution)/shard_map/ppermute | solution.py:320
  7.7 3.9 %collective-permute-start.3 = (bf16[128,256]{1,0:T(8,128)(2,1)S(1)}, bf16[128,256]{1,0:T(8,128)(2,1)S(1)}, u32[]{:S(2)}, u32[]{:S(2)}) collective-permute-start(bf16[128,256]{1,0:T(8,128)(2,1)S(1)} %terms.5), channel_id=1, source_target_pairs={{0,1},{1,2},{2,3},{3,0},{4,5},{5,6},{6,7},{7,4},{8,9},{9,10},{10,1... | collective-permute-start | bytes 196616 | tf_op jit(solution)/shard_map/ppermute | solution.py:320
  11.6 5.6 %collective-permute-start.6 = (bf16[128,256]{1,0:T(8,128)(2,1)S(1)}, bf16[128,256]{1,0:T(8,128)(2,1)S(1)}, u32[]{:S(2)}, u32[]{:S(2)}) collective-permute-start(bf16[128,256]{1,0:T(8,128)(2,1)S(1)} %add_convert_fusion.after_ref.sub_ref), channel_id=1, source_target_pairs={{0,9},{1,0},{2,11},{3,2},{4,13},{5,4},{6,15},{7,6},{8,17},{9,8},{1... | collective-permute-start | bytes 196616 | tf_op jit(solution)/shard_map/ppermute | solution.py:372
  12.0 5.2 %collective-permute-start.5 = (bf16[128,256]{1,0:T(8,128)(2,1)S(1)}, bf16[128,256]{1,0:T(8,128)(2,1)S(1)}, u32[]{:S(2)}, u32[]{:S(2)}) collective-permute-start(bf16[128,256]{1,0:T(8,128)(2,1)S(1)} %add_convert_fusion.after_ref.sub_ref), channel_id=1, source_target_pairs={{0,17},{1,0},{2,19},{3,2},{4,21},{5,4},{6,23},{7,6},{8,25},{9,8},{... | collective-permute-start | bytes 196616 | tf_op jit(solution)/shard_map/ppermute | solution.py:372
  14.4 3.0 %collective-permute-start.4 = (bf16[128,256]{1,0:T(8,128)(2,1)S(1)}, bf16[128,256]{1,0:T(8,128)(2,1)S(1)}, u32[]{:S(2)}, u32[]{:S(2)}) collective-permute-start(bf16[128,256]{1,0:T(8,128)(2,1)S(1)} %add_convert_fusion.after_ref.sub_ref), channel_id=1, source_target_pairs={{0,25},{1,0},{2,27},{3,2},{4,29},{5,4},{6,31},{7,6},{8,1},{9,8},{1... | collective-permute-start | bytes 196616 | tf_op jit(solution)/shard_map/ppermute | solution.py:372
  17.4 1.8 %collective-permute-start.7 = (bf16[192,256]{1,0:T(8,128)(2,1)S(1)}, bf16[192,256]{1,0:T(8,128)(2,1)S(1)}, u32[]{:S(2)}, u32[]{:S(2)}) collective-permute-start(bf16[192,256]{1,0:T(8,128)(2,1)S(1)} %maximum_select_fusion), channel_id=1, source_target_pairs={{0,1},{1,0},{2,3},{3,2},{4,5},{5,4},{6,7},{7,6},{8,9},{9,8},{10,11... | collective-permute-start | bytes 294920 | tf_op jit(solution)/shard_map/ppermute | solution.py:269
